TPU v7x, 32 devices: a whole 2x2x4 slice. The times are simulated.
32 devices in a mesh: grp: 2 (over y), dp: 4 (over z), tp: 4 (over x, core).
Axes of the slice: x: 2, y: 2, z: 4, core: 2. Of those that a mesh axis runs over, the one named last changes fastest.
Arguments:
- dino_stream: bfloat16 [4, 256, 1536], P(None, 'dp'), may hold values from -6 to 6
- siglip_stream: bfloat16 [4, 256, 1152], P(None, 'dp'), may hold values from -6 to 6
- student_stream: bfloat16 [4, 256, 1280], P('dp'), may hold values from -6 to 6
- dino_mlp: bfloat16 [3, 1536, 4096], P(None, 'dp', 'tp'), may hold values from -0.15625 to 0.15625
- siglip_mlp: bfloat16 [2, 1152, 4304], P(None, 'dp', 'tp'), may hold values from -0.1875 to 0.1875
- student_mlp: bfloat16 [2, 1280, 5120], P(None, 'dp', 'tp'), may hold values from -0.15625 to 0.15625
- dino_head: bfloat16 [1280, 1536], P('dp', 'tp'), may hold values from -0.15625 to 0.15625
- siglip_head: bfloat16 [1280, 1152], P('dp', 'tp'), may hold values from -0.15625 to 0.15625
- assign: int32 [4], replicated, may hold values from 0 to 3, each once
Outputs:
- grad_student_mlp: float32 [2, 1280, 5120], P(None, ('grp', 'dp'), 'tp')
- grad_dino_head: float32 [1280, 1536], P(('grp', 'dp'), 'tp')
- grad_siglip_head: float32 [1280, 1152], P(('grp', 'dp'), 'tp')
Inputs may be any that keep to these rules, and one draw needn't show every extreme that they name: assign names each image once.
All inputs are finite; a program needn't handle non-finite values.
Results may differ from a plain program's by a relative error of at most 0.013.
Values may be sent and summed in bfloat16 or wider, within the bound.
A program may use at most 192 MiB of HBM per device.

v0:
```python
import math

import jax
import jax.numpy as jnp
from jax import lax
from jax.sharding import PartitionSpec as P


def shifted(array, axis, by):
    size = lax.axis_size(axis)
    pairs = [(i, i + by) for i in range(size) if 0 <= i + by < size]
    return lax.ppermute(array, axis, pairs)


def norm_rows(values):
    center = values - jnp.mean(values, axis=-1, keepdims=True)
    spread = jnp.mean(center * center, axis=-1, keepdims=True)
    return center * lax.rsqrt(spread + 1e-06)


def norm_back(values, upstream):
    center = values - jnp.mean(values, axis=-1, keepdims=True)
    factor = lax.rsqrt(jnp.mean(center * center, axis=-1, keepdims=True) + 1e-06)
    normed = center * factor
    first = jnp.mean(upstream, axis=-1, keepdims=True)
    second = jnp.mean(upstream * normed, axis=-1, keepdims=True)
    return factor * (upstream - first - normed * second)


def gelu_slope(values):
    cdf = 0.5 * (1.0 + lax.erf(values * (1.0 / math.sqrt(2.0))))
    pdf = jnp.exp(-0.5 * values * values) * (1.0 / math.sqrt(2.0 * math.pi))
    return cdf + values * pdf


def times_transposed(left, right):
    return lax.dot_general(
        left, right, (((1,), (1,)), ((), ())), preferred_element_type=jnp.float32
    )


def over_rows(left, right):
    return lax.dot_general(
        left, right, (((0,), (0,)), ((), ())), preferred_element_type=jnp.float32
    )


def unstack_rows(gathered, offset, shape):
    count = gathered.shape[0]
    length = 1
    for extent in shape:
        length = length * extent
    piece = gathered[:, offset : offset + length]
    if len(shape) == 3:
        piece = piece.reshape(count, shape[0], shape[1], shape[2]).transpose(1, 0, 2, 3)
        return (piece.reshape(shape[0], count * shape[1], shape[2]), offset + length)
    return (piece.reshape(count * shape[0], shape[1]), offset + length)


def body(
    dino_stream,
    siglip_stream,
    student_stream,
    dino_mlp,
    siglip_mlp,
    student_mlp,
    dino_head,
    siglip_head,
    assign,
):
    is_teacher = lax.axis_index("grp") == 0
    column = lax.axis_index("tp")
    count_dp = lax.axis_size("dp")
    img_dev, patches, width = student_stream.shape
    rows = img_dev * patches
    images = assign.shape[0]
    slab = dino_stream.shape[1]
    width_d = dino_stream.shape[2]
    width_s = siglip_stream.shape[2]
    cols_d = dino_head.shape[1]
    cols_s = siglip_head.shape[1]
    ff_local = student_mlp.shape[2]
    block = width // (2 * count_dp)
    scale = 1.0 / math.sqrt(images * patches)
    teacher_flat = jnp.concatenate([dino_mlp.reshape(-1), siglip_mlp.reshape(-1)])
    student_flat = jnp.concatenate(
        [student_mlp.reshape(-1), dino_head.reshape(-1), siglip_head.reshape(-1)]
    )
    length = max(teacher_flat.shape[0], student_flat.shape[0])
    student_flat = jnp.pad(student_flat, (0, length - student_flat.shape[0]))
    packed = jnp.where(is_teacher, teacher_flat, student_flat).reshape(1, length)
    gathered = lax.all_gather(packed, "dp", axis=0, tiled=True)
    w_mlp, offset = unstack_rows(gathered, 0, student_mlp.shape)
    w_dino, offset = unstack_rows(gathered, offset, dino_head.shape)
    w_sig, offset = unstack_rows(gathered, offset, siglip_head.shape)
    flat = student_stream.reshape(rows, width).astype(jnp.float32)

    def teacher_one():
        dino_full, place = unstack_rows(gathered, 0, dino_mlp.shape)
        siglip_full, place = unstack_rows(gathered, place, siglip_mlp.shape)
        normed_d = norm_rows(
            dino_stream.reshape(images * slab, width_d).astype(jnp.float32)
        ).astype(jnp.bfloat16)
        gate = jnp.dot(normed_d, dino_full[0], preferred_element_type=jnp.float32)
        upper = jnp.dot(normed_d, dino_full[1], preferred_element_type=jnp.float32)
        hidden_d = (jax.nn.silu(gate) * upper).astype(jnp.bfloat16)
        part_d = times_transposed(hidden_d, dino_full[2]).reshape(images, slab, width_d)
        normed_s = norm_rows(
            siglip_stream.reshape(images * slab, width_s).astype(jnp.float32)
        ).astype(jnp.bfloat16)
        first = jnp.dot(normed_s, siglip_full[0], preferred_element_type=jnp.float32)
        hidden_s = jax.nn.gelu(first, approximate=True).astype(jnp.bfloat16)
        part_s = times_transposed(hidden_s, siglip_full[1]).reshape(images, slab, width_s)
        return (
            part_d,
            part_s,
            jnp.zeros((rows, width), jnp.bfloat16),
            jnp.zeros((rows, ff_local), jnp.float32),
            jnp.zeros((rows, ff_local), jnp.bfloat16),
            jnp.zeros((rows, width), jnp.float32),
        )

    def student_one():
        normed = norm_rows(flat).astype(jnp.bfloat16)
        act = jnp.dot(normed, w_mlp[0], preferred_element_type=jnp.float32)
        hidden = jax.nn.gelu(act, approximate=False).astype(jnp.bfloat16)
        partial_out = times_transposed(hidden, w_mlp[1])
        return (
            jnp.zeros((images, slab, width_d), jnp.float32),
            jnp.zeros((images, slab, width_s), jnp.float32),
            normed,
            act,
            hidden,
            partial_out,
        )

    section_one = lax.cond(is_teacher, teacher_one, student_one)
    summed_d, summed_s = (
        lax.psum_scatter(
            section_one[0].astype(jnp.bfloat16), "tp", scatter_dimension=2, tiled=True
        ).astype(jnp.float32),
        lax.psum_scatter(
            section_one[1].astype(jnp.bfloat16), "tp", scatter_dimension=2, tiled=True
        ).astype(jnp.float32),
    )
    reduced = lax.psum(section_one[5].astype(jnp.bfloat16), "tp").astype(jnp.float32)
    normed, act, hidden = (section_one[2], section_one[3], section_one[4])

    def teacher_two():
        own_d = lax.dynamic_slice_in_dim(dino_stream, column * cols_d, cols_d, 2)
        own_s = lax.dynamic_slice_in_dim(siglip_stream, column * cols_s, cols_s, 2)
        feat_d = (own_d.astype(jnp.float32) + summed_d).astype(jnp.bfloat16)
        feat_s = (own_s.astype(jnp.float32) + summed_s).astype(jnp.bfloat16)
        return (
            feat_d,
            feat_s,
            jnp.zeros((rows, width), jnp.float32),
            jnp.zeros((rows, width), jnp.bfloat16),
            jnp.zeros((rows, cols_d), jnp.float32),
            jnp.zeros((rows, cols_s), jnp.float32),
        )

    def student_two():
        mixed = flat + reduced
        feat = norm_rows(mixed).astype(jnp.bfloat16)
        pred_d = jnp.dot(feat, w_dino, preferred_element_type=jnp.float32)
        pred_s = jnp.dot(feat, w_sig, preferred_element_type=jnp.float32)
        return (
            jnp.zeros((images, slab, cols_d), jnp.bfloat16),
            jnp.zeros((images, slab, cols_s), jnp.bfloat16),
            mixed,
            feat,
            pred_d,
            pred_s,
        )

    section_two = lax.cond(is_teacher, teacher_two, student_two)
    mixed, feat, pred_d, pred_s = (section_two[2], section_two[3], section_two[4], section_two[5])
    sent_d, sent_s = (section_two[0], section_two[1])
    got_d, got_s = shifted((sent_d, sent_s), "grp", 1)
    arranged = (jnp.take(got_d, assign, axis=0), jnp.take(got_s, assign, axis=0))
    target_d, target_s = (
        lax.all_to_all(arranged[0], "dp", split_axis=0, concat_axis=1, tiled=True),
        lax.all_to_all(arranged[1], "dp", split_axis=0, concat_axis=1, tiled=True),
    )

    def teacher_three():
        return (
            jnp.zeros((rows, cols_d), jnp.bfloat16),
            jnp.zeros((rows, cols_s), jnp.bfloat16),
            jnp.zeros((rows, width), jnp.float32),
        )

    def student_three():
        diff_d = ((pred_d - target_d.reshape(rows, cols_d).astype(jnp.float32)) * scale).astype(
            jnp.bfloat16
        )
        diff_s = ((pred_s - target_s.reshape(rows, cols_s).astype(jnp.float32)) * scale).astype(
            jnp.bfloat16
        )
        return (diff_d, diff_s, times_transposed(diff_d, w_dino) + times_transposed(diff_s, w_sig))

    section_three = lax.cond(is_teacher, teacher_three, student_three)
    diff_d, diff_s = (section_three[0], section_three[1])
    dfeat = lax.psum(section_three[2].astype(jnp.bfloat16), "tp").astype(jnp.float32)

    def student_four():
        grad_d = over_rows(feat, diff_d)
        grad_s = over_rows(feat, diff_s)
        dmixed = norm_back(mixed, dfeat).astype(jnp.bfloat16)
        grad_down = over_rows(dmixed, hidden)
        dhidden = jnp.dot(dmixed, w_mlp[1], preferred_element_type=jnp.float32)
        dact = (dhidden * gelu_slope(act)).astype(jnp.bfloat16)
        grad_up = over_rows(normed, dact)
        grad_mlp = jnp.stack([grad_up, grad_down])
        order_mlp = (
            grad_mlp.reshape(2, 2, count_dp, block, ff_local)
            .transpose(0, 2, 1, 3, 4)
            .reshape(2, width, ff_local)
        )
        order_d = (
            grad_d.reshape(2, count_dp, block, cols_d).transpose(1, 0, 2, 3).reshape(width, cols_d)
        )
        order_s = (
            grad_s.reshape(2, count_dp, block, cols_s).transpose(1, 0, 2, 3).reshape(width, cols_s)
        )
        return (order_mlp, order_d, order_s)

    def teacher_four():
        return (
            jnp.zeros((2, width, ff_local), jnp.float32),
            jnp.zeros((width, cols_d), jnp.float32),
            jnp.zeros((width, cols_s), jnp.float32),
        )

    section_four = lax.cond(is_teacher, teacher_four, student_four)
    sum_mlp, sum_d, sum_s = (
        lax.psum_scatter(
            section_four[0].astype(jnp.bfloat16), "dp", scatter_dimension=1, tiled=True
        ).astype(jnp.float32),
        lax.psum_scatter(
            section_four[1].astype(jnp.bfloat16), "dp", scatter_dimension=0, tiled=True
        ).astype(jnp.float32),
        lax.psum_scatter(
            section_four[2].astype(jnp.bfloat16), "dp", scatter_dimension=0, tiled=True
        ).astype(jnp.float32),
    )
    sum_mlp = sum_mlp.reshape(2, 2, block, ff_local)
    sum_d = sum_d.reshape(2, block, cols_d)
    sum_s = sum_s.reshape(2, block, cols_s)
    kept = (sum_mlp[:, 1], sum_d[1], sum_s[1])
    arrived = (
        shifted(sum_mlp[:, 0].astype(jnp.bfloat16), "grp", -1).astype(jnp.float32),
        shifted(sum_d[0].astype(jnp.bfloat16), "grp", -1).astype(jnp.float32),
        shifted(sum_s[0].astype(jnp.bfloat16), "grp", -1).astype(jnp.float32),
    )
    results = tuple((jnp.where(is_teacher, come, stay) for come, stay in zip(arrived, kept)))
    return (results[0], results[1], results[2])


def solution(mesh):
    in_specs = (
        P(None, "dp", None),
        P(None, "dp", None),
        P("dp", None, None),
        P(None, "dp", "tp"),
        P(None, "dp", "tp"),
        P(None, "dp", "tp"),
        P("dp", "tp"),
        P("dp", "tp"),
        P(),
    )
    out_specs = (P(None, ("grp", "dp"), "tp"), P(("grp", "dp"), "tp"), P(("grp", "dp"), "tp"))
    return jax.shard_map(body, mesh=mesh, in_specs=in_specs, out_specs=out_specs, check_vma=False)
```

profile of v0, /device:TPU:0, one launch (start us, length us, event | category | flops | bytes accessed | tf_op | source)
XLA Modules:
  0.0 1051.0 jit_solution(3029473109390517732)
XLA Ops:
  7.2 2.3 copy.78
  9.5 4.4 reshape.242
  13.9 4.3 reshape.241
  19.0 15.5 %fusion.81 = bf16[1799424]{0:T(1024)(128)(2,1)S(1)} fusion(bf16[92160]{0:T(1024)(128)(2,1)S(1)} %reshape.244, bf16[122880]{0:T(1024)(128)(2,1)S(1)} %reshape.243, bf16[819200]{0:T(1024)(128)(2,1)} %reshape.242, bf16[619776]{0:T(1024)(128)(2,1)} %reshape.241, bf16[1179648]{0:T(1024)(128)(2,1)S(1)} %bitcast.125, pred[]{:T(512)S(6)} %eq.3), kind=kLoop, calls=%fused_computation.120 | loop fusion | flops 26991360 | bytes 9266177 | tf_op jit(solution)/shard_map/jit(_where)/select_n | solution.py:91
  34.5 42.2 %reshape.274 = bf16[1,1,1799424]{2,1,0:T(2,128)(2,1)} reshape(bf16[1799424]{0:T(1024)(128)(2,1)S(1)} %fusion.81) | data formatting | bytes 7197696
  77.9 485.6 %all-gather.4.cloned.1.call-done = bf16[4,1,1799424]{2,1,0:T(2,128)(2,1)} async-done(((bf16[1,1,1799424]{2,1,0:T(2,128)(2,1)}), bf16[4,1,1799424]{2,1,0:T(2,128)(2,1)}) %all-gather.4.cloned.1.call-update) | async-done | bytes 14395408 | tf_op jit(solution)/shard_map/all_gather | solution.py:92
  563.5 21.5 %copy.85 = bf16[4,1,1799424]{2,0,1:T(4,128)(2,1)} copy(bf16[4,1,1799424]{2,1,0:T(2,128)(2,1)} %all-gather.4.cloned.1.call-done) | data formatting | bytes 28790784
  585.1 4.7 slice.96
  590.6 3.2 copy.65
  593.8 91.8 %conditional.4 = (bf16[4,64,1536]{2,1,0:T(8,128)(2,1)}, bf16[4,64,1152]{2,1,0:T(8,128)(2,1)}, bf16[256,1280]{1,0:T(8,128)(2,1)}, f32[256,1280]{1,0:T(8,128)}, bf...) conditional(s32[]{:T(128)} %convert_element_type.144, (f32[256,1280]{1,0:T(8,128)S(1)}, ...), branch_computations={%region_0.3_spmd, %region_3.8_spmd} | conditional | flops 3696154112 | bytes 163324016 | solution.py:137
  594.4 1.2 fusion.19
  595.5 19.2 %slice.57 = bf16[4,1179648]{1,0:T(4,128)(2,1)} slice(bf16[4,1799424]{1,0:T(4,128)(2,1)} %get-tuple-element.65), slice={[0:4], [0:1179648]} | slice | bytes 18874368 | tf_op jit(solution)/shard_map/cond/branch_1_fun/slice | solution.py:53
  614.8 10.6 %copy.77 = bf16[1,4,1152,1024]{3,2,1,0:T(8,128)(2,1)} copy(bf16[1,4,1152,1024]{3,1,2,0:T(4,128)(2,1)} %bitcast.120) | data formatting | bytes 18874368 | tf_op jit(solution)/shard_map/cond
  625.3 8.4 copy.83
  633.8 4.3 fusion.83
  639.1 1.1 fusion.22
  640.2 2.0 fusion.91
  642.6 1.1 fusion.24
  643.8 7.1 slice.61
  650.8 6.5 reshape.283
  657.3 12.0 %reshape.223 = bf16[4,2,288,1076]{3,2,1,0:T(8,128)(2,1)} reshape(bf16[2479104]{0:T(1024)(128)(2,1)} %reshape.283) | data formatting | bytes 9916416 | tf_op jit(solution)/shard_map/cond/branch_1_fun/reshape | solution.py:55
  669.4 2.9 copy.84
  672.3 2.0 fusion.84
  674.3 2.1 fusion.32
  676.4 2.1 copy.57
  678.5 3.8 fusion.92
  682.3 1.2 broadcast.308
  686.6 3.2 copy.73
  689.8 2.9 reshape.281
  692.8 3.4 copy.71
  696.2 3.6 reshape.279
  699.9 2.5 slice.97
  702.4 2.2 slice.98
  704.6 2.8 reshape.248
  707.4 3.5 reshape.249
  710.9 6.9 all-reduce.4.cloned.1.call-done
  717.8 24.6 %reduce-scatter.18.cloned.1.call-done = bf16[288,256]{1,0:T(8,128)(2,1)} async-done(((bf16[1152,256]{1,0:T(8,128)(2,1)}), bf16[288,256]{1,0:T(8,128)(2,1)}) %reduce-scatter.18.cloned.1.call-update) | async-done | bytes 147472
  742.4 1.1 reshape.282
  744.5 23.5 %reduce-scatter.16.cloned.1.call-done = bf16[384,256]{1,0:T(8,128)(2,1)} async-done(((bf16[1536,256]{1,0:T(8,128)(2,1)}), bf16[384,256]{1,0:T(8,128)(2,1)}) %reduce-scatter.16.cloned.1.call-update) | async-done | bytes 196624
  768.1 1.2 reshape.280
  770.3 5.2 conditional.5
  770.3 1.8 add_convert_fusion
  772.1 1.7 add_convert_fusion.1
  775.5 5.0 collective-permute-start.1
  780.5 1.3 collective-permute-start
  781.9 4.3 collective-permute-done.1
  787.5 4.6 all-to-all-start.1
  793.4 4.9 all-to-all-done.1
  798.3 3.4 all-to-all-start
  801.7 6.2 all-to-all-done
  808.9 36.5 %all-reduce.6.cloned.1.call-done = bf16[256,1280]{1,0:T(8,128)(2,1)} async-done(((bf16[256,1280]{1,0:T(8,128)(2,1)}), bf16[256,1280]{1,0:T(8,128)(2,1)}) %all-reduce.6.cloned.1.call-update) | async-done | bytes 655376 | tf_op jit(solution)/shard_map/psum | solution.py:205
  845.5 3.6 conditional.7
  845.7 3.1 broadcast.329
  851.9 124.4 %reduce-scatter.10.cloned.1.call-done = bf16[2,320,1280]{2,1,0:T(8,128)(2,1)} async-done(((bf16[2,1280,1280]{2,1,0:T(8,128)(2,1)}), bf16[2,320,1280]{2,1,0:T(8,128)(2,1)}) %reduce-scatter.10.cloned.1.call-update) | async-done | bytes 1638416 | tf_op jit(solution)/shard_map/reduce_scatter | solution.py:238
  976.3 1.3 slice_bitcast_fusion.1
  977.6 1.3 collective-permute-start.2
  978.9 26.5 %reduce-scatter.14.cloned.1.call-done = bf16[320,288]{1,0:T(8,128)(2,1)} async-done(((bf16[1280,288]{1,0:T(8,128)(2,1)}), bf16[320,288]{1,0:T(8,128)(2,1)}) %reduce-scatter.14.cloned.1.call-update) | async-done | bytes 184336 | tf_op jit(solution)/shard_map/reduce_scatter | solution.py:244
  1006.3 1.3 collective-permute-start.4
  1007.6 25.4 %reduce-scatter.12.cloned.1.call-done = bf16[320,384]{1,0:T(8,128)(2,1)} async-done(((bf16[1280,384]{1,0:T(8,128)(2,1)}), bf16[320,384]{1,0:T(8,128)(2,1)}) %reduce-scatter.12.cloned.1.call-update) | async-done | bytes 245776 | tf_op jit(solution)/shard_map/reduce_scatter | solution.py:241
  1034.0 1.3 collective-permute-start.3
  1035.3 1.6 convert_select_fusion.1
  1036.9 3.9 collective-permute-done.3
  1040.8 1.6 convert_select_fusion.2
  1042.4 1.3 convert_select_fusion
  (86 shorter events, 20.2 us)
Async XLA Ops:
  7.2 556.4 %all-gather.4.cloned.1.call-start = ((), (), s32[]{:S(2)}) async-start(), calls=%async_computation.12 | async-start | bytes 35988480 | tf_op jit(solution)/shard_map/all_gather | solution.py:92
  13.9 4.3 copy-start.16
  13.9 5.0 copy-start.15
  76.7 1.1 copy-start.13
  76.8 641.0 %all-reduce.4.cloned.1.call-start = ((), (), s32[]{:S(2)}) async-start(), calls=%async_computation.7 | async-start | bytes 1310720 | tf_op jit(solution)/shard_map/psum | solution.py:146
  590.6 3.2 copy-start.4
  590.6 3.2 copy-start.5
  633.8 4.3 copy-start.12
  672.3 2.0 copy-start.14
  686.6 55.8 %reduce-scatter.18.cloned.1.call-start = ((), (), s32[]{:S(2)}) async-start(), calls=%async_computation.14 | async-start | bytes 737280
  692.7 75.3 %reduce-scatter.16.cloned.1.call-start = ((), (), s32[]{:S(2)}) async-start(), calls=%async_computation.13 | async-start | bytes 983040
  696.2 3.6 copy-start.17
  775.5 32.4 %copy-start = (bf16[1280,384]{1,0:T(8,128)(2,1)S(1)}, bf16[1280,384]{1,0:T(8,128)(2,1)}, u32[]{:S(2)}) copy-start(bf16[1280,384]{1,0:T(8,128)(2,1)} %reshape.248) | copy-start | bytes 2949124
  775.5 10.6 %collective-permute-start.1 = (bf16[4,64,288]{2,1,0:T(8,128)(2,1)}, bf16[4,64,288]{2,1,0:T(8,128)(2,1)S(1)}, u32[]{:S(2)}, u32[]{:S(2)}) collective-permute-start(bf16[4,64,288]{2,1,0:T(8,128)(2,1)} %get-tuple-element.118), channel_id=1, source_target_pairs={{0,16},{1,17},{2,18},{3,19},{4,20},{5,21},{6,22},{7,23},{8,24},{9,... | collective-permute-start | bytes 442376 | tf_op jit(solution)/shard_map/ppermute | solution.py:12
  780.5 11.5 %collective-permute-start = (bf16[4,64,384]{2,1,0:T(8,128)(2,1)}, bf16[4,64,384]{2,1,0:T(8,128)(2,1)S(1)}, u32[]{:S(2)}, u32[]{:S(2)}) collective-permute-start(bf16[4,64,384]{2,1,0:T(8,128)(2,1)} %get-tuple-element.116), channel_id=1, source_target_pairs={{0,16},{1,17},{2,18},{3,19},{4,20},{5,21},{6,22},{7,23},{8,24},{9,... | collective-permute-start | bytes 589832 | tf_op jit(solution)/shard_map/ppermute | solution.py:12
  787.5 10.8 %all-to-all-start.1 = ((bf16[4,64,288]{2,1,0:T(8,128)(2,1)}), bf16[4,64,288]{2,1,0:T(8,128)(2,1)S(1)}, u32[]{:S(2)}, u32[]{:S(2)}) async-start(bf16[4,64,288]{2,1,0:T(8,128)(2,1)} %broadcast_select_fusion), calls=%async_computation.1 | async-start | bytes 393216 | tf_op jit(solution)/shard_map/all_to_all | solution.py:184
  798.3 9.6 all-to-all-start
  801.7 43.8 %all-reduce.6.cloned.1.call-start = ((), (), s32[]{:S(2)}) async-start(), calls=%async_computation.8 | async-start | bytes 1310720 | tf_op jit(solution)/shard_map/psum | solution.py:205
  808.0 0.8 copy-start.10
  808.9 167.4 %reduce-scatter.10.cloned.1.call-start = ((), (), s32[]{:S(2)}) async-start(), calls=%async_computation.9 | async-start | bytes 8192000 | tf_op jit(solution)/shard_map/reduce_scatter | solution.py:238
  849.1 0.9 copy-start.7
  849.1 1.3 copy-start.8
  850.4 155.0 %reduce-scatter.14.cloned.1.call-start = ((), (), s32[]{:S(2)}) async-start(), calls=%async_computation.11 | async-start | bytes 1228800 | tf_op jit(solution)/shard_map/reduce_scatter | solution.py:244
  851.1 181.9 %reduce-scatter.12.cloned.1.call-start = ((), (), s32[]{:S(2)}) async-start(), calls=%async_computation.10 | async-start | bytes 1228800 | tf_op jit(solution)/shard_map/reduce_scatter | solution.py:241
  976.3 66.1 %copy-start.11 = (bf16[2,320,1280]{2,1,0:T(8,128)(2,1)S(1)}, bf16[2,320,1280]{2,1,0:T(8,128)(2,1)}, u32[]{:S(2)}) copy-start(bf16[2,320,1280]{2,1,0:T(8,128)(2,1)} %reduce-scatter.10.cloned.1.call-done) | copy-start | bytes 4915204
  977.6 64.8 %collective-permute-start.2 = (bf16[2,160,1280]{2,1,0:T(8,128)(2,1)S(1)}, bf16[2,160,1280]{2,1,0:T(8,128)(2,1)S(1)}, u32[]{:S(2)}, u32[]{:S(2)}) collective-permute-start(bf16[2,160,1280]{2,1,0:T(8,128)(2,1)S(1)} %slice_bitcast_fusion.1), channel_id=1, source_target_pairs={{16,0},{17,1},{18,2},{19,3},{20,4},{21,5},{22,6},{23,7},{24,8},{25... | collective-permute-start | bytes 2457608 | tf_op jit(solution)/shard_map/ppermute | solution.py:12
  1006.3 28.9 %collective-permute-start.4 = (bf16[160,288]{1,0:T(8,128)(2,1)S(1)}, bf16[160,288]{1,0:T(8,128)(2,1)S(1)}, u32[]{:S(2)}, u32[]{:S(2)}) collective-permute-start(bf16[160,288]{1,0:T(8,128)(2,1)S(1)} %slice.103), channel_id=1, source_target_pairs={{16,0},{17,1},{18,2},{19,3},{20,4},{21,5},{22,6},{23,7},{24,8},{25... | collective-permute-start | bytes 276488 | tf_op jit(solution)/shard_map/ppermute | solution.py:12
  1034.0 6.8 collective-permute-start.3
Sparse Core Ops, SparseCore 0:
  76.9 486.5 all-gather.3
  686.7 31.0 all-reduce.3
  720.3 22.0 reduce-scatter.17
  744.8 23.2 reduce-scatter.15
  809.0 36.4 all-reduce.5
  849.2 127.0 reduce-scatter.9
  978.7 26.6 reduce-scatter.13
  1008.3 24.6 reduce-scatter.11
where the time goes:
time: 1060 us; the launch traced here: 1050 us
  waiting for transfers between devices  774 us (73%)
  local copies, waits for them, and re-layouts  202 us (19%)
  other arithmetic  31.1 us (3%)
  starting transfers between devices  18.4 us (2%)
  between operations  14.9 us (1%)
    all_gather x1, waiting for transfers between devices, body(): gathered = lax.all_gather(packed, 'dp', axis=0, tiled=True)  486 us
    reduce_scatter x1, waiting for transfers between devices, body(): lax.psum_scatter(section_four[0].astype(jnp.bfloat16), 'dp', scatter_dime...  124 us
    unnamed x35, local copies, waits for them, and re-layouts  86.1 us
    unnamed x10, waiting for transfers between devices  49.7 us
    psum x1, waiting for transfers between devices, body(): lax.psum(section_three[2].astype(jnp.bfloat16), 'tp').astype(jnp.float32)  36.5 us
    slice x5, local copies, waits for them, and re-layouts, unstack_rows(): piece = gathered[:, offset:offset + length]  35.7 us
    reduce_scatter x1, waiting for transfers between devices, body(): lax.psum_scatter(section_four[2].astype(jnp.bfloat16), 'dp', scatter_dime...  26.5 us
    reduce_scatter x1, waiting for transfers between devices, body(): lax.psum_scatter(section_four[1].astype(jnp.bfloat16), 'dp', scatter_dime...  25.4 us
  transfers between devices with their start and end apart: 15, of which 12 were waited for; matrix products, arithmetic and copies ran while one was open for 3% of the time, Pallas kernels for 0%

commit v1 on v0

v1 whole, which is shorter than its diff:
```python
import math

import jax
import jax.numpy as jnp
from jax import lax
from jax.sharding import PartitionSpec as P


def norm_rows(values):
    center = values - jnp.mean(values, axis=-1, keepdims=True)
    spread = jnp.mean(center * center, axis=-1, keepdims=True)
    return center * lax.rsqrt(spread + 1e-06)


def norm_back(values, upstream):
    center = values - jnp.mean(values, axis=-1, keepdims=True)
    factor = lax.rsqrt(jnp.mean(center * center, axis=-1, keepdims=True) + 1e-06)
    normed = center * factor
    first = jnp.mean(upstream, axis=-1, keepdims=True)
    second = jnp.mean(upstream * normed, axis=-1, keepdims=True)
    return factor * (upstream - first - normed * second)


def gelu_slope(values):
    cdf = 0.5 * (1.0 + lax.erf(values * (1.0 / math.sqrt(2.0))))
    pdf = jnp.exp(-0.5 * values * values) * (1.0 / math.sqrt(2.0 * math.pi))
    return cdf + values * pdf


def times_transposed(left, right):
    return lax.dot_general(
        left, right, (((1,), (1,)), ((), ())), preferred_element_type=jnp.float32
    )


def over_rows(left, right):
    return lax.dot_general(
        left, right, (((0,), (0,)), ((), ())), preferred_element_type=jnp.float32
    )


def gathered_rows(block, axis):
    count = lax.axis_size("dp")
    if count > 8:
        return lax.all_gather(block, "dp", axis=axis, tiled=True)
    up, down = [block], [block]
    for step in range(1, count):
        up.append(lax.ppermute(up[-1], "dp", [(i, i + 1) for i in range(step - 1, count - 1)]))
        down.append(
            lax.ppermute(down[-1], "dp", [(i, i - 1) for i in range(1, count - step + 1)])
        )
    line = jnp.concatenate(up[:0:-1] + down, axis=axis)
    length = block.shape[axis]
    start = (count - 1 - lax.axis_index("dp")) * length
    return lax.dynamic_slice_in_dim(line, start, count * length, axis)


def own_units(weights, group, low):
    count = weights.shape[-1]
    return jnp.where(group == 0, weights[..., : count - low], weights[..., low:])


def across(array):
    return lax.ppermute(array, "grp", [(0, 1), (1, 0)])


def body(
    dino_stream,
    siglip_stream,
    student_stream,
    dino_mlp,
    siglip_mlp,
    student_mlp,
    dino_head,
    siglip_head,
    assign,
):
    bf16, f32 = jnp.bfloat16, jnp.float32
    group = lax.axis_index("grp")
    column = lax.axis_index("tp")
    count_dp = lax.axis_size("dp")
    count_tp = lax.axis_size("tp")
    img_dev, patches, width = student_stream.shape
    rows = img_dev * patches
    images, slab, width_d = dino_stream.shape
    width_s = siglip_stream.shape[2]
    cols_d = dino_head.shape[1]
    cols_s = siglip_head.shape[1]
    units = student_mlp.shape[2] // 2
    half = width // 2
    block = half // count_dp
    scale = 1.0 / math.sqrt(images * patches)

    low_d = dino_mlp.shape[2] // 2 // 128 * 128
    low_s = siglip_mlp.shape[2] // 2 // 128 * 128
    dino_full = gathered_rows(own_units(dino_mlp, group, low_d), 1)
    siglip_full = gathered_rows(own_units(siglip_mlp, group, low_s), 1)
    w_mlp = gathered_rows(own_units(student_mlp, group, units), 1)
    w_dino = gathered_rows(dino_head, 0)
    w_sig = gathered_rows(siglip_head, 0)

    def once(hidden, low):
        place = lax.broadcasted_iota(jnp.int32, hidden.shape, 1)
        return jnp.where((group == 1) | (place < low), hidden, jnp.zeros_like(hidden))

    normed_d = norm_rows(dino_stream.reshape(images * slab, width_d).astype(f32)).astype(bf16)
    gate = jnp.dot(normed_d, dino_full[0], preferred_element_type=f32)
    upper = jnp.dot(normed_d, dino_full[1], preferred_element_type=f32)
    hidden_d = once((jax.nn.silu(gate) * upper).astype(bf16), low_d)
    part_d = times_transposed(hidden_d, dino_full[2]).astype(bf16)
    normed_s = norm_rows(siglip_stream.reshape(images * slab, width_s).astype(f32)).astype(bf16)
    first = jnp.dot(normed_s, siglip_full[0], preferred_element_type=f32)
    hidden_s = once(jax.nn.gelu(first, approximate=True).astype(bf16), low_s)
    part_s = times_transposed(hidden_s, siglip_full[1]).astype(bf16)
    parts = jnp.stack(
        [
            jnp.concatenate(
                [
                    part_d[:, i * cols_d : (i + 1) * cols_d],
                    part_s[:, i * cols_s : (i + 1) * cols_s],
                ],
                axis=1,
            )
            for i in range(count_tp)
        ]
    )
    summed = lax.psum_scatter(parts, "tp", scatter_dimension=0, tiled=True)[0].astype(bf16)
    summed = summed.astype(f32) + across(summed).astype(f32)
    own = jnp.concatenate(
        [
            lax.dynamic_slice_in_dim(dino_stream, column * cols_d, cols_d, 2),
            lax.dynamic_slice_in_dim(siglip_stream, column * cols_s, cols_s, 2),
        ],
        axis=2,
    )
    features = (own.astype(f32) + summed.reshape(own.shape)).astype(bf16)
    arranged = jnp.take(features, assign, axis=0)
    target = lax.all_to_all(arranged, "dp", split_axis=0, concat_axis=1, tiled=True)
    target = target.reshape(rows, cols_d + cols_s).astype(f32)

    flat = student_stream.reshape(rows, width).astype(f32)
    normed = norm_rows(flat).astype(bf16)
    act = jnp.dot(normed, w_mlp[0], preferred_element_type=f32)
    hidden = jax.nn.gelu(act, approximate=False).astype(bf16)
    partial_out = times_transposed(hidden, w_mlp[1])
    mixed = flat + lax.psum(partial_out.astype(bf16), ("grp", "tp")).astype(f32)
    feat = norm_rows(mixed).astype(bf16)
    pred_d = jnp.dot(feat, w_dino, preferred_element_type=f32)
    pred_s = jnp.dot(feat, w_sig, preferred_element_type=f32)
    diff_d = ((pred_d - target[:, :cols_d]) * scale).astype(bf16)
    diff_s = ((pred_s - target[:, cols_d:]) * scale).astype(bf16)

    dfeat = times_transposed(diff_d, w_dino) + times_transposed(diff_s, w_sig)
    dfeat = lax.psum(dfeat.astype(bf16), "tp").astype(f32)
    own_feat = lax.dynamic_slice_in_dim(feat, group * half, half, 1)
    grad_heads = over_rows(own_feat, jnp.concatenate([diff_d, diff_s], axis=1)).astype(bf16)
    sum_heads = lax.psum_scatter(grad_heads, "dp", scatter_dimension=0, tiled=True).astype(f32)
    dmixed = norm_back(mixed, dfeat).astype(bf16)
    grad_down = over_rows(dmixed, hidden).astype(bf16)
    dhidden = jnp.dot(dmixed, w_mlp[1], preferred_element_type=f32)
    dact = (dhidden * gelu_slope(act)).astype(bf16)
    grad_up = over_rows(normed, dact).astype(bf16)

    def ordered(grad):
        return grad.reshape(2, count_dp, block, units).transpose(1, 0, 2, 3).reshape(width, units)

    grad_mlp = jnp.stack([ordered(grad_up), ordered(grad_down)])
    sum_mlp = lax.psum_scatter(grad_mlp, "dp", scatter_dimension=1, tiled=True)
    sum_mlp = sum_mlp.reshape(2, 2, block, units)
    away = across(jnp.where(group == 0, sum_mlp[:, 1], sum_mlp[:, 0]).astype(bf16)).astype(f32)
    here = jnp.where(group == 0, sum_mlp[:, 0], sum_mlp[:, 1]).astype(f32)
    left = jnp.where(group == 0, here, away)
    right = jnp.where(group == 0, away, here)
    return (
        jnp.concatenate([left, right], axis=2),
        sum_heads[:, :cols_d],
        sum_heads[:, cols_d:],
    )


def solution(mesh):
    in_specs = (
        P(None, "dp", None),
        P(None, "dp", None),
        P("dp", None, None),
        P(None, "dp", "tp"),
        P(None, "dp", "tp"),
        P(None, "dp", "tp"),
        P("dp", "tp"),
        P("dp", "tp"),
        P(),
    )
    out_specs = (P(None, ("grp", "dp"), "tp"), P(("grp", "dp"), "tp"), P(("grp", "dp"), "tp"))
    return jax.shard_map(body, mesh=mesh, in_specs=in_specs, out_specs=out_specs, check_vma=False)
```

time: 1060 us -> 445 us (0.42)
  waiting for transfers between devices: 774 us -> 262 us
  local copies, waits for them, and re-layouts: 202 us -> 52.8 us
  starting transfers between devices: 18.4 us -> 64.2 us
  matrix products: 9.95 us -> 26 us
    all_gather x1 -> x0, waiting for transfers between devices: 486 us -> none  [body(): gathered = lax.all_gather(packed, 'dp', axis=0, tiled=True)]
    ppermute x5 -> x32, waiting for transfers between devices: 8.14 us -> 133 us  [the longest x15 99.2 us: gathered_rows(): lax.ppermute(down[-1], 'dp', [(i, i - 1) for i in range(1, count - step +...]
    reduce_scatter x3, waiting for transfers between devices: 176 us -> 86.5 us  [the longest x1 60.1 us: body(): sum_mlp = lax.psum_scatter(grad_mlp, 'dp', scatter_dimension=1, tiled=True)]
    unnamed x35 -> x85, local copies, waits for them, and re-layouts: 86.1 us -> 35.2 us
    unnamed x10 -> x5, waiting for transfers between devices: 49.7 us -> 0.08 us
    ppermute x5 -> x32, starting transfers between devices: 10.2 us -> 59.7 us  [the longest x15 37.3 us: gathered_rows(): lax.ppermute(up[-1], 'dp', [(i, i + 1) for i in range(step - 1, count - 1)])]
    slice x9 -> x4, local copies, waits for them, and re-layouts: 43.9 us -> 5.49 us  [the longest x1 2.19 us: body(): part_s[:, i * cols_s:(i + 1) * cols_s]]
    reshape x9 -> x2, local copies, waits for them, and re-layouts: 38.9 us -> 1.76 us  [ordered(): grad.reshape(2, count_dp, block, units).transpose(1, 0, 2, 3)]
  transfers between devices with their start and end apart: 15 -> 38, of which waited for: 12 -> 17; matrix products, arithmetic and copies ran while one was open for 3% -> 15% of each run, Pallas kernels for 0% -> 0%
where the time goes in v1:
time: 445 us; the launch traced here: 442 us
  waiting for transfers between devices  262 us (59%)
  starting transfers between devices  64.2 us (14%)
  local copies, waits for them, and re-layouts  52.8 us (12%)
  matrix products  26 us (6%)
  other arithmetic  21.5 us (5%)
  between operations  16 us (4%)
    ppermute x15, waiting for transfers between devices, gathered_rows(): lax.ppermute(down[-1], 'dp', [(i, i - 1) for i in range(1, count - step +...  99.2 us
    reduce_scatter x1, waiting for transfers between devices, body(): sum_mlp = lax.psum_scatter(grad_mlp, 'dp', scatter_dimension=1, tiled=True)  60.1 us
    ppermute x15, starting transfers between devices, gathered_rows(): lax.ppermute(up[-1], 'dp', [(i, i + 1) for i in range(step - 1, count - 1)])  37.3 us
    unnamed x85, local copies, waits for them, and re-layouts  35.2 us
    psum x1, waiting for transfers between devices, body(): dfeat = lax.psum(dfeat.astype(bf16), 'tp').astype(f32)  33.2 us
    ppermute x15, waiting for transfers between devices, gathered_rows(): lax.ppermute(up[-1], 'dp', [(i, i + 1) for i in range(step - 1, count - 1)])  28.2 us
    reduce_scatter x1, waiting for transfers between devices, body(): lax.psum_scatter(grad_heads, 'dp', scatter_dimension=0, tiled=True)  26.4 us
    ppermute x15, starting transfers between devices, gathered_rows(): lax.ppermute(down[-1], 'dp', [(i, i - 1) for i in range(1, count - step +...  19.3 us
  transfers between devices with their start and end apart: 38, of which 17 were waited for; matrix products, arithmetic and copies ran while one was open for 15% of the time, Pallas kernels for 0%

profile of v1, /device:TPU:0, one launch (start us, length us, event | category | flops | bytes accessed | tf_op | source)
XLA Modules:
  0.0 442.4 jit_solution(7649763721956343160)
XLA Ops:
  8.1 1.5 slice_select_fusion.2
  9.6 6.0 %collective-permute-start.18 = (bf16[2,288,564]{2,1,0:T(8,128)(2,1)S(1)}, bf16[2,288,564]{2,1,0:T(8,128)(2,1)}, u32[]{:S(2)}, u32[]{:S(2)}) collective-permute-start(bf16[2,288,564]{2,1,0:T(8,128)(2,1)S(1)} %slice_select_fusion.2), channel_id=1, source_target_pairs={{0,4},{4,8},{8,12},{1,5},{5,9},{9,13},{2,6},{6,10},{10,14},{3,7},{... | collective-permute-start | bytes 1949192 | tf_op jit(solution)/shard_map/ppermute | solution.py:48
  17.0 5.7 %collective-permute-start = (bf16[2,320,640]{2,1,0:T(8,128)(2,1)S(1)}, bf16[2,320,640]{2,1,0:T(8,128)(2,1)}, u32[]{:S(2)}, u32[]{:S(2)}) collective-permute-start(bf16[2,320,640]{2,1,0:T(8,128)(2,1)S(1)} %slice_select_fusion.1), channel_id=1, source_target_pairs={{0,4},{4,8},{8,12},{1,5},{5,9},{9,13},{2,6},{6,10},{10,14},{3,7},{... | collective-permute-start | bytes 2457608 | tf_op jit(solution)/shard_map/ppermute | solution.py:48
  25.1 5.7 %collective-permute-start.12 = (bf16[3,384,512]{2,1,0:T(8,128)(2,1)}, bf16[3,384,512]{2,1,0:T(8,128)(2,1)}, u32[]{:S(2)}, u32[]{:S(2)}) collective-permute-start(bf16[3,384,512]{2,1,0:T(8,128)(2,1)} %slice_select_fusion), channel_id=1, source_target_pairs={{0,4},{4,8},{8,12},{1,5},{5,9},{9,13},{2,6},{6,10},{10,14},{3,7},{... | collective-permute-start | bytes 3538952 | tf_op jit(solution)/shard_map/ppermute | solution.py:48
  32.9 1.5 collective-permute-start.19
  34.8 2.1 collective-permute-done.21
  38.5 10.6 %collective-permute-done = bf16[2,320,640]{2,1,0:T(8,128)(2,1)} collective-permute-done((bf16[2,320,640]{2,1,0:T(8,128)(2,1)S(1)}, bf16[2,320,640]{2,1,0:T(8,128)(2,1)}, u32[]{:S(2)}, u32[]{:S(2)}) %collective-permute-start) | collective-permute-done | bytes 819232 | tf_op jit(solution)/shard_map/ppermute | solution.py:48
  49.1 1.6 collective-permute-start.1
  50.7 3.9 collective-permute-done.3
  55.9 17.5 %collective-permute-done.12 = bf16[3,384,512]{2,1,0:T(8,128)(2,1)} collective-permute-done((bf16[3,384,512]{2,1,0:T(8,128)(2,1)}, bf16[3,384,512]{2,1,0:T(8,128)(2,1)}, u32[]{:S(2)}, u32[]{:S(2)}) %collective-permute-start.12) | collective-permute-done | bytes 1179680 | tf_op jit(solution)/shard_map/ppermute | solution.py:48
  74.7 1.6 collective-permute-start.20
  76.2 2.2 fusion.31
  78.4 1.4 collective-permute-done.15
  79.8 1.7 collective-permute-start.13
  81.5 30.2 %collective-permute-done.22 = bf16[2,288,564]{2,1,0:T(8,128)(2,1)} collective-permute-done((bf16[2,288,564]{2,1,0:T(8,128)(2,1)}, bf16[2,288,564]{2,1,0:T(8,128)(2,1)}, u32[]{:S(2)}, u32[]{:S(2)}) %collective-permute-start.22) | collective-permute-done | bytes 649760 | tf_op jit(solution)/shard_map/ppermute | solution.py:50
  114.3 1.6 collective-permute-start.2
  122.6 35.9 %collective-permute-done.23 = bf16[2,288,564]{2,1,0:T(8,128)(2,1)S(1)} collective-permute-done((bf16[2,288,564]{2,1,0:T(8,128)(2,1)}, bf16[2,288,564]{2,1,0:T(8,128)(2,1)S(1)}, u32[]{:S(2)}, u32[]{:S(2)}) %collective-permute-start.23) | collective-permute-done | bytes 649760 | tf_op jit(solution)/shard_map/ppermute | solution.py:50
  158.6 2.3 copy-done.29
  160.9 4.8 %convolution_convert_fusion.2 = bf16[256,1152]{1,0:T(8,128)(2,1)} fusion(bf16[2,2016,564]{2,1,0:T(8,128)(2,1)} %copy-done.29, s32[]{:T(128)S(6)} %add.119, s32[]{:T(128)S(6)} %select_n.103, bf16[256,1152]{1,0:T(8,128)(2,1)} %bitcast.151, pred[564]{0:T(1024)(128)(4,1)S(1)} %fusion.96), kind=kOutput, calls=%fused_computation.6 | convolution fusion | flops 667060224 | bytes 4130868 | tf_op jit(solution)/shard_map/dot_general | solution.py:31
  165.7 2.2 fusion.129
  167.9 1.7 collective-permute-start.14
  172.1 1.4 constant_dynamic-update-slice_fusion.5
  178.9 2.8 fusion.40
  182.5 1.5 convolution_convert_fusion.4
  185.7 1.3 constant_dynamic-update-slice_fusion.19
  187.0 1.3 constant_dynamic-update-slice_fusion.18
  190.0 1.4 constant_dynamic-update-slice_fusion.15
  191.5 7.6 %collective-permute-done.17 = bf16[3,384,512]{2,1,0:T(8,128)(2,1)} collective-permute-done((bf16[3,384,512]{2,1,0:T(8,128)(2,1)}, bf16[3,384,512]{2,1,0:T(8,128)(2,1)}, u32[]{:S(2)}, u32[]{:S(2)}) %collective-permute-start.17) | collective-permute-done | bytes 1179680 | tf_op jit(solution)/shard_map/ppermute | solution.py:50
  200.4 3.2 copy-done.13
  203.7 1.4 fusion.8
  205.0 3.2 convolution_convert_fusion.3
  209.5 1.4 pad_maximum_fusion.2
  211.8 1.4 collective-permute-start.6
  214.5 4.9 %collective-permute-start.25 = (bf16[320,288]{0,1:T(8,128)(2,1)S(1)}, bf16[320,288]{0,1:T(8,128)(2,1)S(1)}, u32[]{:S(2)}, u32[]{:S(2)}) collective-permute-start(bf16[320,288]{0,1:T(8,128)(2,1)S(1)} %copy-done.23), channel_id=1, source_target_pairs={{0,4},{4,8},{8,12},{1,5},{5,9},{9,13},{2,6},{6,10},{10,14},{3,7},{... | collective-permute-start | bytes 552968 | tf_op jit(solution)/shard_map/ppermute | solution.py:48
  220.8 1.4 collective-permute-start.7
  223.9 3.9 collective-permute-done.28
  231.4 1.4 collective-permute-start.8
  233.5 7.6 %collective-permute-done.29 = bf16[320,288]{0,1:T(8,128)(2,1)S(1)} collective-permute-done((bf16[320,288]{0,1:T(8,128)(2,1)S(1)}, bf16[320,288]{0,1:T(8,128)(2,1)S(1)}, u32[]{:S(2)}, u32[]{:S(2)}) %collective-permute-start.29) | collective-permute-done | bytes 184352 | tf_op jit(solution)/shard_map/ppermute | solution.py:50
  242.3 3.9 collective-permute-done.10
  248.3 2.7 collective-permute-done.30
  251.0 2.5 concatenate.45
  253.5 1.7 constant_dynamic-update-slice_fusion.13
  255.2 1.7 constant_dynamic-update-slice_fusion.12
  259.0 1.7 constant_dynamic-update-slice_fusion.8
  260.6 1.7 constant_dynamic-update-slice_fusion.7
  262.3 1.4 fusion.26
  263.8 1.6 collective-permute-start.24
  265.7 6.1 %collective-permute-done.24 = bf16[256,672]{1,0:T(8,128)(2,1)S(1)} collective-permute-done((bf16[256,672]{1,0:T(8,128)(2,1)}, bf16[256,672]{1,0:T(8,128)(2,1)S(1)}, u32[]{:S(2)}, u32[]{:S(2)}) %collective-permute-start.24) | collective-permute-done | bytes 344096 | tf_op jit(solution)/shard_map/ppermute | solution.py:64
  273.3 1.8 broadcast_select_fusion
  275.2 4.1 all-to-all-start
  279.6 8.6 %all-to-all-done = bf16[4,64,672]{2,1,0:T(8,128)(2,1)} async-done(((bf16[4,64,672]{2,1,0:T(8,128)(2,1)}), bf16[4,64,672]{2,1,0:T(8,128)(2,1)}, u32[]{:S(2)}, u32[]{:S(2)}) %all-to-all-start) | async-done | bytes 344096 | tf_op jit(solution)/shard_map/all_to_all | solution.py:138
  289.3 1.7 fusion.33
  292.2 2.6 fusion
  294.9 33.2 %all-reduce.5.cloned.1.call-done = bf16[256,1280]{1,0:T(8,128)(2,1)} async-done(((bf16[256,1280]{1,0:T(8,128)(2,1)}), bf16[256,1280]{1,0:T(8,128)(2,1)}) %all-reduce.5.cloned.1.call-update) | async-done | bytes 655376 | tf_op jit(solution)/shard_map/psum | solution.py:154
  328.1 1.7 convert_reduce_fusion
  329.8 4.2 convolution_convert_fusion.1
  334.1 1.6 copy.14
  336.9 2.0 pad_maximum_fusion
  339.8 1.4 convolution_convert_fusion.5
  341.3 60.1 %reduce-scatter.6.cloned.1.call-done = bf16[2,320,640]{2,1,0:T(8,128)(2,1)} async-done(((bf16[2,1280,640]{2,1,0:T(8,128)(2,1)}), bf16[2,320,640]{2,1,0:T(8,128)(2,1)}) %reduce-scatter.6.cloned.1.call-update) | async-done | bytes 819216 | tf_op jit(solution)/shard_map/reduce_scatter | solution.py:168
  402.6 1.6 collective-permute-start.31
  404.2 26.4 %reduce-scatter.8.cloned.1.call-done = bf16[160,672]{1,0:T(8,128)(2,1)} async-done(((bf16[640,672]{1,0:T(8,128)(2,1)}), bf16[160,672]{1,0:T(8,128)(2,1)}) %reduce-scatter.8.cloned.1.call-update) | async-done | bytes 215056 | tf_op jit(solution)/shard_map/reduce_scatter | solution.py:157
  430.6 1.6 slice.125
  432.2 1.6 slice.126
  (172 shorter events, 58.5 us)
Async XLA Ops:
  8.0 254.3 %all-reduce.3.cloned.1.call-start = ((), (), s32[]{:S(2)}) async-start(), calls=%async_computation.4 | async-start | bytes 1310720 | tf_op jit(solution)/shard_map/psum | solution.py:146
  8.0 8.8 %copy-start.6 = (bf16[2,320,1280]{2,1,0:T(8,128)(2,1)S(1)}, bf16[2,320,1280]{2,1,0:T(8,128)(2,1)}, u32[]{:S(2)}) copy-start(bf16[2,320,1280]{2,1,0:T(8,128)(2,1)} %param.14) | copy-start | bytes 4915204
  9.6 14.3 %copy-start.2 = (bf16[3,384,1024]{2,1,0:T(8,128)(2,1)S(1)}, bf16[3,384,1024]{2,1,0:T(8,128)(2,1)}, u32[]{:S(2)}) copy-start(bf16[3,384,1024]{2,1,0:T(8,128)(2,1)} %param.12) | copy-start | bytes 7077892
  9.6 23.3 %collective-permute-start.18 = (bf16[2,288,564]{2,1,0:T(8,128)(2,1)S(1)}, bf16[2,288,564]{2,1,0:T(8,128)(2,1)}, u32[]{:S(2)}, u32[]{:S(2)}) collective-permute-start(bf16[2,288,564]{2,1,0:T(8,128)(2,1)S(1)} %slice_select_fusion.2), channel_id=1, source_target_pairs={{0,4},{4,8},{8,12},{1,5},{5,9},{9,13},{2,6},{6,10},{10,14},{3,7},{... | collective-permute-start | bytes 1949192 | tf_op jit(solution)/shard_map/ppermute | solution.py:48
  15.6 21.3 %collective-permute-start.21 = (bf16[2,288,564]{2,1,0:T(8,128)(2,1)S(1)}, bf16[2,288,564]{2,1,0:T(8,128)(2,1)S(1)}, u32[]{:S(2)}, u32[]{:S(2)}) collective-permute-start(bf16[2,288,564]{2,1,0:T(8,128)(2,1)S(1)} %slice_select_fusion.2), channel_id=1, source_target_pairs={{4,0},{8,4},{12,8},{5,1},{9,5},{13,9},{6,2},{10,6},{14,10},{7,3},{... | collective-permute-start | bytes 1949192 | tf_op jit(solution)/shard_map/ppermute | solution.py:50
  17.0 13.8 %copy-start.3 = (bf16[4,64,1536]{2,1,0:T(8,128)(2,1)S(1)}, bf16[4,64,1536]{2,1,0:T(8,128)(2,1)}, u32[]{:S(2)}) copy-start(bf16[4,64,1536]{2,1,0:T(8,128)(2,1)} %param.9) | copy-start | bytes 2359300
  17.0 32.1 %collective-permute-start = (bf16[2,320,640]{2,1,0:T(8,128)(2,1)S(1)}, bf16[2,320,640]{2,1,0:T(8,128)(2,1)}, u32[]{:S(2)}, u32[]{:S(2)}) collective-permute-start(bf16[2,320,640]{2,1,0:T(8,128)(2,1)S(1)} %slice_select_fusion.1), channel_id=1, source_target_pairs={{0,4},{4,8},{8,12},{1,5},{5,9},{9,13},{2,6},{6,10},{10,14},{3,7},{... | collective-permute-start | bytes 2457608 | tf_op jit(solution)/shard_map/ppermute | solution.py:48
  22.7 31.9 %collective-permute-start.3 = (bf16[2,320,640]{2,1,0:T(8,128)(2,1)S(1)}, bf16[2,320,640]{2,1,0:T(8,128)(2,1)}, u32[]{:S(2)}, u32[]{:S(2)}) collective-permute-start(bf16[2,320,640]{2,1,0:T(8,128)(2,1)S(1)} %slice_select_fusion.1), channel_id=1, source_target_pairs={{4,0},{8,4},{12,8},{5,1},{9,5},{13,9},{6,2},{10,6},{14,10},{7,3},{... | collective-permute-start | bytes 2457608 | tf_op jit(solution)/shard_map/ppermute | solution.py:50
  25.1 7.5 %copy-start = (bf16[1,256,1280]{2,1,0:T(8,128)(2,1)S(1)}, bf16[1,256,1280]{2,1,0:T(8,128)(2,1)}, u32[]{:S(2)}) copy-start(bf16[1,256,1280]{2,1,0:T(8,128)(2,1)} %param.11) | copy-start | bytes 1966084
  25.1 48.3 %collective-permute-start.12 = (bf16[3,384,512]{2,1,0:T(8,128)(2,1)}, bf16[3,384,512]{2,1,0:T(8,128)(2,1)}, u32[]{:S(2)}, u32[]{:S(2)}) collective-permute-start(bf16[3,384,512]{2,1,0:T(8,128)(2,1)} %slice_select_fusion), channel_id=1, source_target_pairs={{0,4},{4,8},{8,12},{1,5},{5,9},{9,13},{2,6},{6,10},{10,14},{3,7},{... | collective-permute-start | bytes 3538952 | tf_op jit(solution)/shard_map/ppermute | solution.py:48
  31.0 1.8 copy-start.5
  32.9 41.7 %collective-permute-start.19 = (bf16[2,288,564]{2,1,0:T(8,128)(2,1)}, bf16[2,288,564]{2,1,0:T(8,128)(2,1)}, u32[]{:S(2)}, u32[]{:S(2)}) collective-permute-start(bf16[2,288,564]{2,1,0:T(8,128)(2,1)} %collective-permute-done.18), channel_id=1, source_target_pairs={{4,8},{8,12},{5,9},{9,13},{6,10},{10,14},{7,11},{11,15},{20,24},{2... | collective-permute-start | bytes 1949192 | tf_op jit(solution)/shard_map/ppermute | solution.py:48
  36.9 17.7 %copy-start.16 = (bf16[2,288,564]{2,1,0:T(8,128)(2,1)}, bf16[2,288,564]{2,1,0:T(8,128)(2,1)S(1)}, u32[]{:S(2)}) copy-start(bf16[2,288,564]{2,1,0:T(8,128)(2,1)S(1)} %collective-permute-done.21) | copy-start | bytes 1949188
  36.9 42.9 %collective-permute-start.15 = (bf16[3,384,512]{2,1,0:T(8,128)(2,1)}, bf16[3,384,512]{2,1,0:T(8,128)(2,1)}, u32[]{:S(2)}, u32[]{:S(2)}) collective-permute-start(bf16[3,384,512]{2,1,0:T(8,128)(2,1)} %slice_select_fusion), channel_id=1, source_target_pairs={{4,0},{8,4},{12,8},{5,1},{9,5},{13,9},{6,2},{10,6},{14,10},{7,3},{... | collective-permute-start | bytes 3538952 | tf_op jit(solution)/shard_map/ppermute | solution.py:50
  49.1 63.9 %collective-permute-start.1 = (bf16[2,320,640]{2,1,0:T(8,128)(2,1)}, bf16[2,320,640]{2,1,0:T(8,128)(2,1)}, u32[]{:S(2)}, u32[]{:S(2)}) collective-permute-start(bf16[2,320,640]{2,1,0:T(8,128)(2,1)} %collective-permute-done), channel_id=1, source_target_pairs={{4,8},{8,12},{5,9},{9,13},{6,10},{10,14},{7,11},{11,15},{20,24},{2... | collective-permute-start | bytes 2457608 | tf_op jit(solution)/shard_map/ppermute | solution.py:48
  54.6 59.8 %collective-permute-start.4 = (bf16[2,320,640]{2,1,0:T(8,128)(2,1)}, bf16[2,320,640]{2,1,0:T(8,128)(2,1)}, u32[]{:S(2)}, u32[]{:S(2)}) collective-permute-start(bf16[2,320,640]{2,1,0:T(8,128)(2,1)} %collective-permute-done.3), channel_id=1, source_target_pairs={{4,0},{8,4},{5,1},{9,5},{6,2},{10,6},{7,3},{11,7},{20,16},{24,20},... | collective-permute-start | bytes 2457608 | tf_op jit(solution)/shard_map/ppermute | solution.py:50
  73.4 38.4 %collective-permute-start.22 = (bf16[2,288,564]{2,1,0:T(8,128)(2,1)}, bf16[2,288,564]{2,1,0:T(8,128)(2,1)}, u32[]{:S(2)}, u32[]{:S(2)}) collective-permute-start(bf16[2,288,564]{2,1,0:T(8,128)(2,1)} %copy-done.16), channel_id=1, source_target_pairs={{4,0},{8,4},{5,1},{9,5},{6,2},{10,6},{7,3},{11,7},{20,16},{24,20},... | collective-permute-start | bytes 1949192 | tf_op jit(solution)/shard_map/ppermute | solution.py:50
  74.7 41.3 %collective-permute-start.20 = (bf16[2,288,564]{2,1,0:T(8,128)(2,1)}, bf16[2,288,564]{2,1,0:T(8,128)(2,1)}, u32[]{:S(2)}, u32[]{:S(2)}) collective-permute-start(bf16[2,288,564]{2,1,0:T(8,128)(2,1)} %collective-permute-done.19), channel_id=1, source_target_pairs={{8,12},{9,13},{10,14},{11,15},{24,28},{25,29},{26,30},{27,31}} | collective-permute-start | bytes 1949192 | tf_op jit(solution)/shard_map/ppermute | solution.py:48
  79.8 88.1 %collective-permute-start.13 = (bf16[3,384,512]{2,1,0:T(8,128)(2,1)}, bf16[3,384,512]{2,1,0:T(8,128)(2,1)}, u32[]{:S(2)}, u32[]{:S(2)}) collective-permute-start(bf16[3,384,512]{2,1,0:T(8,128)(2,1)} %collective-permute-done.12), channel_id=1, source_target_pairs={{4,8},{8,12},{5,9},{9,13},{6,10},{10,14},{7,11},{11,15},{20,24},{2... | collective-permute-start | bytes 3538952 | tf_op jit(solution)/shard_map/ppermute | solution.py:48
  111.7 57.9 %collective-permute-start.16 = (bf16[3,384,512]{2,1,0:T(8,128)(2,1)}, bf16[3,384,512]{2,1,0:T(8,128)(2,1)}, u32[]{:S(2)}, u32[]{:S(2)}) collective-permute-start(bf16[3,384,512]{2,1,0:T(8,128)(2,1)} %collective-permute-done.15), channel_id=1, source_target_pairs={{4,0},{8,4},{5,1},{9,5},{6,2},{10,6},{7,3},{11,7},{20,16},{24,20},... | collective-permute-start | bytes 3538952 | tf_op jit(solution)/shard_map/ppermute | solution.py:50
  113.0 45.5 %collective-permute-start.23 = (bf16[2,288,564]{2,1,0:T(8,128)(2,1)}, bf16[2,288,564]{2,1,0:T(8,128)(2,1)S(1)}, u32[]{:S(2)}, u32[]{:S(2)}) collective-permute-start(bf16[2,288,564]{2,1,0:T(8,128)(2,1)} %collective-permute-done.22), channel_id=1, source_target_pairs={{4,0},{5,1},{6,2},{7,3},{20,16},{21,17},{22,18},{23,19}} | collective-permute-start | bytes 1949192 | tf_op jit(solution)/shard_map/ppermute | solution.py:50
  114.3 56.6 %collective-permute-start.2 = (bf16[2,320,640]{2,1,0:T(8,128)(2,1)}, bf16[2,320,640]{2,1,0:T(8,128)(2,1)}, u32[]{:S(2)}, u32[]{:S(2)}) collective-permute-start(bf16[2,320,640]{2,1,0:T(8,128)(2,1)} %collective-permute-done.1), channel_id=1, source_target_pairs={{8,12},{9,13},{10,14},{11,15},{24,28},{25,29},{26,30},{27,31}} | collective-permute-start | bytes 2457608 | tf_op jit(solution)/shard_map/ppermute | solution.py:48
  115.9 61.7 %collective-permute-start.5 = (bf16[2,320,640]{2,1,0:T(8,128)(2,1)}, bf16[2,320,640]{2,1,0:T(8,128)(2,1)}, u32[]{:S(2)}, u32[]{:S(2)}) collective-permute-start(bf16[2,320,640]{2,1,0:T(8,128)(2,1)} %collective-permute-done.4), channel_id=1, source_target_pairs={{4,0},{5,1},{6,2},{7,3},{20,16},{21,17},{22,18},{23,19}} | collective-permute-start | bytes 2457608 | tf_op jit(solution)/shard_map/ppermute | solution.py:50
  118.4 2.7 copy-start.4
  119.7 1.5 copy-start.17
  158.6 2.3 copy-start.29
  167.9 16.4 %collective-permute-start.14 = (bf16[3,384,512]{2,1,0:T(8,128)(2,1)}, bf16[3,384,512]{2,1,0:T(8,128)(2,1)}, u32[]{:S(2)}, u32[]{:S(2)}) collective-permute-start(bf16[3,384,512]{2,1,0:T(8,128)(2,1)} %collective-permute-done.13), channel_id=1, source_target_pairs={{8,12},{9,13},{10,14},{11,15},{24,28},{25,29},{26,30},{27,31}} | collective-permute-start | bytes 3538952 | tf_op jit(solution)/shard_map/ppermute | solution.py:48
  169.6 29.5 %collective-permute-start.17 = (bf16[3,384,512]{2,1,0:T(8,128)(2,1)}, bf16[3,384,512]{2,1,0:T(8,128)(2,1)}, u32[]{:S(2)}, u32[]{:S(2)}) collective-permute-start(bf16[3,384,512]{2,1,0:T(8,128)(2,1)} %collective-permute-done.16), channel_id=1, source_target_pairs={{4,0},{5,1},{6,2},{7,3},{20,16},{21,17},{22,18},{23,19}} | collective-permute-start | bytes 3538952 | tf_op jit(solution)/shard_map/ppermute | solution.py:50
  172.1 2.7 copy-start.7
  178.9 2.8 copy-start.12
  184.1 79.7 %reduce-scatter.4.cloned.1.call-start = ((), (), s32[]{:S(2)}) async-start(), calls=%async_computation.5 | async-start | bytes 1966080 | tf_op jit(solution)/shard_map/reduce_scatter | solution.py:127
  191.5 12.2 %copy-start.9 = (bf16[4,64,1536]{2,1,0:T(8,128)(2,1)S(1)}, bf16[4,64,1536]{2,1,0:T(8,128)(2,1)}, u32[]{:S(2)}) copy-start(bf16[4,64,1536]{2,1,0:T(8,128)(2,1)} %fusion.7) | copy-start | bytes 2359300
  200.4 3.2 copy-start.13
  210.9 3.7 copy-start.23
  210.9 11.3 %copy-start.30 = (s32[4]{0:T(128)S(1)}, s32[4]{0:T(128)}, u32[]{:S(2)}) copy-start(s32[4]{0:T(128)} %param.17) | copy-start | bytes 52
  211.8 8.9 %collective-permute-start.6 = (bf16[320,384]{1,0:T(8,128)(2,1)S(1)}, bf16[320,384]{1,0:T(8,128)(2,1)S(1)}, u32[]{:S(2)}, u32[]{:S(2)}) collective-permute-start(bf16[320,384]{1,0:T(8,128)(2,1)S(1)} %copy-done.22), channel_id=1, source_target_pairs={{0,4},{4,8},{8,12},{1,5},{5,9},{9,13},{2,6},{6,10},{10,14},{3,7},{... | collective-permute-start | bytes 737288 | tf_op jit(solution)/shard_map/ppermute | solution.py:48
  213.2 16.9 %collective-permute-start.9 = (bf16[320,384]{1,0:T(8,128)(2,1)S(1)}, bf16[320,384]{1,0:T(8,128)(2,1)S(1)}, u32[]{:S(2)}, u32[]{:S(2)}) collective-permute-start(bf16[320,384]{1,0:T(8,128)(2,1)S(1)} %copy-done.22), channel_id=1, source_target_pairs={{4,0},{8,4},{12,8},{5,1},{9,5},{13,9},{6,2},{10,6},{14,10},{7,3},{... | collective-permute-start | bytes 737288 | tf_op jit(solution)/shard_map/ppermute | solution.py:50
  214.5 8.7 %collective-permute-start.25 = (bf16[320,288]{0,1:T(8,128)(2,1)S(1)}, bf16[320,288]{0,1:T(8,128)(2,1)S(1)}, u32[]{:S(2)}, u32[]{:S(2)}) collective-permute-start(bf16[320,288]{0,1:T(8,128)(2,1)S(1)} %copy-done.23), channel_id=1, source_target_pairs={{0,4},{4,8},{8,12},{1,5},{5,9},{9,13},{2,6},{6,10},{10,14},{3,7},{... | collective-permute-start | bytes 552968 | tf_op jit(solution)/shard_map/ppermute | solution.py:48
  219.4 8.4 %collective-permute-start.28 = (bf16[320,288]{0,1:T(8,128)(2,1)S(1)}, bf16[320,288]{0,1:T(8,128)(2,1)S(1)}, u32[]{:S(2)}, u32[]{:S(2)}) collective-permute-start(bf16[320,288]{0,1:T(8,128)(2,1)S(1)} %copy-done.23), channel_id=1, source_target_pairs={{4,0},{8,4},{12,8},{5,1},{9,5},{13,9},{6,2},{10,6},{14,10},{7,3},{... | collective-permute-start | bytes 552968 | tf_op jit(solution)/shard_map/ppermute | solution.py:50
  220.8 10.7 %collective-permute-start.7 = (bf16[320,384]{1,0:T(8,128)(2,1)S(1)}, bf16[320,384]{1,0:T(8,128)(2,1)}, u32[]{:S(2)}, u32[]{:S(2)}) collective-permute-start(bf16[320,384]{1,0:T(8,128)(2,1)S(1)} %collective-permute-done.6), channel_id=1, source_target_pairs={{4,8},{8,12},{5,9},{9,13},{6,10},{10,14},{7,11},{11,15},{20,24},{2... | collective-permute-start | bytes 737288 | tf_op jit(solution)/shard_map/ppermute | solution.py:48
  223.2 24.4 %copy-start.24 = (bf16[320,288]{0,1:T(8,128)(2,1)}, bf16[320,288]{0,1:T(8,128)(2,1)S(1)}, u32[]{:S(2)}) copy-start(bf16[320,288]{0,1:T(8,128)(2,1)S(1)} %collective-permute-done.25) | copy-start | bytes 552964
  223.2 9.6 %collective-permute-start.26 = (bf16[320,288]{0,1:T(8,128)(2,1)S(1)}, bf16[320,288]{0,1:T(8,128)(2,1)S(1)}, u32[]{:S(2)}, u32[]{:S(2)}) collective-permute-start(bf16[320,288]{0,1:T(8,128)(2,1)S(1)} %collective-permute-done.25), channel_id=1, source_target_pairs={{4,8},{8,12},{5,9},{9,13},{6,10},{10,14},{7,11},{11,15},{20,24},{2... | collective-permute-start | bytes 552968 | tf_op jit(solution)/shard_map/ppermute | solution.py:48
  227.8 19.7 %copy-start.25 = (bf16[320,288]{0,1:T(8,128)(2,1)}, bf16[320,288]{0,1:T(8,128)(2,1)S(1)}, u32[]{:S(2)}) copy-start(bf16[320,288]{0,1:T(8,128)(2,1)S(1)} %collective-permute-done.28) | copy-start | bytes 552964
  227.8 13.2 %collective-permute-start.29 = (bf16[320,288]{0,1:T(8,128)(2,1)S(1)}, bf16[320,288]{0,1:T(8,128)(2,1)S(1)}, u32[]{:S(2)}, u32[]{:S(2)}) collective-permute-start(bf16[320,288]{0,1:T(8,128)(2,1)S(1)} %collective-permute-done.28), channel_id=1, source_target_pairs={{4,0},{8,4},{5,1},{9,5},{6,2},{10,6},{7,3},{11,7},{20,16},{24,20},... | collective-permute-start | bytes 552968 | tf_op jit(solution)/shard_map/ppermute | solution.py:50
  230.1 16.2 %collective-permute-start.10 = (bf16[320,384]{1,0:T(8,128)(2,1)S(1)}, bf16[320,384]{1,0:T(8,128)(2,1)}, u32[]{:S(2)}, u32[]{:S(2)}) collective-permute-start(bf16[320,384]{1,0:T(8,128)(2,1)S(1)} %collective-permute-done.9), channel_id=1, source_target_pairs={{4,0},{8,4},{5,1},{9,5},{6,2},{10,6},{7,3},{11,7},{20,16},{24,20},... | collective-permute-start | bytes 737288 | tf_op jit(solution)/shard_map/ppermute | solution.py:50
  231.4 22.1 %collective-permute-start.8 = (bf16[320,384]{1,0:T(8,128)(2,1)}, bf16[320,384]{1,0:T(8,128)(2,1)}, u32[]{:S(2)}, u32[]{:S(2)}) collective-permute-start(bf16[320,384]{1,0:T(8,128)(2,1)} %collective-permute-done.7), channel_id=1, source_target_pairs={{8,12},{9,13},{10,14},{11,15},{24,28},{25,29},{26,30},{27,31}} | collective-permute-start | bytes 737288 | tf_op jit(solution)/shard_map/ppermute | solution.py:48
  232.8 14.8 %copy-start.26 = (bf16[320,288]{0,1:T(8,128)(2,1)}, bf16[320,288]{0,1:T(8,128)(2,1)S(1)}, u32[]{:S(2)}) copy-start(bf16[320,288]{0,1:T(8,128)(2,1)S(1)} %collective-permute-done.26) | copy-start | bytes 552964
  232.8 14.8 %collective-permute-start.27 = (bf16[320,288]{0,1:T(8,128)(2,1)S(1)}, bf16[320,288]{0,1:T(8,128)(2,1)S(1)}, u32[]{:S(2)}, u32[]{:S(2)}) collective-permute-start(bf16[320,288]{0,1:T(8,128)(2,1)S(1)} %collective-permute-done.26), channel_id=1, source_target_pairs={{8,12},{9,13},{10,14},{11,15},{24,28},{25,29},{26,30},{27,31}} | collective-permute-start | bytes 552968 | tf_op jit(solution)/shard_map/ppermute | solution.py:48
  241.0 6.6 %copy-start.27 = (bf16[320,288]{0,1:T(8,128)(2,1)}, bf16[320,288]{0,1:T(8,128)(2,1)S(1)}, u32[]{:S(2)}) copy-start(bf16[320,288]{0,1:T(8,128)(2,1)S(1)} %collective-permute-done.29) | copy-start | bytes 552964
  241.0 9.9 %collective-permute-start.30 = (bf16[320,288]{0,1:T(8,128)(2,1)S(1)}, bf16[320,288]{0,1:T(8,128)(2,1)}, u32[]{:S(2)}, u32[]{:S(2)}) collective-permute-start(bf16[320,288]{0,1:T(8,128)(2,1)S(1)} %collective-permute-done.29), channel_id=1, source_target_pairs={{4,0},{5,1},{6,2},{7,3},{20,16},{21,17},{22,18},{23,19}} | collective-permute-start | bytes 552968 | tf_op jit(solution)/shard_map/ppermute | solution.py:50
  246.3 14.3 %collective-permute-start.11 = (bf16[320,384]{1,0:T(8,128)(2,1)}, bf16[320,384]{1,0:T(8,128)(2,1)}, u32[]{:S(2)}, u32[]{:S(2)}) collective-permute-start(bf16[320,384]{1,0:T(8,128)(2,1)} %collective-permute-done.10), channel_id=1, source_target_pairs={{4,0},{5,1},{6,2},{7,3},{20,16},{21,17},{22,18},{23,19}} | collective-permute-start | bytes 737288 | tf_op jit(solution)/shard_map/ppermute | solution.py:50
  262.3 3.0 copy-start.1
  263.8 8.1 %copy-start.19 = (bf16[1,256,672]{2,1,0:T(8,128)(2,1)S(1)}, bf16[1,256,672]{2,1,0:T(8,128)(2,1)}, u32[]{:S(2)}) copy-start(bf16[1,256,672]{2,1,0:T(8,128)(2,1)} %reduce-scatter.4.cloned.1.call-done) | copy-start | bytes 1032196
  263.8 8.1 %collective-permute-start.24 = (bf16[256,672]{1,0:T(8,128)(2,1)}, bf16[256,672]{1,0:T(8,128)(2,1)S(1)}, u32[]{:S(2)}, u32[]{:S(2)}) collective-permute-start(bf16[256,672]{1,0:T(8,128)(2,1)} %bitcast.152), channel_id=1, source_target_pairs={{0,16},{16,0},{1,17},{17,1},{2,18},{18,2},{3,19},{19,3},{4,20},{20... | collective-permute-start | bytes 1032200 | tf_op jit(solution)/shard_map/ppermute | solution.py:64
  275.2 13.1 %all-to-all-start = ((bf16[4,64,672]{2,1,0:T(8,128)(2,1)}), bf16[4,64,672]{2,1,0:T(8,128)(2,1)}, u32[]{:S(2)}, u32[]{:S(2)}) async-start(bf16[4,64,672]{2,1,0:T(8,128)(2,1)} %broadcast_select_fusion), calls=%async_computation.1 | async-start | bytes 786432 | tf_op jit(solution)/shard_map/all_to_all | solution.py:138
  279.3 48.8 %all-reduce.5.cloned.1.call-start = ((), (), s32[]{:S(2)}) async-start(), calls=%async_computation.6 | async-start | bytes 1310720 | tf_op jit(solution)/shard_map/psum | solution.py:154
  291.0 1.2 copy-start.10
  294.8 35.0 %copy-start.31 = (f32[256,640]{1,0:T(8,128)S(1)}, f32[256,640]{1,0:T(8,128)}, u32[]{:S(2)}) copy-start(f32[256,640]{1,0:T(8,128)} %get-tuple-element.16) | copy-start | bytes 1966084
  294.8 106.5 %reduce-scatter.6.cloned.1.call-start = ((), (), s32[]{:S(2)}) async-start(), calls=%async_computation.7 | async-start | bytes 4096000 | tf_op jit(solution)/shard_map/reduce_scatter | solution.py:168
  328.1 1.7 copy-start.18
  334.1 1.6 copy-start.21
  338.9 91.6 %reduce-scatter.8.cloned.1.call-start = ((), (), s32[]{:S(2)}) async-start(), calls=%async_computation.8 | async-start | bytes 1228800 | tf_op jit(solution)/shard_map/reduce_scatter | solution.py:157
  401.4 32.4 %copy-start.8 = (bf16[2,320,640]{2,1,0:T(8,128)(2,1)S(1)}, bf16[2,320,640]{2,1,0:T(8,128)(2,1)}, u32[]{:S(2)}) copy-start(bf16[2,320,640]{2,1,0:T(8,128)(2,1)} %reduce-scatter.6.cloned.1.call-done) | copy-start | bytes 2457604
  402.6 31.2 %collective-permute-start.31 = (bf16[2,160,640]{2,1,0:T(8,128)(2,1)S(1)}, bf16[2,160,640]{2,1,0:T(8,128)(2,1)S(1)}, u32[]{:S(2)}, u32[]{:S(2)}) collective-permute-start(bf16[2,160,640]{2,1,0:T(8,128)(2,1)S(1)} %fusion.76), channel_id=1, source_target_pairs={{0,16},{16,0},{1,17},{17,1},{2,18},{18,2},{3,19},{19,3},{4,20},{20... | collective-permute-start | bytes 1228808 | tf_op jit(solution)/shard_map/ppermute | solution.py:64
  (6 other events, 5.2 us)
Sparse Core Ops, SparseCore 0:
  184.2 62.3 all-reduce.2
  339.1 62.2 reduce-scatter.5
  404.3 26.2 reduce-scatter.7
Sparse Core Ops, SparseCore 1:
  211.0 29.3 reduce-scatter.3
  294.9 33.1 all-reduce.4

commit v2 on v1

--- a/solution.py
+++ b/solution.py
@@ -58,6 +58,31 @@
 def own_units(weights, group, low):
     count = weights.shape[-1]
     return jnp.where(group == 0, weights[..., : count - low], weights[..., low:])
+
+
+def summed_piece(pieces, axis):
+    count = lax.axis_size(axis)
+    if count > 8:
+        return lax.psum_scatter(pieces, axis, scatter_dimension=0).astype(jnp.float32)
+    me = lax.axis_index(axis)
+    total = lax.dynamic_index_in_dim(pieces, me, 0, keepdims=False).astype(jnp.float32)
+    for step in range(1, count):
+        piece = lax.dynamic_index_in_dim(pieces, (me + step) % count, 0, keepdims=False)
+        pairs = [(i, (i + step) % count) for i in range(count)]
+        total = total + lax.ppermute(piece, axis, pairs).astype(jnp.float32)
+    return total
+
+
+def joined_pieces(piece, axis):
+    count = lax.axis_size(axis)
+    if count > 8:
+        return lax.all_gather(piece, axis, axis=0)
+    got = [piece]
+    for step in range(1, count):
+        got.append(lax.ppermute(piece, axis, [(i, (i + step) % count) for i in range(count)]))
+    got = got[::-1]
+    line = jnp.stack(got + got[:-1])
+    return lax.dynamic_slice_in_dim(line, count - 1 - lax.axis_index(axis), count, 0)
 
 
 def across(array):
@@ -124,7 +149,7 @@
             for i in range(count_tp)
         ]
     )
-    summed = lax.psum_scatter(parts, "tp", scatter_dimension=0, tiled=True)[0].astype(bf16)
+    summed = summed_piece(parts, "tp").astype(bf16)
     summed = summed.astype(f32) + across(summed).astype(f32)
     own = jnp.concatenate(
         [
@@ -151,11 +176,14 @@
     diff_s = ((pred_s - target[:, cols_d:]) * scale).astype(bf16)
 
     dfeat = times_transposed(diff_d, w_dino) + times_transposed(diff_s, w_sig)
-    dfeat = lax.psum(dfeat.astype(bf16), "tp").astype(f32)
+    dfeat = summed_piece(dfeat.astype(bf16).reshape(count_tp, rows // count_tp, width), "tp")
+    own_mixed = lax.dynamic_slice_in_dim(
+        mixed, column * (rows // count_tp), rows // count_tp, 0
+    )
+    dmixed = joined_pieces(norm_back(own_mixed, dfeat).astype(bf16), "tp").reshape(rows, width)
     own_feat = lax.dynamic_slice_in_dim(feat, group * half, half, 1)
     grad_heads = over_rows(own_feat, jnp.concatenate([diff_d, diff_s], axis=1)).astype(bf16)
-    sum_heads = lax.psum_scatter(grad_heads, "dp", scatter_dimension=0, tiled=True).astype(f32)
-    dmixed = norm_back(mixed, dfeat).astype(bf16)
+    sum_heads = summed_piece(grad_heads.reshape(count_dp, block, cols_d + cols_s), "dp")
     grad_down = over_rows(dmixed, hidden).astype(bf16)
     dhidden = jnp.dot(dmixed, w_mlp[1], preferred_element_type=f32)
     dact = (dhidden * gelu_slope(act)).astype(bf16)

time: 445 us -> 476 us (1.070)
  waiting for transfers between devices: 262 us -> 282 us
  starting transfers between devices: 64.2 us -> 73.4 us
  other arithmetic: 21.5 us -> 26.4 us
    ppermute x15, waiting for transfers between devices: 99.2 us -> 145 us  [gathered_rows(): lax.ppermute(down[-1], 'dp', [(i, i - 1) for i in range(1, count - step +...]
    psum x1 -> x0, waiting for transfers between devices: 33.2 us -> none  [body(): dfeat = lax.psum(dfeat.astype(bf16), 'tp').astype(f32)]
    psum x1, waiting for transfers between devices: 0.01 us -> 30.7 us  [body(): mixed = flat + lax.psum(partial_out.astype(bf16), ('grp', 'tp')).astype(f32)]
    ppermute x15, waiting for transfers between devices: 28.2 us -> 0.04 us  [gathered_rows(): lax.ppermute(up[-1], 'dp', [(i, i + 1) for i in range(step - 1, count - 1)])]
    reduce_scatter x2 -> x0, waiting for transfers between devices: 26.4 us -> none  [the longest x1 26.4 us: body(): lax.psum_scatter(grad_heads, 'dp', scatter_dimension=0, tiled=True)]
    ppermute x0 -> x12, waiting for transfers between devices: none -> 13.9 us  [the longest x3 8.04 us: joined_pieces(): lax.ppermute(piece, axis, [(i, (i + step) % count) for i in range(count)])]
    ppermute x0 -> x12, starting transfers between devices: none -> 12.5 us  [the longest x9 8.66 us: summed_piece(): total = total + lax.ppermute(piece, axis, pairs).astype(jnp.float32)]
    ppermute x2, waiting for transfers between devices: 6.12 us -> 16.5 us  [across(): return lax.ppermute(array, 'grp', [(0, 1), (1, 0)])]
  transfers between devices with their start and end apart: 38 -> 47, of which waited for: 17 -> 17; matrix products, arithmetic and copies ran while one was open for 15% -> 15% of each run, Pallas kernels for 0% -> 0%
where the time goes in v2:
time: 476 us; the launch traced here: 471 us
  waiting for transfers between devices  282 us (59%)
  starting transfers between devices  73.4 us (15%)
  local copies, waits for them, and re-layouts  49.3 us (10%)
  other arithmetic  26.4 us (6%)
  matrix products  25 us (5%)
  between operations  15.3 us (3%)
    ppermute x15, waiting for transfers between devices, gathered_rows(): lax.ppermute(down[-1], 'dp', [(i, i - 1) for i in range(1, count - step +...  145 us
    reduce_scatter x1, waiting for transfers between devices, body(): sum_mlp = lax.psum_scatter(grad_mlp, 'dp', scatter_dimension=1, tiled=True)  67 us
    ppermute x15, starting transfers between devices, gathered_rows(): lax.ppermute(up[-1], 'dp', [(i, i + 1) for i in range(step - 1, count - 1)])  34.9 us
    psum x1, waiting for transfers between devices, body(): mixed = flat + lax.psum(partial_out.astype(bf16), ('grp', 'tp')).astype(f32)  30.7 us
    unnamed x141, local copies, waits for them, and re-layouts  30.3 us
    ppermute x15, starting transfers between devices, gathered_rows(): lax.ppermute(down[-1], 'dp', [(i, i - 1) for i in range(1, count - step +...  19.5 us
    ppermute x2, waiting for transfers between devices, across(): return lax.ppermute(array, 'grp', [(0, 1), (1, 0)])  16.5 us
    dot_general x5, matrix products, times_transposed(): lax.dot_general(left, right, (((1,), (1,)), ((), ())), preferred_element_...  12.7 us
  transfers between devices with their start and end apart: 47, of which 17 were waited for; matrix products, arithmetic and copies ran while one was open for 15% of the time, Pallas kernels for 0%

profile of v2, /device:TPU:0, one launch (start us, length us, event | category | flops | bytes accessed | tf_op | source)
XLA Modules:
  0.0 470.9 jit_solution(13698602644856803414)
XLA Ops:
  7.2 4.9 %collective-permute-start.6 = (bf16[320,384]{1,0:T(8,128)(2,1)}, bf16[320,384]{1,0:T(8,128)(2,1)S(1)}, u32[]{:S(2)}, u32[]{:S(2)}) collective-permute-start(bf16[320,384]{1,0:T(8,128)(2,1)} %param.15), channel_id=1, source_target_pairs={{0,4},{4,8},{8,12},{1,5},{5,9},{9,13},{2,6},{6,10},{10,14},{3,7},{... | collective-permute-start | bytes 737288 | tf_op jit(solution)/shard_map/ppermute | solution.py:48
  13.5 4.6 collective-permute-start.28
  19.3 1.4 slice_select_fusion.2
  20.8 5.6 %collective-permute-start.18 = (bf16[2,288,564]{2,1,0:T(8,128)(2,1)S(1)}, bf16[2,288,564]{2,1,0:T(8,128)(2,1)}, u32[]{:S(2)}, u32[]{:S(2)}) collective-permute-start(bf16[2,288,564]{2,1,0:T(8,128)(2,1)S(1)} %slice_select_fusion.2), channel_id=1, source_target_pairs={{0,4},{4,8},{8,12},{1,5},{5,9},{9,13},{2,6},{6,10},{10,14},{3,7},{... | collective-permute-start | bytes 1949192 | tf_op jit(solution)/shard_map/ppermute | solution.py:48
  26.4 2.8 slice_select_fusion
  39.1 23.3 %collective-permute-done.32 = bf16[320,288]{0,1:T(8,128)(2,1)S(1)} collective-permute-done((bf16[320,288]{0,1:T(8,128)(2,1)S(1)}, bf16[320,288]{0,1:T(8,128)(2,1)S(1)}, u32[]{:S(2)}, u32[]{:S(2)}) %collective-permute-start.32) | collective-permute-done | bytes 184352 | tf_op jit(solution)/shard_map/ppermute | solution.py:50
  62.4 3.6 collective-permute-start.12
  66.7 1.3 collective-permute-start.33
  68.6 5.5 %collective-permute-start = (bf16[2,320,640]{2,1,0:T(8,128)(2,1)}, bf16[2,320,640]{2,1,0:T(8,128)(2,1)}, u32[]{:S(2)}, u32[]{:S(2)}) collective-permute-start(bf16[2,320,640]{2,1,0:T(8,128)(2,1)} %slice_select_fusion.1), channel_id=1, source_target_pairs={{0,4},{4,8},{8,12},{1,5},{5,9},{9,13},{2,6},{6,10},{10,14},{3,7},{... | collective-permute-start | bytes 2457608 | tf_op jit(solution)/shard_map/ppermute | solution.py:48
  79.6 1.5 collective-permute-start.19
  81.7 35.2 %collective-permute-done.11 = bf16[320,384]{1,0:T(8,128)(2,1)S(1)} collective-permute-done((bf16[320,384]{1,0:T(8,128)(2,1)S(1)}, bf16[320,384]{1,0:T(8,128)(2,1)S(1)}, u32[]{:S(2)}, u32[]{:S(2)}) %collective-permute-start.11) | collective-permute-done | bytes 245792 | tf_op jit(solution)/shard_map/ppermute | solution.py:50
  120.1 2.6 concatenate.45
  122.8 1.7 collective-permute-start.1
  125.8 1.7 constant_dynamic-update-slice_fusion.13
  133.9 15.8 %collective-permute-done.15 = bf16[3,384,512]{2,1,0:T(8,128)(2,1)} collective-permute-done((bf16[3,384,512]{2,1,0:T(8,128)(2,1)}, bf16[3,384,512]{2,1,0:T(8,128)(2,1)}, u32[]{:S(2)}, u32[]{:S(2)}) %collective-permute-start.15) | collective-permute-done | bytes 1179680 | tf_op jit(solution)/shard_map/ppermute | solution.py:50
  150.4 27.7 %collective-permute-done.22 = bf16[2,288,564]{2,1,0:T(8,128)(2,1)S(1)} collective-permute-done((bf16[2,288,564]{2,1,0:T(8,128)(2,1)}, bf16[2,288,564]{2,1,0:T(8,128)(2,1)S(1)}, u32[]{:S(2)}, u32[]{:S(2)}) %collective-permute-start.22) | collective-permute-done | bytes 649760 | tf_op jit(solution)/shard_map/ppermute | solution.py:50
  179.3 1.3 collective-permute-start.23
  180.6 1.6 collective-permute-start.2
  183.6 1.3 constant_dynamic-update-slice_fusion.26
  187.8 37.0 %collective-permute-done.23 = bf16[2,288,564]{2,1,0:T(8,128)(2,1)S(1)} collective-permute-done((bf16[2,288,564]{2,1,0:T(8,128)(2,1)S(1)}, bf16[2,288,564]{2,1,0:T(8,128)(2,1)S(1)}, u32[]{:S(2)}, u32[]{:S(2)}) %collective-permute-start.23) | collective-permute-done | bytes 649760 | tf_op jit(solution)/shard_map/ppermute | solution.py:50
  225.0 2.3 copy-done.45
  227.3 4.8 %convolution_convert_fusion.2 = bf16[256,1152]{1,0:T(8,128)(2,1)} fusion(bf16[2,2016,564]{2,1,0:T(8,128)(2,1)} %copy-done.45, s32[]{:T(128)S(6)} %add.264, s32[]{:T(128)S(6)} %select_n.174, bf16[256,1152]{1,0:T(8,128)(2,1)} %bitcast.186, pred[564]{0:T(1024)(128)(4,1)S(1)} %copy-done.55), kind=kOutput, calls=%fused_computation.6 | convolution fusion | flops 667060224 | bytes 4130868 | tf_op jit(solution)/shard_map/dot_general | solution.py:31
  232.1 2.3 fusion.128
  234.4 1.7 collective-permute-start.14
  236.1 1.5 collective-permute-start.17
  238.8 1.4 constant_dynamic-update-slice_fusion.5
  245.7 2.8 fusion.35
  248.5 1.6 convolution_convert_fusion.4
  250.1 1.3 constant_dynamic-update-slice_fusion.20
  251.5 1.5 constant_dynamic-update-slice_fusion.18
  253.9 1.3 constant_dynamic-update-slice_fusion.16
  255.3 1.3 constant_dynamic-update-slice_fusion.15
  256.6 5.3 %collective-permute-done.17 = bf16[3,384,512]{2,1,0:T(8,128)(2,1)} collective-permute-done((bf16[3,384,512]{2,1,0:T(8,128)(2,1)}, bf16[3,384,512]{2,1,0:T(8,128)(2,1)}, u32[]{:S(2)}, u32[]{:S(2)}) %collective-permute-start.17) | collective-permute-done | bytes 1179680 | tf_op jit(solution)/shard_map/ppermute | solution.py:50
  261.9 1.3 constant_dynamic-update-slice_fusion.14
  263.3 3.3 copy-done.20
  267.2 3.9 convolution_convert_fusion.3
  271.1 1.4 fusion.127
  274.0 1.5 collective-permute-start.25
  275.5 1.4 collective-permute-start.26
  276.9 30.7 %all-reduce.2.cloned.1.call-done = bf16[256,1280]{1,0:T(8,128)(2,1)} async-done(((bf16[256,1280]{1,0:T(8,128)(2,1)}), bf16[256,1280]{1,0:T(8,128)(2,1)}) %all-reduce.2.cloned.1.call-update) | async-done | bytes 655376 | tf_op jit(solution)/shard_map/psum | solution.py:171
  307.6 1.4 fusion.124
  309.1 1.4 fusion.32
  311.8 8.8 %collective-permute-done.27 = bf16[256,672]{1,0:T(8,128)(2,1)S(1)} collective-permute-done((bf16[256,672]{1,0:T(8,128)(2,1)S(1)}, bf16[256,672]{1,0:T(8,128)(2,1)S(1)}, u32[]{:S(2)}, u32[]{:S(2)}) %collective-permute-start.27) | collective-permute-done | bytes 344096 | tf_op jit(solution)/shard_map/ppermute | solution.py:89
  320.7 1.6 gather_fusion
  322.3 1.8 broadcast_select_fusion
  324.2 4.6 all-to-all-start
  330.3 8.5 %all-to-all-done = bf16[4,64,672]{2,1,0:T(8,128)(2,1)} async-done(((bf16[4,64,672]{2,1,0:T(8,128)(2,1)}), bf16[4,64,672]{2,1,0:T(8,128)(2,1)}, u32[]{:S(2)}, u32[]{:S(2)}) %all-to-all-start) | async-done | bytes 344096 | tf_op jit(solution)/shard_map/all_to_all | solution.py:163
  339.8 1.7 fusion.27
  343.5 1.8 fusion
  345.6 1.6 collective-permute-start.36
  347.2 4.1 collective-permute-done.34
  353.5 2.0 collective-permute-start.37
  355.5 1.9 collective-permute-start.38
  357.4 2.7 collective-permute-done.37
  360.1 5.4 %collective-permute-done.38 = bf16[64,1280]{1,0:T(8,128)(2,1)S(1)} collective-permute-done((bf16[64,1280]{1,0:T(8,128)(2,1)S(1)}, bf16[64,1280]{1,0:T(8,128)(2,1)S(1)}, u32[]{:S(2)}, u32[]{:S(2)}) %collective-permute-start.38) | collective-permute-done | bytes 163872 | tf_op jit(solution)/shard_map/ppermute | solution.py:82
  366.5 1.8 convolution_convert_fusion
  368.3 4.3 convolution_convert_fusion.1
  372.6 1.6 copy.18
  374.3 2.0 pad_maximum_fusion
  378.9 2.0 collective-permute-start.42
  380.9 1.8 collective-permute-start.43
  382.7 67.0 %reduce-scatter.2.cloned.1.call-done = bf16[2,320,640]{2,1,0:T(8,128)(2,1)} async-done(((bf16[2,1280,640]{2,1,0:T(8,128)(2,1)}), bf16[2,320,640]{2,1,0:T(8,128)(2,1)}) %reduce-scatter.2.cloned.1.call-update) | async-done | bytes 819216 | tf_op jit(solution)/shard_map/reduce_scatter | solution.py:196
  452.1 1.3 fusion.72
  454.8 7.8 %collective-permute-done.40 = bf16[2,160,640]{2,1,0:T(8,128)(2,1)S(1)} collective-permute-done((bf16[2,160,640]{2,1,0:T(8,128)(2,1)S(1)}, bf16[2,160,640]{2,1,0:T(8,128)(2,1)S(1)}, u32[]{:S(2)}, u32[]{:S(2)}) %collective-permute-start.40) | collective-permute-done | bytes 409632 | tf_op jit(solution)/shard_map/ppermute | solution.py:89
  (256 shorter events, 63.5 us)
Async XLA Ops:
  7.2 300.5 %all-reduce.2.cloned.1.call-start = ((), (), s32[]{:S(2)}) async-start(), calls=%async_computation.2 | async-start | bytes 1310720 | tf_op jit(solution)/shard_map/psum | solution.py:171
  7.2 28.5 %collective-permute-start.6 = (bf16[320,384]{1,0:T(8,128)(2,1)}, bf16[320,384]{1,0:T(8,128)(2,1)S(1)}, u32[]{:S(2)}, u32[]{:S(2)}) collective-permute-start(bf16[320,384]{1,0:T(8,128)(2,1)} %param.15), channel_id=1, source_target_pairs={{0,4},{4,8},{8,12},{1,5},{5,9},{9,13},{2,6},{6,10},{10,14},{3,7},{... | collective-permute-start | bytes 737288 | tf_op jit(solution)/shard_map/ppermute | solution.py:48
  12.2 24.2 %collective-permute-start.9 = (bf16[320,384]{1,0:T(8,128)(2,1)}, bf16[320,384]{1,0:T(8,128)(2,1)S(1)}, u32[]{:S(2)}, u32[]{:S(2)}) collective-permute-start(bf16[320,384]{1,0:T(8,128)(2,1)} %param.15), channel_id=1, source_target_pairs={{4,0},{8,4},{12,8},{5,1},{9,5},{13,9},{6,2},{10,6},{14,10},{7,3},{... | collective-permute-start | bytes 737288 | tf_op jit(solution)/shard_map/ppermute | solution.py:50
  13.5 20.2 %collective-permute-start.28 = (bf16[320,288]{0,1:T(8,128)(2,1)}, bf16[320,288]{0,1:T(8,128)(2,1)S(1)}, u32[]{:S(2)}, u32[]{:S(2)}) collective-permute-start(bf16[320,288]{0,1:T(8,128)(2,1)} %param.16), channel_id=1, source_target_pairs={{0,4},{4,8},{8,12},{1,5},{5,9},{9,13},{2,6},{6,10},{10,14},{3,7},{... | collective-permute-start | bytes 552968 | tf_op jit(solution)/shard_map/ppermute | solution.py:48
  18.0 17.0 %collective-permute-start.31 = (bf16[320,288]{0,1:T(8,128)(2,1)}, bf16[320,288]{0,1:T(8,128)(2,1)S(1)}, u32[]{:S(2)}, u32[]{:S(2)}) collective-permute-start(bf16[320,288]{0,1:T(8,128)(2,1)} %param.16), channel_id=1, source_target_pairs={{4,0},{8,4},{12,8},{5,1},{9,5},{13,9},{6,2},{10,6},{14,10},{7,3},{... | collective-permute-start | bytes 552968 | tf_op jit(solution)/shard_map/ppermute | solution.py:50
  20.8 55.1 %collective-permute-start.18 = (bf16[2,288,564]{2,1,0:T(8,128)(2,1)S(1)}, bf16[2,288,564]{2,1,0:T(8,128)(2,1)}, u32[]{:S(2)}, u32[]{:S(2)}) collective-permute-start(bf16[2,288,564]{2,1,0:T(8,128)(2,1)S(1)} %slice_select_fusion.2), channel_id=1, source_target_pairs={{0,4},{4,8},{8,12},{1,5},{5,9},{9,13},{2,6},{6,10},{10,14},{3,7},{... | collective-permute-start | bytes 1949192 | tf_op jit(solution)/shard_map/ppermute | solution.py:48
  33.7 43.2 %copy-start.39 = (bf16[320,288]{0,1:T(8,128)(2,1)}, bf16[320,288]{0,1:T(8,128)(2,1)S(1)}, u32[]{:S(2)}) copy-start(bf16[320,288]{0,1:T(8,128)(2,1)S(1)} %collective-permute-done.28) | copy-start | bytes 552964
  33.7 43.2 %collective-permute-start.21 = (bf16[2,288,564]{2,1,0:T(8,128)(2,1)S(1)}, bf16[2,288,564]{2,1,0:T(8,128)(2,1)}, u32[]{:S(2)}, u32[]{:S(2)}) collective-permute-start(bf16[2,288,564]{2,1,0:T(8,128)(2,1)S(1)} %slice_select_fusion.2), channel_id=1, source_target_pairs={{4,0},{8,4},{12,8},{5,1},{9,5},{13,9},{6,2},{10,6},{14,10},{7,3},{... | collective-permute-start | bytes 1949192 | tf_op jit(solution)/shard_map/ppermute | solution.py:50
  35.0 40.9 %copy-start.40 = (bf16[320,288]{0,1:T(8,128)(2,1)}, bf16[320,288]{0,1:T(8,128)(2,1)S(1)}, u32[]{:S(2)}) copy-start(bf16[320,288]{0,1:T(8,128)(2,1)S(1)} %collective-permute-done.31) | copy-start | bytes 552964
  35.0 2.7 collective-permute-start.29
  35.7 83.8 %copy-start.30 = (bf16[320,384]{1,0:T(8,128)(2,1)}, bf16[320,384]{1,0:T(8,128)(2,1)S(1)}, u32[]{:S(2)}) copy-start(bf16[320,384]{1,0:T(8,128)(2,1)S(1)} %collective-permute-done.6) | copy-start | bytes 737284
  35.7 30.3 %collective-permute-start.7 = (bf16[320,384]{1,0:T(8,128)(2,1)S(1)}, bf16[320,384]{1,0:T(8,128)(2,1)S(1)}, u32[]{:S(2)}, u32[]{:S(2)}) collective-permute-start(bf16[320,384]{1,0:T(8,128)(2,1)S(1)} %collective-permute-done.6), channel_id=1, source_target_pairs={{4,8},{8,12},{5,9},{9,13},{6,10},{10,14},{7,11},{11,15},{20,24},{2... | collective-permute-start | bytes 737288 | tf_op jit(solution)/shard_map/ppermute | solution.py:48
  36.4 83.1 %copy-start.28 = (bf16[320,384]{1,0:T(8,128)(2,1)}, bf16[320,384]{1,0:T(8,128)(2,1)S(1)}, u32[]{:S(2)}) copy-start(bf16[320,384]{1,0:T(8,128)(2,1)S(1)} %collective-permute-done.9) | copy-start | bytes 737284
  36.4 30.3 %collective-permute-start.10 = (bf16[320,384]{1,0:T(8,128)(2,1)S(1)}, bf16[320,384]{1,0:T(8,128)(2,1)S(1)}, u32[]{:S(2)}, u32[]{:S(2)}) collective-permute-start(bf16[320,384]{1,0:T(8,128)(2,1)S(1)} %collective-permute-done.9), channel_id=1, source_target_pairs={{4,0},{8,4},{5,1},{9,5},{6,2},{10,6},{7,3},{11,7},{20,16},{24,20},... | collective-permute-start | bytes 737288 | tf_op jit(solution)/shard_map/ppermute | solution.py:50
  37.7 39.2 %copy-start.48 = (f32[256]{0:T(256)}, f32[256]{0:T(256)S(1)}, u32[]{:S(2)}) copy-start(f32[256]{0:T(256)S(1)} %broadcast_multiply_fusion.3) | copy-start | bytes 3076
  37.7 38.1 %copy-start.41 = (bf16[320,288]{0,1:T(8,128)(2,1)}, bf16[320,288]{0,1:T(8,128)(2,1)S(1)}, u32[]{:S(2)}) copy-start(bf16[320,288]{0,1:T(8,128)(2,1)S(1)} %collective-permute-done.29) | copy-start | bytes 552964
  37.8 24.7 %collective-permute-start.32 = (bf16[320,288]{0,1:T(8,128)(2,1)S(1)}, bf16[320,288]{0,1:T(8,128)(2,1)S(1)}, u32[]{:S(2)}, u32[]{:S(2)}) collective-permute-start(bf16[320,288]{0,1:T(8,128)(2,1)S(1)} %collective-permute-done.31), channel_id=1, source_target_pairs={{4,0},{8,4},{5,1},{9,5},{6,2},{10,6},{7,3},{11,7},{20,16},{24,20},... | collective-permute-start | bytes 552968 | tf_op jit(solution)/shard_map/ppermute | solution.py:50
  62.4 13.5 %copy-start.42 = (bf16[320,288]{0,1:T(8,128)(2,1)}, bf16[320,288]{0,1:T(8,128)(2,1)S(1)}, u32[]{:S(2)}) copy-start(bf16[320,288]{0,1:T(8,128)(2,1)S(1)} %collective-permute-done.32) | copy-start | bytes 552964
  62.4 65.0 %collective-permute-start.12 = (bf16[3,384,512]{2,1,0:T(8,128)(2,1)}, bf16[3,384,512]{2,1,0:T(8,128)(2,1)}, u32[]{:S(2)}, u32[]{:S(2)}) collective-permute-start(bf16[3,384,512]{2,1,0:T(8,128)(2,1)} %slice_select_fusion), channel_id=1, source_target_pairs={{0,4},{4,8},{8,12},{1,5},{5,9},{9,13},{2,6},{6,10},{10,14},{3,7},{... | collective-permute-start | bytes 3538952 | tf_op jit(solution)/shard_map/ppermute | solution.py:48
  66.0 53.5 %copy-start.34 = (bf16[320,384]{1,0:T(8,128)(2,1)}, bf16[320,384]{1,0:T(8,128)(2,1)S(1)}, u32[]{:S(2)}) copy-start(bf16[320,384]{1,0:T(8,128)(2,1)S(1)} %collective-permute-done.7) | copy-start | bytes 737284
  66.0 2.5 collective-permute-start.30
  66.7 52.8 %copy-start.32 = (bf16[320,384]{1,0:T(8,128)(2,1)}, bf16[320,384]{1,0:T(8,128)(2,1)S(1)}, u32[]{:S(2)}) copy-start(bf16[320,384]{1,0:T(8,128)(2,1)S(1)} %collective-permute-done.10) | copy-start | bytes 737284
  66.7 7.8 %collective-permute-start.33 = (bf16[320,288]{0,1:T(8,128)(2,1)S(1)}, bf16[320,288]{0,1:T(8,128)(2,1)S(1)}, u32[]{:S(2)}, u32[]{:S(2)}) collective-permute-start(bf16[320,288]{0,1:T(8,128)(2,1)S(1)} %collective-permute-done.32), channel_id=1, source_target_pairs={{4,0},{5,1},{6,2},{7,3},{20,16},{21,17},{22,18},{23,19}} | collective-permute-start | bytes 552968 | tf_op jit(solution)/shard_map/ppermute | solution.py:50
  68.6 54.2 %collective-permute-start = (bf16[2,320,640]{2,1,0:T(8,128)(2,1)}, bf16[2,320,640]{2,1,0:T(8,128)(2,1)}, u32[]{:S(2)}, u32[]{:S(2)}) collective-permute-start(bf16[2,320,640]{2,1,0:T(8,128)(2,1)} %slice_select_fusion.1), channel_id=1, source_target_pairs={{0,4},{4,8},{8,12},{1,5},{5,9},{9,13},{2,6},{6,10},{10,14},{3,7},{... | collective-permute-start | bytes 2457608 | tf_op jit(solution)/shard_map/ppermute | solution.py:48
  74.6 49.9 %collective-permute-start.3 = (bf16[2,320,640]{2,1,0:T(8,128)(2,1)}, bf16[2,320,640]{2,1,0:T(8,128)(2,1)}, u32[]{:S(2)}, u32[]{:S(2)}) collective-permute-start(bf16[2,320,640]{2,1,0:T(8,128)(2,1)} %slice_select_fusion.1), channel_id=1, source_target_pairs={{4,0},{8,4},{12,8},{5,1},{9,5},{13,9},{6,2},{10,6},{14,10},{7,3},{... | collective-permute-start | bytes 2457608 | tf_op jit(solution)/shard_map/ppermute | solution.py:50
  75.9 3.7 collective-permute-start.8
  76.9 40.0 %collective-permute-start.11 = (bf16[320,384]{1,0:T(8,128)(2,1)S(1)}, bf16[320,384]{1,0:T(8,128)(2,1)S(1)}, u32[]{:S(2)}, u32[]{:S(2)}) collective-permute-start(bf16[320,384]{1,0:T(8,128)(2,1)S(1)} %collective-permute-done.10), channel_id=1, source_target_pairs={{4,0},{5,1},{6,2},{7,3},{20,16},{21,17},{22,18},{23,19}} | collective-permute-start | bytes 737288 | tf_op jit(solution)/shard_map/ppermute | solution.py:50
  79.6 39.9 %copy-start.38 = (bf16[320,384]{1,0:T(8,128)(2,1)}, bf16[320,384]{1,0:T(8,128)(2,1)S(1)}, u32[]{:S(2)}) copy-start(bf16[320,384]{1,0:T(8,128)(2,1)S(1)} %collective-permute-done.8) | copy-start | bytes 737284
  79.6 49.1 %collective-permute-start.19 = (bf16[2,288,564]{2,1,0:T(8,128)(2,1)}, bf16[2,288,564]{2,1,0:T(8,128)(2,1)}, u32[]{:S(2)}, u32[]{:S(2)}) collective-permute-start(bf16[2,288,564]{2,1,0:T(8,128)(2,1)} %collective-permute-done.18), channel_id=1, source_target_pairs={{4,8},{8,12},{5,9},{9,13},{6,10},{10,14},{7,11},{11,15},{20,24},{2... | collective-permute-start | bytes 1949192 | tf_op jit(solution)/shard_map/ppermute | solution.py:48
  117.0 32.7 %collective-permute-start.15 = (bf16[3,384,512]{2,1,0:T(8,128)(2,1)}, bf16[3,384,512]{2,1,0:T(8,128)(2,1)}, u32[]{:S(2)}, u32[]{:S(2)}) collective-permute-start(bf16[3,384,512]{2,1,0:T(8,128)(2,1)} %slice_select_fusion), channel_id=1, source_target_pairs={{4,0},{8,4},{12,8},{5,1},{9,5},{13,9},{6,2},{10,6},{14,10},{7,3},{... | collective-permute-start | bytes 3538952 | tf_op jit(solution)/shard_map/ppermute | solution.py:50
  120.1 10.1 %copy-start.31 = (bf16[320,384]{1,0:T(8,128)(2,1)S(1)}, bf16[320,384]{1,0:T(8,128)(2,1)}, u32[]{:S(2)}) copy-start(bf16[320,384]{1,0:T(8,128)(2,1)} %copy-done.30) | copy-start | bytes 737284
  120.1 10.8 %copy-start.27 = (bf16[320,384]{1,0:T(8,128)(2,1)S(1)}, bf16[320,384]{1,0:T(8,128)(2,1)}, u32[]{:S(2)}) copy-start(bf16[320,384]{1,0:T(8,128)(2,1)} %param.15) | copy-start | bytes 737284
  122.8 10.3 %copy-start.37 = (bf16[320,384]{1,0:T(8,128)(2,1)S(1)}, bf16[320,384]{1,0:T(8,128)(2,1)}, u32[]{:S(2)}) copy-start(bf16[320,384]{1,0:T(8,128)(2,1)} %copy-done.36) | copy-start | bytes 737284
  122.8 56.5 %collective-permute-start.1 = (bf16[2,320,640]{2,1,0:T(8,128)(2,1)}, bf16[2,320,640]{2,1,0:T(8,128)(2,1)}, u32[]{:S(2)}, u32[]{:S(2)}) collective-permute-start(bf16[2,320,640]{2,1,0:T(8,128)(2,1)} %collective-permute-done), channel_id=1, source_target_pairs={{4,8},{8,12},{5,9},{9,13},{6,10},{10,14},{7,11},{11,15},{20,24},{2... | collective-permute-start | bytes 2457608 | tf_op jit(solution)/shard_map/ppermute | solution.py:48
  124.5 56.1 %collective-permute-start.4 = (bf16[2,320,640]{2,1,0:T(8,128)(2,1)}, bf16[2,320,640]{2,1,0:T(8,128)(2,1)}, u32[]{:S(2)}, u32[]{:S(2)}) collective-permute-start(bf16[2,320,640]{2,1,0:T(8,128)(2,1)} %collective-permute-done.3), channel_id=1, source_target_pairs={{4,0},{8,4},{5,1},{9,5},{6,2},{10,6},{7,3},{11,7},{20,16},{24,20},... | collective-permute-start | bytes 2457608 | tf_op jit(solution)/shard_map/ppermute | solution.py:50
  127.5 50.6 %collective-permute-start.22 = (bf16[2,288,564]{2,1,0:T(8,128)(2,1)}, bf16[2,288,564]{2,1,0:T(8,128)(2,1)S(1)}, u32[]{:S(2)}, u32[]{:S(2)}) collective-permute-start(bf16[2,288,564]{2,1,0:T(8,128)(2,1)} %collective-permute-done.21), channel_id=1, source_target_pairs={{4,0},{8,4},{5,1},{9,5},{6,2},{10,6},{7,3},{11,7},{20,16},{24,20},... | collective-permute-start | bytes 1949192 | tf_op jit(solution)/shard_map/ppermute | solution.py:50
  128.8 53.5 %collective-permute-start.20 = (bf16[2,288,564]{2,1,0:T(8,128)(2,1)}, bf16[2,288,564]{2,1,0:T(8,128)(2,1)S(1)}, u32[]{:S(2)}, u32[]{:S(2)}) collective-permute-start(bf16[2,288,564]{2,1,0:T(8,128)(2,1)} %collective-permute-done.19), channel_id=1, source_target_pairs={{8,12},{9,13},{10,14},{11,15},{24,28},{25,29},{26,30},{27,31}} | collective-permute-start | bytes 1949192 | tf_op jit(solution)/shard_map/ppermute | solution.py:48
  149.7 84.8 %collective-permute-start.13 = (bf16[3,384,512]{2,1,0:T(8,128)(2,1)}, bf16[3,384,512]{2,1,0:T(8,128)(2,1)S(1)}, u32[]{:S(2)}, u32[]{:S(2)}) collective-permute-start(bf16[3,384,512]{2,1,0:T(8,128)(2,1)} %collective-permute-done.12), channel_id=1, source_target_pairs={{4,8},{8,12},{5,9},{9,13},{6,10},{10,14},{7,11},{11,15},{20,24},{2... | collective-permute-start | bytes 3538952 | tf_op jit(solution)/shard_map/ppermute | solution.py:48
  178.0 58.1 %collective-permute-start.16 = (bf16[3,384,512]{2,1,0:T(8,128)(2,1)}, bf16[3,384,512]{2,1,0:T(8,128)(2,1)}, u32[]{:S(2)}, u32[]{:S(2)}) collective-permute-start(bf16[3,384,512]{2,1,0:T(8,128)(2,1)} %collective-permute-done.15), channel_id=1, source_target_pairs={{4,0},{8,4},{5,1},{9,5},{6,2},{10,6},{7,3},{11,7},{20,16},{24,20},... | collective-permute-start | bytes 3538952 | tf_op jit(solution)/shard_map/ppermute | solution.py:50
  179.3 45.5 %collective-permute-start.23 = (bf16[2,288,564]{2,1,0:T(8,128)(2,1)S(1)}, bf16[2,288,564]{2,1,0:T(8,128)(2,1)S(1)}, u32[]{:S(2)}, u32[]{:S(2)}) collective-permute-start(bf16[2,288,564]{2,1,0:T(8,128)(2,1)S(1)} %collective-permute-done.22), channel_id=1, source_target_pairs={{4,0},{5,1},{6,2},{7,3},{20,16},{21,17},{22,18},{23,19}} | collective-permute-start | bytes 1949192 | tf_op jit(solution)/shard_map/ppermute | solution.py:50
  180.6 56.9 %collective-permute-start.2 = (bf16[2,320,640]{2,1,0:T(8,128)(2,1)}, bf16[2,320,640]{2,1,0:T(8,128)(2,1)}, u32[]{:S(2)}, u32[]{:S(2)}) collective-permute-start(bf16[2,320,640]{2,1,0:T(8,128)(2,1)} %collective-permute-done.1), channel_id=1, source_target_pairs={{8,12},{9,13},{10,14},{11,15},{24,28},{25,29},{26,30},{27,31}} | collective-permute-start | bytes 2457608 | tf_op jit(solution)/shard_map/ppermute | solution.py:48
  182.3 62.1 %collective-permute-start.5 = (bf16[2,320,640]{2,1,0:T(8,128)(2,1)}, bf16[2,320,640]{2,1,0:T(8,128)(2,1)}, u32[]{:S(2)}, u32[]{:S(2)}) collective-permute-start(bf16[2,320,640]{2,1,0:T(8,128)(2,1)} %collective-permute-done.4), channel_id=1, source_target_pairs={{4,0},{5,1},{6,2},{7,3},{20,16},{21,17},{22,18},{23,19}} | collective-permute-start | bytes 2457608 | tf_op jit(solution)/shard_map/ppermute | solution.py:50
  187.7 39.6 %copy-start.55 = (pred[564]{0:T(1024)(128)(4,1)S(1)}, pred[564]{0:T(1024)(128)(4,1)}, u32[]{:S(2)}) copy-start(pred[564]{0:T(1024)(128)(4,1)} %fusion.109) | copy-start | bytes 1696
  234.4 15.7 %collective-permute-start.14 = (bf16[3,384,512]{2,1,0:T(8,128)(2,1)S(1)}, bf16[3,384,512]{2,1,0:T(8,128)(2,1)}, u32[]{:S(2)}, u32[]{:S(2)}) collective-permute-start(bf16[3,384,512]{2,1,0:T(8,128)(2,1)S(1)} %collective-permute-done.13), channel_id=1, source_target_pairs={{8,12},{9,13},{10,14},{11,15},{24,28},{25,29},{26,30},{27,31}} | collective-permute-start | bytes 3538952 | tf_op jit(solution)/shard_map/ppermute | solution.py:48
  236.1 25.8 %collective-permute-start.17 = (bf16[3,384,512]{2,1,0:T(8,128)(2,1)}, bf16[3,384,512]{2,1,0:T(8,128)(2,1)}, u32[]{:S(2)}, u32[]{:S(2)}) collective-permute-start(bf16[3,384,512]{2,1,0:T(8,128)(2,1)} %collective-permute-done.16), channel_id=1, source_target_pairs={{4,0},{5,1},{6,2},{7,3},{20,16},{21,17},{22,18},{23,19}} | collective-permute-start | bytes 3538952 | tf_op jit(solution)/shard_map/ppermute | solution.py:50
  274.0 35.1 %collective-permute-start.24 = (bf16[256,672]{1,0:T(8,128)(2,1)}, bf16[256,672]{1,0:T(8,128)(2,1)}, u32[]{:S(2)}, u32[]{:S(2)}) collective-permute-start(bf16[256,672]{1,0:T(8,128)(2,1)} %get-tuple-element.6), channel_id=1, source_target_pairs={{0,1},{1,2},{2,3},{3,0},{4,5},{5,6},{6,7},{7,4},{8,9},{9,10},{10,1... | collective-permute-start | bytes 1032200 | tf_op jit(solution)/shard_map/ppermute | solution.py:72
  274.0 35.1 %collective-permute-start.25 = (bf16[256,672]{1,0:T(8,128)(2,1)}, bf16[256,672]{1,0:T(8,128)(2,1)}, u32[]{:S(2)}, u32[]{:S(2)}) collective-permute-start(bf16[256,672]{1,0:T(8,128)(2,1)} %get-tuple-element.8), channel_id=1, source_target_pairs={{0,2},{1,3},{2,0},{3,1},{4,6},{5,7},{6,4},{7,5},{8,10},{9,11},{10,... | collective-permute-start | bytes 1032200 | tf_op jit(solution)/shard_map/ppermute | solution.py:72
  275.5 33.6 %collective-permute-start.26 = (bf16[256,672]{1,0:T(8,128)(2,1)}, bf16[256,672]{1,0:T(8,128)(2,1)}, u32[]{:S(2)}, u32[]{:S(2)}) collective-permute-start(bf16[256,672]{1,0:T(8,128)(2,1)} %get-tuple-element.7), channel_id=1, source_target_pairs={{0,3},{1,0},{2,1},{3,2},{4,7},{5,4},{6,5},{7,6},{8,11},{9,8},{10,9... | collective-permute-start | bytes 1032200 | tf_op jit(solution)/shard_map/ppermute | solution.py:72
  310.5 10.1 %copy-start.25 = (bf16[4,64,288]{2,1,0:T(8,128)(2,1)S(1)}, bf16[4,64,288]{2,1,0:T(8,128)(2,1)}, u32[]{:S(2)}) copy-start(bf16[4,64,288]{2,1,0:T(8,128)(2,1)} %constant_dynamic-slice_fusion.1) | copy-start | bytes 442372
  310.6 10.0 %collective-permute-start.27 = (bf16[256,672]{1,0:T(8,128)(2,1)S(1)}, bf16[256,672]{1,0:T(8,128)(2,1)S(1)}, u32[]{:S(2)}, u32[]{:S(2)}) collective-permute-start(bf16[256,672]{1,0:T(8,128)(2,1)S(1)} %fusion.32), channel_id=1, source_target_pairs={{0,16},{16,0},{1,17},{17,1},{2,18},{18,2},{3,19},{19,3},{4,20},{20... | collective-permute-start | bytes 1032200 | tf_op jit(solution)/shard_map/ppermute | solution.py:89
  311.7 10.6 %copy-start.53 = (pred[4]{0:T(512)(128)(4,1)S(1)}, pred[4]{0:T(512)(128)(4,1)}, u32[]{:S(2)}) copy-start(pred[4]{0:T(512)(128)(4,1)} %compare_and_fusion) | copy-start | bytes 16
  324.2 14.6 %all-to-all-start = ((bf16[4,64,672]{2,1,0:T(8,128)(2,1)}), bf16[4,64,672]{2,1,0:T(8,128)(2,1)}, u32[]{:S(2)}, u32[]{:S(2)}) async-start(bf16[4,64,672]{2,1,0:T(8,128)(2,1)} %broadcast_select_fusion), calls=%async_computation | async-start | bytes 786432 | tf_op jit(solution)/shard_map/all_to_all | solution.py:163
  328.8 121.0 %reduce-scatter.2.cloned.1.call-start = ((), (), s32[]{:S(2)}) async-start(), calls=%async_computation.3 | async-start | bytes 4096000 | tf_op jit(solution)/shard_map/reduce_scatter | solution.py:196
  345.4 5.9 %collective-permute-start.34 = (bf16[64,1280]{1,0:T(8,128)(2,1)S(1)}, bf16[64,1280]{1,0:T(8,128)(2,1)S(1)}, u32[]{:S(2)}, u32[]{:S(2)}) collective-permute-start(bf16[64,1280]{1,0:T(8,128)(2,1)S(1)} %get-tuple-element.20), channel_id=1, source_target_pairs={{0,1},{1,2},{2,3},{3,0},{4,5},{5,6},{6,7},{7,4},{8,9},{9,10},{10,1... | collective-permute-start | bytes 491528 | tf_op jit(solution)/shard_map/ppermute | solution.py:72
  345.4 7.1 %collective-permute-start.35 = (bf16[64,1280]{1,0:T(8,128)(2,1)S(1)}, bf16[64,1280]{1,0:T(8,128)(2,1)S(1)}, u32[]{:S(2)}, u32[]{:S(2)}) collective-permute-start(bf16[64,1280]{1,0:T(8,128)(2,1)S(1)} %get-tuple-element.22), channel_id=1, source_target_pairs={{0,2},{1,3},{2,0},{3,1},{4,6},{5,7},{6,4},{7,5},{8,10},{9,11},{10,... | collective-permute-start | bytes 491528 | tf_op jit(solution)/shard_map/ppermute | solution.py:72
  345.6 7.5 %collective-permute-start.36 = (bf16[64,1280]{1,0:T(8,128)(2,1)S(1)}, bf16[64,1280]{1,0:T(8,128)(2,1)S(1)}, u32[]{:S(2)}, u32[]{:S(2)}) collective-permute-start(bf16[64,1280]{1,0:T(8,128)(2,1)S(1)} %get-tuple-element.21), channel_id=1, source_target_pairs={{0,3},{1,0},{2,1},{3,2},{4,7},{5,4},{6,5},{7,6},{8,11},{9,8},{10,9... | collective-permute-start | bytes 491528 | tf_op jit(solution)/shard_map/ppermute | solution.py:72
  353.5 6.5 %collective-permute-start.37 = (bf16[64,1280]{1,0:T(8,128)(2,1)S(1)}, bf16[64,1280]{1,0:T(8,128)(2,1)S(1)}, u32[]{:S(2)}, u32[]{:S(2)}) collective-permute-start(bf16[64,1280]{1,0:T(8,128)(2,1)S(1)} %multiply_convert_fusion.2), channel_id=1, source_target_pairs={{0,3},{1,0},{2,1},{3,2},{4,7},{5,4},{6,5},{7,6},{8,11},{9,8},{10,9... | collective-permute-start | bytes 491528 | tf_op jit(solution)/shard_map/ppermute | solution.py:82
  355.5 10.0 %collective-permute-start.38 = (bf16[64,1280]{1,0:T(8,128)(2,1)S(1)}, bf16[64,1280]{1,0:T(8,128)(2,1)S(1)}, u32[]{:S(2)}, u32[]{:S(2)}) collective-permute-start(bf16[64,1280]{1,0:T(8,128)(2,1)S(1)} %multiply_convert_fusion.2), channel_id=1, source_target_pairs={{0,2},{1,3},{2,0},{3,1},{4,6},{5,7},{6,4},{7,5},{8,10},{9,11},{10,... | collective-permute-start | bytes 491528 | tf_op jit(solution)/shard_map/ppermute | solution.py:82
  357.4 8.1 %collective-permute-start.39 = (bf16[64,1280]{1,0:T(8,128)(2,1)S(1)}, bf16[64,1280]{1,0:T(8,128)(2,1)S(1)}, u32[]{:S(2)}, u32[]{:S(2)}) collective-permute-start(bf16[64,1280]{1,0:T(8,128)(2,1)S(1)} %multiply_convert_fusion.2), channel_id=1, source_target_pairs={{0,1},{1,2},{2,3},{3,0},{4,5},{5,6},{6,7},{7,4},{8,9},{9,10},{10,1... | collective-permute-start | bytes 491528 | tf_op jit(solution)/shard_map/ppermute | solution.py:82
  378.9 73.2 %collective-permute-start.41 = (bf16[160,672]{1,0:T(8,128)(2,1)S(1)}, bf16[160,672]{1,0:T(8,128)(2,1)}, u32[]{:S(2)}, u32[]{:S(2)}) collective-permute-start(bf16[160,672]{1,0:T(8,128)(2,1)S(1)} %get-tuple-element.13), channel_id=1, source_target_pairs={{0,4},{4,8},{8,12},{12,0},{1,5},{5,9},{9,13},{13,1},{2,6},{6,10},{... | collective-permute-start | bytes 645128 | tf_op jit(solution)/shard_map/ppermute | solution.py:72
  378.9 73.1 %collective-permute-start.42 = (bf16[160,672]{1,0:T(8,128)(2,1)S(1)}, bf16[160,672]{1,0:T(8,128)(2,1)}, u32[]{:S(2)}, u32[]{:S(2)}) collective-permute-start(bf16[160,672]{1,0:T(8,128)(2,1)S(1)} %get-tuple-element.15), channel_id=1, source_target_pairs={{0,8},{4,12},{8,0},{12,4},{1,9},{5,13},{9,1},{13,5},{2,10},{6,14},... | collective-permute-start | bytes 645128 | tf_op jit(solution)/shard_map/ppermute | solution.py:72
  380.9 71.1 %collective-permute-start.43 = (bf16[160,672]{1,0:T(8,128)(2,1)S(1)}, bf16[160,672]{1,0:T(8,128)(2,1)}, u32[]{:S(2)}, u32[]{:S(2)}) collective-permute-start(bf16[160,672]{1,0:T(8,128)(2,1)S(1)} %get-tuple-element.14), channel_id=1, source_target_pairs={{0,12},{4,0},{8,4},{12,8},{1,13},{5,1},{9,5},{13,9},{2,14},{6,2},{... | collective-permute-start | bytes 645128 | tf_op jit(solution)/shard_map/ppermute | solution.py:72
  449.8 12.8 %copy-start.11 = (bf16[2,320,640]{2,1,0:T(8,128)(2,1)S(1)}, bf16[2,320,640]{2,1,0:T(8,128)(2,1)}, u32[]{:S(2)}) copy-start(bf16[2,320,640]{2,1,0:T(8,128)(2,1)} %reduce-scatter.2.cloned.1.call-done) | copy-start | bytes 2457604
  451.0 11.5 %collective-permute-start.40 = (bf16[2,160,640]{2,1,0:T(8,128)(2,1)S(1)}, bf16[2,160,640]{2,1,0:T(8,128)(2,1)S(1)}, u32[]{:S(2)}, u32[]{:S(2)}) collective-permute-start(bf16[2,160,640]{2,1,0:T(8,128)(2,1)S(1)} %fusion.73), channel_id=1, source_target_pairs={{0,16},{16,0},{1,17},{17,1},{2,18},{18,2},{3,19},{19,3},{4,20},{20... | collective-permute-start | bytes 1228808 | tf_op jit(solution)/shard_map/ppermute | solution.py:89
  (40 other events, 160.8 us)
Sparse Core Ops, SparseCore 0:
  250.2 57.4 all-reduce.1
  376.5 73.2 reduce-scatter.1

commit v3 on v2

--- a/solution.py
+++ b/solution.py
@@ -39,12 +39,14 @@
     )
 
 
-def gathered_rows(block, axis):
+def gathered_rows(block, axis, held=()):
     count = lax.axis_size("dp")
     if count > 8:
-        return lax.all_gather(block, "dp", axis=axis, tiled=True)
+        return (lax.all_gather(block, "dp", axis=axis, tiled=True), *held)
     up, down = [block], [block]
     for step in range(1, count):
+        if held and step == count - 1:
+            up[-1], down[-1], *held = lax.optimization_barrier((up[-1], down[-1], *held))
         up.append(lax.ppermute(up[-1], "dp", [(i, i + 1) for i in range(step - 1, count - 1)]))
         down.append(
             lax.ppermute(down[-1], "dp", [(i, i - 1) for i in range(1, count - step + 1)])
@@ -52,7 +54,7 @@
     line = jnp.concatenate(up[:0:-1] + down, axis=axis)
     length = block.shape[axis]
     start = (count - 1 - lax.axis_index("dp")) * length
-    return lax.dynamic_slice_in_dim(line, start, count * length, axis)
+    return (lax.dynamic_slice_in_dim(line, start, count * length, axis), *held)
 
 
 def own_units(weights, group, low):
@@ -118,11 +120,14 @@
 
     low_d = dino_mlp.shape[2] // 2 // 128 * 128
     low_s = siglip_mlp.shape[2] // 2 // 128 * 128
-    dino_full = gathered_rows(own_units(dino_mlp, group, low_d), 1)
-    siglip_full = gathered_rows(own_units(siglip_mlp, group, low_s), 1)
-    w_mlp = gathered_rows(own_units(student_mlp, group, units), 1)
-    w_dino = gathered_rows(dino_head, 0)
-    w_sig = gathered_rows(siglip_head, 0)
+    own_dino = own_units(dino_mlp, group, low_d)
+    own_siglip = own_units(siglip_mlp, group, low_s)
+    own_student = own_units(student_mlp, group, units)
+    w_mlp, own_dino, own_siglip = gathered_rows(own_student, 1, (own_dino, own_siglip))
+    siglip_full, = gathered_rows(own_siglip, 1)
+    dino_full, own_hd, own_hs = gathered_rows(own_dino, 1, (dino_head, siglip_head))
+    w_dino, = gathered_rows(own_hd, 0)
+    w_sig, = gathered_rows(own_hs, 0)
 
     def once(hidden, low):
         place = lax.broadcasted_iota(jnp.int32, hidden.shape, 1)
@@ -193,6 +198,7 @@
         return grad.reshape(2, count_dp, block, units).transpose(1, 0, 2, 3).reshape(width, units)
 
     grad_mlp = jnp.stack([ordered(grad_up), ordered(grad_down)])
+    grad_mlp, sum_heads = lax.optimization_barrier((grad_mlp, sum_heads))
     sum_mlp = lax.psum_scatter(grad_mlp, "dp", scatter_dimension=1, tiled=True)
     sum_mlp = sum_mlp.reshape(2, 2, block, units)
     away = across(jnp.where(group == 0, sum_mlp[:, 1], sum_mlp[:, 0]).astype(bf16)).astype(f32)

time: 476 us -> 470 us (0.987)
  starting transfers between devices: 73.4 us -> 81.8 us
  other arithmetic: 26.4 us -> 20.1 us
    ppermute x15, waiting for transfers between devices: 145 us -> 117 us  [gathered_rows(): lax.ppermute(down[-1], 'dp', [(i, i - 1) for i in range(1, count - step +...]
    psum x1, waiting for transfers between devices: 30.7 us -> 50.6 us  [body(): mixed = flat + lax.psum(partial_out.astype(bf16), ('grp', 'tp')).astype(f32)]
    ppermute x9, waiting for transfers between devices: 5.88 us -> 23.6 us  [summed_piece(): total = total + lax.ppermute(piece, axis, pairs).astype(jnp.float32)]
    ppermute x15, waiting for transfers between devices: 0.04 us -> 9.97 us  [gathered_rows(): lax.ppermute(up[-1], 'dp', [(i, i + 1) for i in range(step - 1, count - 1)])]
    ppermute x2, waiting for transfers between devices: 16.5 us -> 8.15 us  [across(): return lax.ppermute(array, 'grp', [(0, 1), (1, 0)])]
    ppermute x3, waiting for transfers between devices: 8.04 us -> 0.01 us  [joined_pieces(): lax.ppermute(piece, axis, [(i, (i + step) % count) for i in range(count)])]
    ppermute x15, starting transfers between devices: 34.9 us -> 41.1 us  [gathered_rows(): lax.ppermute(up[-1], 'dp', [(i, i + 1) for i in range(step - 1, count - 1)])]
    unnamed x141 -> x87, local copies, waits for them, and re-layouts: 30.3 us -> 33.2 us
  transfers between devices with their start and end apart: 47 -> 47, of which waited for: 17 -> 16; matrix products, arithmetic and copies ran while one was open for 15% -> 15% of each run, Pallas kernels for 0% -> 0%
where the time goes in v3:
time: 470 us; the launch traced here: 468 us
  waiting for transfers between devices  278 us (59%)
  starting transfers between devices  81.8 us (17%)
  local copies, waits for them, and re-layouts  49.5 us (11%)
  matrix products  23.6 us (5%)
  other arithmetic  20.1 us (4%)
  between operations  15 us (3%)
    ppermute x15, waiting for transfers between devices, gathered_rows(): lax.ppermute(down[-1], 'dp', [(i, i - 1) for i in range(1, count - step +...  117 us
    reduce_scatter x1, waiting for transfers between devices, body(): sum_mlp = lax.psum_scatter(grad_mlp, 'dp', scatter_dimension=1, tiled=True)  63.8 us
    psum x1, waiting for transfers between devices, body(): mixed = flat + lax.psum(partial_out.astype(bf16), ('grp', 'tp')).astype(f32)  50.6 us
    ppermute x15, starting transfers between devices, gathered_rows(): lax.ppermute(up[-1], 'dp', [(i, i + 1) for i in range(step - 1, count - 1)])  41.1 us
    unnamed x87, local copies, waits for them, and re-layouts  33.2 us
    ppermute x9, waiting for transfers between devices, summed_piece(): total = total + lax.ppermute(piece, axis, pairs).astype(jnp.float32)  23.6 us
    ppermute x15, starting transfers between devices, gathered_rows(): lax.ppermute(down[-1], 'dp', [(i, i - 1) for i in range(1, count - step +...  19.4 us
    dot_general x5, matrix products, times_transposed(): lax.dot_general(left, right, (((1,), (1,)), ((), ())), preferred_element_...  10.8 us
  transfers between devices with their start and end apart: 47, of which 16 were waited for; matrix products, arithmetic and copies ran while one was open for 15% of the time, Pallas kernels for 0%

profile of v3, /device:TPU:0, one launch (start us, length us, event | category | flops | bytes accessed | tf_op | source)
XLA Modules:
  0.0 467.6 jit_solution(12144464816649857168)
XLA Ops:
  7.2 1.6 slice_select_fusion.1
  8.8 6.0 %collective-permute-start = (bf16[2,320,640]{2,1,0:T(8,128)(2,1)S(1)}, bf16[2,320,640]{2,1,0:T(8,128)(2,1)}, u32[]{:S(2)}, u32[]{:S(2)}) collective-permute-start(bf16[2,320,640]{2,1,0:T(8,128)(2,1)S(1)} %slice_select_fusion.1), channel_id=1, source_target_pairs={{0,4},{4,8},{8,12},{1,5},{5,9},{9,13},{2,6},{6,10},{10,14},{3,7},{... | collective-permute-start | bytes 2457608 | tf_op jit(solution)/shard_map/ppermute | solution.py:50
  19.2 2.3 slice_select_fusion.2
  21.5 9.9 %collective-permute-done = bf16[2,320,640]{2,1,0:T(8,128)(2,1)} collective-permute-done((bf16[2,320,640]{2,1,0:T(8,128)(2,1)S(1)}, bf16[2,320,640]{2,1,0:T(8,128)(2,1)}, u32[]{:S(2)}, u32[]{:S(2)}) %collective-permute-start) | collective-permute-done | bytes 819232 | tf_op jit(solution)/shard_map/ppermute | solution.py:50
  31.4 1.5 collective-permute-start.1
  32.9 3.6 collective-permute-done.2
  37.8 1.8 slice_select_fusion
  40.9 16.7 %collective-permute-done.3 = bf16[2,320,640]{2,1,0:T(8,128)(2,1)} collective-permute-done((bf16[2,320,640]{2,1,0:T(8,128)(2,1)}, bf16[2,320,640]{2,1,0:T(8,128)(2,1)}, u32[]{:S(2)}, u32[]{:S(2)}) %collective-permute-start.3) | collective-permute-done | bytes 819232 | tf_op jit(solution)/shard_map/ppermute | solution.py:52
  59.5 4.7 %collective-permute-start.6 = (bf16[3,384,512]{2,1,0:T(8,128)(2,1)S(1)}, bf16[3,384,512]{2,1,0:T(8,128)(2,1)}, u32[]{:S(2)}, u32[]{:S(2)}) collective-permute-start(bf16[3,384,512]{2,1,0:T(8,128)(2,1)S(1)} %slice_select_fusion), channel_id=1, source_target_pairs={{0,4},{4,8},{8,12},{1,5},{5,9},{9,13},{2,6},{6,10},{10,14},{3,7},{... | collective-permute-start | bytes 3538952 | tf_op jit(solution)/shard_map/ppermute | solution.py:50
  65.5 4.6 collective-permute-start.18
  72.8 1.4 constant_dynamic-update-slice_fusion.5
  78.3 46.5 %collective-permute-done.5 = bf16[2,320,640]{2,1,0:T(8,128)(2,1)S(1)} collective-permute-done((bf16[2,320,640]{2,1,0:T(8,128)(2,1)}, bf16[2,320,640]{2,1,0:T(8,128)(2,1)S(1)}, u32[]{:S(2)}, u32[]{:S(2)}) %collective-permute-start.5) | collective-permute-done | bytes 819232 | tf_op jit(solution)/shard_map/ppermute | solution.py:52
  124.9 2.8 fusion.35
  128.4 1.6 convolution_convert_fusion.4
  130.1 1.5 collective-permute-start.19
  132.9 50.6 %all-reduce.2.cloned.1.call-done = bf16[256,1280]{1,0:T(8,128)(2,1)} async-done(((bf16[256,1280]{1,0:T(8,128)(2,1)}), bf16[256,1280]{1,0:T(8,128)(2,1)}) %all-reduce.2.cloned.1.call-update) | async-done | bytes 655376 | tf_op jit(solution)/shard_map/psum | solution.py:176
  183.5 1.4 fusion.124
  184.9 1.7 collective-permute-start.7
  189.5 1.4 collective-permute-start.23
  191.0 28.9 %collective-permute-done.9 = bf16[3,384,512]{2,1,0:T(8,128)(2,1)} collective-permute-done((bf16[3,384,512]{2,1,0:T(8,128)(2,1)}, bf16[3,384,512]{2,1,0:T(8,128)(2,1)}, u32[]{:S(2)}, u32[]{:S(2)}) %collective-permute-start.9) | collective-permute-done | bytes 1179680 | tf_op jit(solution)/shard_map/ppermute | solution.py:52
  219.8 1.7 collective-permute-start.16
  225.4 8.0 %collective-permute-done.23 = bf16[2,288,564]{2,1,0:T(8,128)(2,1)S(1)} collective-permute-done((bf16[2,288,564]{2,1,0:T(8,128)(2,1)}, bf16[2,288,564]{2,1,0:T(8,128)(2,1)S(1)}, u32[]{:S(2)}, u32[]{:S(2)}) %collective-permute-start.23) | collective-permute-done | bytes 649760 | tf_op jit(solution)/shard_map/ppermute | solution.py:52
  235.9 4.0 convolution_convert_fusion.2
  239.9 5.3 %collective-permute-start.28 = (bf16[320,288]{0,1:T(8,128)(2,1)S(1)}, bf16[320,288]{0,1:T(8,128)(2,1)}, u32[]{:S(2)}, u32[]{:S(2)}) collective-permute-start(bf16[320,288]{0,1:T(8,128)(2,1)S(1)} %copy-done.25), channel_id=1, source_target_pairs={{0,4},{4,8},{8,12},{1,5},{5,9},{9,13},{2,6},{6,10},{10,14},{3,7},{... | collective-permute-start | bytes 552968 | tf_op jit(solution)/shard_map/ppermute | solution.py:50
  246.5 7.7 %collective-permute-start.10 = (bf16[320,384]{1,0:T(8,128)(2,1)}, bf16[320,384]{1,0:T(8,128)(2,1)}, u32[]{:S(2)}, u32[]{:S(2)}) collective-permute-start(bf16[320,384]{1,0:T(8,128)(2,1)} %param.15), channel_id=1, source_target_pairs={{0,4},{4,8},{8,12},{1,5},{5,9},{9,13},{2,6},{6,10},{10,14},{3,7},{... | collective-permute-start | bytes 737288 | tf_op jit(solution)/shard_map/ppermute | solution.py:50
  256.6 12.6 %collective-permute-done.31 = bf16[320,288]{0,1:T(8,128)(2,1)} collective-permute-done((bf16[320,288]{0,1:T(8,128)(2,1)S(1)}, bf16[320,288]{0,1:T(8,128)(2,1)}, u32[]{:S(2)}, u32[]{:S(2)}) %collective-permute-start.31) | collective-permute-done | bytes 184352 | tf_op jit(solution)/shard_map/ppermute | solution.py:52
  269.1 1.5 collective-permute-start.29
  271.9 1.4 collective-permute-start.11
  276.0 1.4 constant_dynamic-update-slice_fusion.18
  277.7 1.3 constant_dynamic-update-slice_fusion.16
  280.4 1.4 constant_dynamic-update-slice_fusion.14
  281.9 3.2 copy-done.16
  285.0 1.4 fusion.8
  286.4 4.1 convolution_convert_fusion.3
  290.6 1.4 fusion.127
  292.8 1.6 collective-permute-start.26
  296.6 6.8 %collective-permute-done.24 = bf16[256,672]{1,0:T(8,128)(2,1)S(1)} collective-permute-done((bf16[256,672]{1,0:T(8,128)(2,1)S(1)}, bf16[256,672]{1,0:T(8,128)(2,1)S(1)}, u32[]{:S(2)}, u32[]{:S(2)}) %collective-permute-start.24) | collective-permute-done | bytes 344096 | tf_op jit(solution)/shard_map/ppermute | solution.py:74
  304.7 1.4 collective-permute-start.12
  306.1 4.0 collective-permute-done.26
  314.5 2.6 concatenate.45
  317.2 1.7 constant_dynamic-update-slice_fusion.13
  318.9 1.7 constant_dynamic-update-slice_fusion.12
  322.2 6.7 %all-to-all-start = ((bf16[4,64,672]{2,1,0:T(8,128)(2,1)}), bf16[4,64,672]{2,1,0:T(8,128)(2,1)S(1)}, u32[]{:S(2)}, u32[]{:S(2)}) async-start(bf16[4,64,672]{2,1,0:T(8,128)(2,1)} %broadcast_select_fusion), calls=%async_computation | async-start | bytes 786432 | tf_op jit(solution)/shard_map/all_to_all | solution.py:168
  328.9 1.7 constant_dynamic-update-slice_fusion.11
  330.6 1.7 constant_dynamic-update-slice_fusion.10
  332.2 1.7 constant_dynamic-update-slice_fusion.9
  333.9 1.7 constant_dynamic-update-slice_fusion.8
  335.6 1.7 constant_dynamic-update-slice_fusion.7
  337.3 4.2 all-to-all-done
  341.5 1.7 fusion.27
  346.5 2.8 collective-permute-start.35
  349.3 1.4 collective-permute-start.36
  350.7 1.4 convolution_convert_fusion.5
  352.2 1.7 copy.20
  354.0 2.7 collective-permute-start.41
  359.2 1.4 collective-permute-start.37
  360.6 4.1 collective-permute-done.40
  364.8 8.7 %collective-permute-done.41 = bf16[160,672]{1,0:T(8,128)(2,1)S(1)} collective-permute-done((bf16[160,672]{1,0:T(8,128)(2,1)S(1)}, bf16[160,672]{1,0:T(8,128)(2,1)S(1)}, u32[]{:S(2)}, u32[]{:S(2)}) %collective-permute-start.41) | collective-permute-done | bytes 215072 | tf_op jit(solution)/shard_map/ppermute | solution.py:74
  375.3 4.1 convolution_convert_fusion.1
  379.4 1.6 copy.18
  381.1 2.0 pad_maximum_fusion
  383.2 63.8 %reduce-scatter.2.cloned.1.call-done = bf16[2,320,640]{2,1,0:T(8,128)(2,1)} async-done(((bf16[2,1280,640]{2,1,0:T(8,128)(2,1)}), bf16[2,320,640]{2,1,0:T(8,128)(2,1)}) %reduce-scatter.2.cloned.1.call-update) | async-done | bytes 819216 | tf_op jit(solution)/shard_map/reduce_scatter | solution.py:202
  448.2 1.6 collective-permute-start.43
  451.2 8.1 %collective-permute-done.43 = bf16[2,160,640]{2,1,0:T(8,128)(2,1)S(1)} collective-permute-done((bf16[2,160,640]{2,1,0:T(8,128)(2,1)S(1)}, bf16[2,160,640]{2,1,0:T(8,128)(2,1)S(1)}, u32[]{:S(2)}, u32[]{:S(2)}) %collective-permute-start.43) | collective-permute-done | bytes 409632 | tf_op jit(solution)/shard_map/ppermute | solution.py:91
  (200 shorter events, 59.5 us)
Async XLA Ops:
  7.2 8.9 %copy-start.1 = (bf16[4,64,1536]{2,1,0:T(8,128)(2,1)S(1)}, bf16[4,64,1536]{2,1,0:T(8,128)(2,1)}, u32[]{:S(2)}) copy-start(bf16[4,64,1536]{2,1,0:T(8,128)(2,1)} %param.9) | copy-start | bytes 2359300
  7.2 176.3 %all-reduce.2.cloned.1.call-start = ((), (), s32[]{:S(2)}) async-start(), calls=%async_computation.2 | async-start | bytes 1310720 | tf_op jit(solution)/shard_map/psum | solution.py:176
  7.2 9.4 %copy-start.2 = (bf16[4,64,1152]{2,1,0:T(8,128)(2,1)S(1)}, bf16[4,64,1152]{2,1,0:T(8,128)(2,1)}, u32[]{:S(2)}) copy-start(bf16[4,64,1152]{2,1,0:T(8,128)(2,1)} %param.10) | copy-start | bytes 1769476
  8.8 9.1 %copy-start.28 = (s32[4]{0:T(128)S(1)}, s32[4]{0:T(128)}, u32[]{:S(2)}) copy-start(s32[4]{0:T(128)} %param.17) | copy-start | bytes 52
  8.8 9.1 %copy-start = (bf16[1,256,1280]{2,1,0:T(8,128)(2,1)S(1)}, bf16[1,256,1280]{2,1,0:T(8,128)(2,1)}, u32[]{:S(2)}) copy-start(bf16[1,256,1280]{2,1,0:T(8,128)(2,1)} %param.11) | copy-start | bytes 1966084
  8.8 22.6 %collective-permute-start = (bf16[2,320,640]{2,1,0:T(8,128)(2,1)S(1)}, bf16[2,320,640]{2,1,0:T(8,128)(2,1)}, u32[]{:S(2)}, u32[]{:S(2)}) collective-permute-start(bf16[2,320,640]{2,1,0:T(8,128)(2,1)S(1)} %slice_select_fusion.1), channel_id=1, source_target_pairs={{0,4},{4,8},{8,12},{1,5},{5,9},{9,13},{2,6},{6,10},{10,14},{3,7},{... | collective-permute-start | bytes 2457608 | tf_op jit(solution)/shard_map/ppermute | solution.py:50
  14.8 21.7 %collective-permute-start.2 = (bf16[2,320,640]{2,1,0:T(8,128)(2,1)S(1)}, bf16[2,320,640]{2,1,0:T(8,128)(2,1)}, u32[]{:S(2)}, u32[]{:S(2)}) collective-permute-start(bf16[2,320,640]{2,1,0:T(8,128)(2,1)S(1)} %slice_select_fusion.1), channel_id=1, source_target_pairs={{4,0},{8,4},{12,8},{5,1},{9,5},{13,9},{6,2},{10,6},{14,10},{7,3},{... | collective-permute-start | bytes 2457608 | tf_op jit(solution)/shard_map/ppermute | solution.py:52
  31.4 9.5 %collective-permute-start.1 = (bf16[2,320,640]{2,1,0:T(8,128)(2,1)}, bf16[2,320,640]{2,1,0:T(8,128)(2,1)}, u32[]{:S(2)}, u32[]{:S(2)}) collective-permute-start(bf16[2,320,640]{2,1,0:T(8,128)(2,1)} %collective-permute-done), channel_id=1, source_target_pairs={{4,8},{8,12},{5,9},{9,13},{6,10},{10,14},{7,11},{11,15},{20,24},{2... | collective-permute-start | bytes 2457608 | tf_op jit(solution)/shard_map/ppermute | solution.py:50
  36.5 21.1 %collective-permute-start.3 = (bf16[2,320,640]{2,1,0:T(8,128)(2,1)}, bf16[2,320,640]{2,1,0:T(8,128)(2,1)}, u32[]{:S(2)}, u32[]{:S(2)}) collective-permute-start(bf16[2,320,640]{2,1,0:T(8,128)(2,1)} %collective-permute-done.2), channel_id=1, source_target_pairs={{4,0},{8,4},{5,1},{9,5},{6,2},{10,6},{7,3},{11,7},{20,16},{24,20},... | collective-permute-start | bytes 2457608 | tf_op jit(solution)/shard_map/ppermute | solution.py:52
  39.6 33.2 %copy-start.7 = (bf16[3,384,512]{2,1,0:T(8,128)(2,1)}, bf16[3,384,512]{2,1,0:T(8,128)(2,1)S(1)}, u32[]{:S(2)}) copy-start(bf16[3,384,512]{2,1,0:T(8,128)(2,1)S(1)} %slice_select_fusion) | copy-start | bytes 3538948
  57.7 13.7 %collective-permute-start.4 = (bf16[2,320,640]{2,1,0:T(8,128)(2,1)}, bf16[2,320,640]{2,1,0:T(8,128)(2,1)S(1)}, u32[]{:S(2)}, u32[]{:S(2)}) collective-permute-start(bf16[2,320,640]{2,1,0:T(8,128)(2,1)} %collective-permute-done.1), channel_id=1, source_target_pairs={{8,12},{9,13},{10,14},{11,15},{24,28},{25,29},{26,30},{27,31}} | collective-permute-start | bytes 2457608 | tf_op jit(solution)/shard_map/ppermute | solution.py:50
  59.5 125.4 %collective-permute-start.6 = (bf16[3,384,512]{2,1,0:T(8,128)(2,1)S(1)}, bf16[3,384,512]{2,1,0:T(8,128)(2,1)}, u32[]{:S(2)}, u32[]{:S(2)}) collective-permute-start(bf16[3,384,512]{2,1,0:T(8,128)(2,1)S(1)} %slice_select_fusion), channel_id=1, source_target_pairs={{0,4},{4,8},{8,12},{1,5},{5,9},{9,13},{2,6},{6,10},{10,14},{3,7},{... | collective-permute-start | bytes 3538952 | tf_op jit(solution)/shard_map/ppermute | solution.py:50
  64.2 122.4 %collective-permute-start.8 = (bf16[3,384,512]{2,1,0:T(8,128)(2,1)S(1)}, bf16[3,384,512]{2,1,0:T(8,128)(2,1)}, u32[]{:S(2)}, u32[]{:S(2)}) collective-permute-start(bf16[3,384,512]{2,1,0:T(8,128)(2,1)S(1)} %slice_select_fusion), channel_id=1, source_target_pairs={{4,0},{8,4},{12,8},{5,1},{9,5},{13,9},{6,2},{10,6},{14,10},{7,3},{... | collective-permute-start | bytes 3538952 | tf_op jit(solution)/shard_map/ppermute | solution.py:52
  65.5 64.6 %collective-permute-start.18 = (bf16[2,288,564]{2,1,0:T(8,128)(2,1)}, bf16[2,288,564]{2,1,0:T(8,128)(2,1)S(1)}, u32[]{:S(2)}, u32[]{:S(2)}) collective-permute-start(bf16[2,288,564]{2,1,0:T(8,128)(2,1)} %slice_select_fusion.2), channel_id=1, source_target_pairs={{0,4},{4,8},{8,12},{1,5},{5,9},{9,13},{2,6},{6,10},{10,14},{3,7},{... | collective-permute-start | bytes 1949192 | tf_op jit(solution)/shard_map/ppermute | solution.py:50
  70.1 61.5 %collective-permute-start.21 = (bf16[2,288,564]{2,1,0:T(8,128)(2,1)}, bf16[2,288,564]{2,1,0:T(8,128)(2,1)S(1)}, u32[]{:S(2)}, u32[]{:S(2)}) collective-permute-start(bf16[2,288,564]{2,1,0:T(8,128)(2,1)} %slice_select_fusion.2), channel_id=1, source_target_pairs={{4,0},{8,4},{12,8},{5,1},{9,5},{13,9},{6,2},{10,6},{14,10},{7,3},{... | collective-permute-start | bytes 1949192 | tf_op jit(solution)/shard_map/ppermute | solution.py:52
  71.4 53.4 %collective-permute-start.5 = (bf16[2,320,640]{2,1,0:T(8,128)(2,1)}, bf16[2,320,640]{2,1,0:T(8,128)(2,1)S(1)}, u32[]{:S(2)}, u32[]{:S(2)}) collective-permute-start(bf16[2,320,640]{2,1,0:T(8,128)(2,1)} %collective-permute-done.3), channel_id=1, source_target_pairs={{4,0},{5,1},{6,2},{7,3},{20,16},{21,17},{22,18},{23,19}} | collective-permute-start | bytes 2457608 | tf_op jit(solution)/shard_map/ppermute | solution.py:52
  130.1 59.0 %copy-start.23 = (bf16[2,288,564]{2,1,0:T(8,128)(2,1)}, bf16[2,288,564]{2,1,0:T(8,128)(2,1)S(1)}, u32[]{:S(2)}) copy-start(bf16[2,288,564]{2,1,0:T(8,128)(2,1)S(1)} %collective-permute-done.18) | copy-start | bytes 1949188
  130.1 58.2 %collective-permute-start.19 = (bf16[2,288,564]{2,1,0:T(8,128)(2,1)S(1)}, bf16[2,288,564]{2,1,0:T(8,128)(2,1)}, u32[]{:S(2)}, u32[]{:S(2)}) collective-permute-start(bf16[2,288,564]{2,1,0:T(8,128)(2,1)S(1)} %collective-permute-done.18), channel_id=1, source_target_pairs={{4,8},{8,12},{5,9},{9,13},{6,10},{10,14},{7,11},{11,15},{20,24},{2... | collective-permute-start | bytes 1949192 | tf_op jit(solution)/shard_map/ppermute | solution.py:50
  131.6 57.8 %collective-permute-start.22 = (bf16[2,288,564]{2,1,0:T(8,128)(2,1)S(1)}, bf16[2,288,564]{2,1,0:T(8,128)(2,1)}, u32[]{:S(2)}, u32[]{:S(2)}) collective-permute-start(bf16[2,288,564]{2,1,0:T(8,128)(2,1)S(1)} %collective-permute-done.21), channel_id=1, source_target_pairs={{4,0},{8,4},{5,1},{9,5},{6,2},{10,6},{7,3},{11,7},{20,16},{24,20},... | collective-permute-start | bytes 1949192 | tf_op jit(solution)/shard_map/ppermute | solution.py:52
  183.5 4.4 copy-start.4
  184.9 6.1 %collective-permute-start.7 = (bf16[3,384,512]{2,1,0:T(8,128)(2,1)}, bf16[3,384,512]{2,1,0:T(8,128)(2,1)}, u32[]{:S(2)}, u32[]{:S(2)}) collective-permute-start(bf16[3,384,512]{2,1,0:T(8,128)(2,1)} %collective-permute-done.6), channel_id=1, source_target_pairs={{4,8},{8,12},{5,9},{9,13},{6,10},{10,14},{7,11},{11,15},{20,24},{2... | collective-permute-start | bytes 3538952 | tf_op jit(solution)/shard_map/ppermute | solution.py:50
  186.6 33.2 %collective-permute-start.9 = (bf16[3,384,512]{2,1,0:T(8,128)(2,1)}, bf16[3,384,512]{2,1,0:T(8,128)(2,1)}, u32[]{:S(2)}, u32[]{:S(2)}) collective-permute-start(bf16[3,384,512]{2,1,0:T(8,128)(2,1)} %collective-permute-done.8), channel_id=1, source_target_pairs={{4,0},{8,4},{5,1},{9,5},{6,2},{10,6},{7,3},{11,7},{20,16},{24,20},... | collective-permute-start | bytes 3538952 | tf_op jit(solution)/shard_map/ppermute | solution.py:52
  188.3 2.6 collective-permute-start.20
  189.3 105.1 %copy-start.5 = (f32[256,1280]{1,0:T(8,128)}, f32[256,1280]{1,0:T(8,128)S(1)}, u32[]{:S(2)}) copy-start(f32[256,1280]{1,0:T(8,128)S(1)} %get-tuple-element.30) | copy-start | bytes 3932164
  189.3 33.4 %copy-start.24 = (bf16[2,288,564]{2,1,0:T(8,128)(2,1)S(1)}, bf16[2,288,564]{2,1,0:T(8,128)(2,1)}, u32[]{:S(2)}) copy-start(bf16[2,288,564]{2,1,0:T(8,128)(2,1)} %copy-done.23) | copy-start | bytes 1949188
  189.5 44.0 %collective-permute-start.23 = (bf16[2,288,564]{2,1,0:T(8,128)(2,1)}, bf16[2,288,564]{2,1,0:T(8,128)(2,1)S(1)}, u32[]{:S(2)}, u32[]{:S(2)}) collective-permute-start(bf16[2,288,564]{2,1,0:T(8,128)(2,1)} %collective-permute-done.22), channel_id=1, source_target_pairs={{4,0},{5,1},{6,2},{7,3},{20,16},{21,17},{22,18},{23,19}} | collective-permute-start | bytes 1949192 | tf_op jit(solution)/shard_map/ppermute | solution.py:52
  219.8 52.1 %collective-permute-start.16 = (bf16[3,384,512]{2,1,0:T(8,128)(2,1)}, bf16[3,384,512]{2,1,0:T(8,128)(2,1)}, u32[]{:S(2)}, u32[]{:S(2)}) collective-permute-start(bf16[3,384,512]{2,1,0:T(8,128)(2,1)} %collective-permute-done.7), channel_id=1, source_target_pairs={{8,12},{9,13},{10,14},{11,15},{24,28},{25,29},{26,30},{27,31}} | collective-permute-start | bytes 3538952 | tf_op jit(solution)/shard_map/ppermute | solution.py:50
  233.6 46.8 %collective-permute-start.17 = (bf16[3,384,512]{2,1,0:T(8,128)(2,1)}, bf16[3,384,512]{2,1,0:T(8,128)(2,1)}, u32[]{:S(2)}, u32[]{:S(2)}) collective-permute-start(bf16[3,384,512]{2,1,0:T(8,128)(2,1)} %collective-permute-done.9), channel_id=1, source_target_pairs={{4,0},{5,1},{6,2},{7,3},{20,16},{21,17},{22,18},{23,19}} | collective-permute-start | bytes 3538952 | tf_op jit(solution)/shard_map/ppermute | solution.py:52
  235.9 4.0 copy-start.25
  239.9 15.4 %collective-permute-start.28 = (bf16[320,288]{0,1:T(8,128)(2,1)S(1)}, bf16[320,288]{0,1:T(8,128)(2,1)}, u32[]{:S(2)}, u32[]{:S(2)}) collective-permute-start(bf16[320,288]{0,1:T(8,128)(2,1)S(1)} %copy-done.25), channel_id=1, source_target_pairs={{0,4},{4,8},{8,12},{1,5},{5,9},{9,13},{2,6},{6,10},{10,14},{3,7},{... | collective-permute-start | bytes 552968 | tf_op jit(solution)/shard_map/ppermute | solution.py:50
  245.3 23.9 %collective-permute-start.31 = (bf16[320,288]{0,1:T(8,128)(2,1)S(1)}, bf16[320,288]{0,1:T(8,128)(2,1)}, u32[]{:S(2)}, u32[]{:S(2)}) collective-permute-start(bf16[320,288]{0,1:T(8,128)(2,1)S(1)} %copy-done.25), channel_id=1, source_target_pairs={{4,0},{8,4},{12,8},{5,1},{9,5},{13,9},{6,2},{10,6},{14,10},{7,3},{... | collective-permute-start | bytes 552968 | tf_op jit(solution)/shard_map/ppermute | solution.py:52
  246.5 24.1 %collective-permute-start.10 = (bf16[320,384]{1,0:T(8,128)(2,1)}, bf16[320,384]{1,0:T(8,128)(2,1)}, u32[]{:S(2)}, u32[]{:S(2)}) collective-permute-start(bf16[320,384]{1,0:T(8,128)(2,1)} %param.15), channel_id=1, source_target_pairs={{0,4},{4,8},{8,12},{1,5},{5,9},{9,13},{2,6},{6,10},{10,14},{3,7},{... | collective-permute-start | bytes 737288 | tf_op jit(solution)/shard_map/ppermute | solution.py:50
  255.3 37.3 %collective-permute-start.13 = (bf16[320,384]{1,0:T(8,128)(2,1)}, bf16[320,384]{1,0:T(8,128)(2,1)}, u32[]{:S(2)}, u32[]{:S(2)}) collective-permute-start(bf16[320,384]{1,0:T(8,128)(2,1)} %param.15), channel_id=1, source_target_pairs={{4,0},{8,4},{12,8},{5,1},{9,5},{13,9},{6,2},{10,6},{14,10},{7,3},{... | collective-permute-start | bytes 737288 | tf_op jit(solution)/shard_map/ppermute | solution.py:52
  269.1 23.7 %collective-permute-start.29 = (bf16[320,288]{0,1:T(8,128)(2,1)}, bf16[320,288]{0,1:T(8,128)(2,1)}, u32[]{:S(2)}, u32[]{:S(2)}) collective-permute-start(bf16[320,288]{0,1:T(8,128)(2,1)} %collective-permute-done.28), channel_id=1, source_target_pairs={{4,8},{8,12},{5,9},{9,13},{6,10},{10,14},{7,11},{11,15},{20,24},{2... | collective-permute-start | bytes 552968 | tf_op jit(solution)/shard_map/ppermute | solution.py:50
  270.6 24.0 %collective-permute-start.32 = (bf16[320,288]{0,1:T(8,128)(2,1)}, bf16[320,288]{0,1:T(8,128)(2,1)}, u32[]{:S(2)}, u32[]{:S(2)}) collective-permute-start(bf16[320,288]{0,1:T(8,128)(2,1)} %collective-permute-done.31), channel_id=1, source_target_pairs={{4,0},{8,4},{5,1},{9,5},{6,2},{10,6},{7,3},{11,7},{20,16},{24,20},... | collective-permute-start | bytes 552968 | tf_op jit(solution)/shard_map/ppermute | solution.py:52
  271.9 24.0 %collective-permute-start.11 = (bf16[320,384]{1,0:T(8,128)(2,1)}, bf16[320,384]{1,0:T(8,128)(2,1)}, u32[]{:S(2)}, u32[]{:S(2)}) collective-permute-start(bf16[320,384]{1,0:T(8,128)(2,1)} %collective-permute-done.10), channel_id=1, source_target_pairs={{4,8},{8,12},{5,9},{9,13},{6,10},{10,14},{7,11},{11,15},{20,24},{2... | collective-permute-start | bytes 737288 | tf_op jit(solution)/shard_map/ppermute | solution.py:50
  280.4 4.6 copy-start.10
  281.9 3.2 copy-start.16
  292.6 10.8 %collective-permute-start.24 = (bf16[256,672]{1,0:T(8,128)(2,1)S(1)}, bf16[256,672]{1,0:T(8,128)(2,1)S(1)}, u32[]{:S(2)}, u32[]{:S(2)}) collective-permute-start(bf16[256,672]{1,0:T(8,128)(2,1)S(1)} %get-tuple-element.26), channel_id=1, source_target_pairs={{0,1},{1,2},{2,3},{3,0},{4,5},{5,6},{6,7},{7,4},{8,9},{9,10},{10,1... | collective-permute-start | bytes 1032200 | tf_op jit(solution)/shard_map/ppermute | solution.py:74
  292.6 12.1 %collective-permute-start.25 = (bf16[256,672]{1,0:T(8,128)(2,1)S(1)}, bf16[256,672]{1,0:T(8,128)(2,1)S(1)}, u32[]{:S(2)}, u32[]{:S(2)}) collective-permute-start(bf16[256,672]{1,0:T(8,128)(2,1)S(1)} %get-tuple-element.28), channel_id=1, source_target_pairs={{0,2},{1,3},{2,0},{3,1},{4,6},{5,7},{6,4},{7,5},{8,10},{9,11},{10,... | collective-permute-start | bytes 1032200 | tf_op jit(solution)/shard_map/ppermute | solution.py:74
  292.8 17.3 %collective-permute-start.26 = (bf16[256,672]{1,0:T(8,128)(2,1)S(1)}, bf16[256,672]{1,0:T(8,128)(2,1)S(1)}, u32[]{:S(2)}, u32[]{:S(2)}) collective-permute-start(bf16[256,672]{1,0:T(8,128)(2,1)S(1)} %get-tuple-element.27), channel_id=1, source_target_pairs={{0,3},{1,0},{2,1},{3,2},{4,7},{5,4},{6,5},{7,6},{8,11},{9,8},{10,9... | collective-permute-start | bytes 1032200 | tf_op jit(solution)/shard_map/ppermute | solution.py:74
  294.6 17.0 %collective-permute-start.14 = (bf16[320,384]{1,0:T(8,128)(2,1)}, bf16[320,384]{1,0:T(8,128)(2,1)}, u32[]{:S(2)}, u32[]{:S(2)}) collective-permute-start(bf16[320,384]{1,0:T(8,128)(2,1)} %collective-permute-done.13), channel_id=1, source_target_pairs={{4,0},{8,4},{5,1},{9,5},{6,2},{10,6},{7,3},{11,7},{20,16},{24,20},... | collective-permute-start | bytes 737288 | tf_op jit(solution)/shard_map/ppermute | solution.py:52
  295.9 17.0 %collective-permute-start.30 = (bf16[320,288]{0,1:T(8,128)(2,1)}, bf16[320,288]{0,1:T(8,128)(2,1)S(1)}, u32[]{:S(2)}, u32[]{:S(2)}) collective-permute-start(bf16[320,288]{0,1:T(8,128)(2,1)} %collective-permute-done.29), channel_id=1, source_target_pairs={{8,12},{9,13},{10,14},{11,15},{24,28},{25,29},{26,30},{27,31}} | collective-permute-start | bytes 552968 | tf_op jit(solution)/shard_map/ppermute | solution.py:50
  303.4 11.1 %collective-permute-start.33 = (bf16[320,288]{0,1:T(8,128)(2,1)}, bf16[320,288]{0,1:T(8,128)(2,1)}, u32[]{:S(2)}, u32[]{:S(2)}) collective-permute-start(bf16[320,288]{0,1:T(8,128)(2,1)} %collective-permute-done.32), channel_id=1, source_target_pairs={{4,0},{5,1},{6,2},{7,3},{20,16},{21,17},{22,18},{23,19}} | collective-permute-start | bytes 552968 | tf_op jit(solution)/shard_map/ppermute | solution.py:52
  304.7 12.5 %collective-permute-start.12 = (bf16[320,384]{1,0:T(8,128)(2,1)}, bf16[320,384]{1,0:T(8,128)(2,1)}, u32[]{:S(2)}, u32[]{:S(2)}) collective-permute-start(bf16[320,384]{1,0:T(8,128)(2,1)} %collective-permute-done.11), channel_id=1, source_target_pairs={{8,12},{9,13},{10,14},{11,15},{24,28},{25,29},{26,30},{27,31}} | collective-permute-start | bytes 737288 | tf_op jit(solution)/shard_map/ppermute | solution.py:50
  310.3 10.3 %collective-permute-start.27 = (bf16[256,672]{1,0:T(8,128)(2,1)S(1)}, bf16[256,672]{1,0:T(8,128)(2,1)S(1)}, u32[]{:S(2)}, u32[]{:S(2)}) collective-permute-start(bf16[256,672]{1,0:T(8,128)(2,1)S(1)} %fusion.32), channel_id=1, source_target_pairs={{0,16},{16,0},{1,17},{17,1},{2,18},{18,2},{3,19},{19,3},{4,20},{20... | collective-permute-start | bytes 1032200 | tf_op jit(solution)/shard_map/ppermute | solution.py:91
  311.6 23.9 %collective-permute-start.15 = (bf16[320,384]{1,0:T(8,128)(2,1)}, bf16[320,384]{1,0:T(8,128)(2,1)}, u32[]{:S(2)}, u32[]{:S(2)}) collective-permute-start(bf16[320,384]{1,0:T(8,128)(2,1)} %collective-permute-done.14), channel_id=1, source_target_pairs={{4,0},{5,1},{6,2},{7,3},{20,16},{21,17},{22,18},{23,19}} | collective-permute-start | bytes 737288 | tf_op jit(solution)/shard_map/ppermute | solution.py:52
  317.1 3.5 copy-start.21
  317.1 3.5 copy-start.22
  322.2 19.3 %all-to-all-start = ((bf16[4,64,672]{2,1,0:T(8,128)(2,1)}), bf16[4,64,672]{2,1,0:T(8,128)(2,1)S(1)}, u32[]{:S(2)}, u32[]{:S(2)}) async-start(bf16[4,64,672]{2,1,0:T(8,128)(2,1)} %broadcast_select_fusion), calls=%async_computation | async-start | bytes 786432 | tf_op jit(solution)/shard_map/all_to_all | solution.py:168
  328.9 118.1 %reduce-scatter.2.cloned.1.call-start = ((), (), s32[]{:S(2)}) async-start(), calls=%async_computation.3 | async-start | bytes 4096000 | tf_op jit(solution)/shard_map/reduce_scatter | solution.py:202
  345.3 5.5 %copy-start.12 = (bf16[256,1280]{1,0:T(8,128)(2,1)}, bf16[256,1280]{1,0:T(8,128)(2,1)S(1)}, u32[]{:S(2)}) copy-start(bf16[256,1280]{1,0:T(8,128)(2,1)S(1)} %fusion) | copy-start | bytes 1966084
  346.2 10.6 %collective-permute-start.34 = (bf16[64,1280]{1,0:T(8,128)(2,1)}, bf16[64,1280]{1,0:T(8,128)(2,1)S(1)}, u32[]{:S(2)}, u32[]{:S(2)}) collective-permute-start(bf16[64,1280]{1,0:T(8,128)(2,1)} %get-tuple-element.40), channel_id=1, source_target_pairs={{0,1},{1,2},{2,3},{3,0},{4,5},{5,6},{6,7},{7,4},{8,9},{9,10},{10,1... | collective-permute-start | bytes 491528 | tf_op jit(solution)/shard_map/ppermute | solution.py:74
  346.5 11.3 %collective-permute-start.35 = (bf16[64,1280]{1,0:T(8,128)(2,1)}, bf16[64,1280]{1,0:T(8,128)(2,1)S(1)}, u32[]{:S(2)}, u32[]{:S(2)}) collective-permute-start(bf16[64,1280]{1,0:T(8,128)(2,1)} %get-tuple-element.42), channel_id=1, source_target_pairs={{0,2},{1,3},{2,0},{3,1},{4,6},{5,7},{6,4},{7,5},{8,10},{9,11},{10,... | collective-permute-start | bytes 491528 | tf_op jit(solution)/shard_map/ppermute | solution.py:74
  349.3 8.5 %collective-permute-start.36 = (bf16[64,1280]{1,0:T(8,128)(2,1)}, bf16[64,1280]{1,0:T(8,128)(2,1)S(1)}, u32[]{:S(2)}, u32[]{:S(2)}) collective-permute-start(bf16[64,1280]{1,0:T(8,128)(2,1)} %get-tuple-element.41), channel_id=1, source_target_pairs={{0,3},{1,0},{2,1},{3,2},{4,7},{5,4},{6,5},{7,6},{8,11},{9,8},{10,9... | collective-permute-start | bytes 491528 | tf_op jit(solution)/shard_map/ppermute | solution.py:74
  352.2 5.7 %copy-start.6 = (f32[256,1280]{1,0:T(8,128)S(1)}, f32[256,1280]{1,0:T(8,128)}, u32[]{:S(2)}) copy-start(f32[256,1280]{1,0:T(8,128)} %copy-done.5) | copy-start | bytes 3932164
  353.9 10.8 %collective-permute-start.40 = (bf16[160,672]{1,0:T(8,128)(2,1)S(1)}, bf16[160,672]{1,0:T(8,128)(2,1)S(1)}, u32[]{:S(2)}, u32[]{:S(2)}) collective-permute-start(bf16[160,672]{1,0:T(8,128)(2,1)S(1)} %get-tuple-element.33), channel_id=1, source_target_pairs={{0,4},{4,8},{8,12},{12,0},{1,5},{5,9},{9,13},{13,1},{2,6},{6,10},{... | collective-permute-start | bytes 645128 | tf_op jit(solution)/shard_map/ppermute | solution.py:74
  354.0 19.5 %collective-permute-start.41 = (bf16[160,672]{1,0:T(8,128)(2,1)S(1)}, bf16[160,672]{1,0:T(8,128)(2,1)S(1)}, u32[]{:S(2)}, u32[]{:S(2)}) collective-permute-start(bf16[160,672]{1,0:T(8,128)(2,1)S(1)} %get-tuple-element.35), channel_id=1, source_target_pairs={{0,8},{4,12},{8,0},{12,4},{1,9},{5,13},{9,1},{13,5},{2,10},{6,14},... | collective-permute-start | bytes 645128 | tf_op jit(solution)/shard_map/ppermute | solution.py:74
  356.7 16.7 %collective-permute-start.42 = (bf16[160,672]{1,0:T(8,128)(2,1)S(1)}, bf16[160,672]{1,0:T(8,128)(2,1)S(1)}, u32[]{:S(2)}, u32[]{:S(2)}) collective-permute-start(bf16[160,672]{1,0:T(8,128)(2,1)S(1)} %get-tuple-element.34), channel_id=1, source_target_pairs={{0,12},{4,0},{8,4},{12,8},{1,13},{5,1},{9,5},{13,9},{2,14},{6,2},{... | collective-permute-start | bytes 645128 | tf_op jit(solution)/shard_map/ppermute | solution.py:74
  359.2 14.4 %collective-permute-start.37 = (bf16[64,1280]{1,0:T(8,128)(2,1)S(1)}, bf16[64,1280]{1,0:T(8,128)(2,1)S(1)}, u32[]{:S(2)}, u32[]{:S(2)}) collective-permute-start(bf16[64,1280]{1,0:T(8,128)(2,1)S(1)} %multiply_convert_fusion.2), channel_id=1, source_target_pairs={{0,3},{1,0},{2,1},{3,2},{4,7},{5,4},{6,5},{7,6},{8,11},{9,8},{10,9... | collective-permute-start | bytes 491528 | tf_op jit(solution)/shard_map/ppermute | solution.py:84
  360.6 13.0 %collective-permute-start.38 = (bf16[64,1280]{1,0:T(8,128)(2,1)S(1)}, bf16[64,1280]{1,0:T(8,128)(2,1)S(1)}, u32[]{:S(2)}, u32[]{:S(2)}) collective-permute-start(bf16[64,1280]{1,0:T(8,128)(2,1)S(1)} %multiply_convert_fusion.2), channel_id=1, source_target_pairs={{0,2},{1,3},{2,0},{3,1},{4,6},{5,7},{6,4},{7,5},{8,10},{9,11},{10,... | collective-permute-start | bytes 491528 | tf_op jit(solution)/shard_map/ppermute | solution.py:84
  364.8 8.9 %collective-permute-start.39 = (bf16[64,1280]{1,0:T(8,128)(2,1)S(1)}, bf16[64,1280]{1,0:T(8,128)(2,1)S(1)}, u32[]{:S(2)}, u32[]{:S(2)}) collective-permute-start(bf16[64,1280]{1,0:T(8,128)(2,1)S(1)} %multiply_convert_fusion.2), channel_id=1, source_target_pairs={{0,1},{1,2},{2,3},{3,0},{4,5},{5,6},{6,7},{7,4},{8,9},{9,10},{10,1... | collective-permute-start | bytes 491528 | tf_op jit(solution)/shard_map/ppermute | solution.py:84
  447.0 12.4 %copy-start.9 = (bf16[2,320,640]{2,1,0:T(8,128)(2,1)S(1)}, bf16[2,320,640]{2,1,0:T(8,128)(2,1)}, u32[]{:S(2)}) copy-start(bf16[2,320,640]{2,1,0:T(8,128)(2,1)} %reduce-scatter.2.cloned.1.call-done) | copy-start | bytes 2457604
  448.2 11.1 %collective-permute-start.43 = (bf16[2,160,640]{2,1,0:T(8,128)(2,1)S(1)}, bf16[2,160,640]{2,1,0:T(8,128)(2,1)S(1)}, u32[]{:S(2)}, u32[]{:S(2)}) collective-permute-start(bf16[2,160,640]{2,1,0:T(8,128)(2,1)S(1)} %fusion.73), channel_id=1, source_target_pairs={{0,16},{16,0},{1,17},{17,1},{2,18},{18,2},{3,19},{19,3},{4,20},{20... | collective-permute-start | bytes 1228808 | tf_op jit(solution)/shard_map/ppermute | solution.py:91
  (12 other events, 19.1 us)
Sparse Core Ops, SparseCore 0:
  130.1 53.2 all-reduce.1
  383.3 63.6 reduce-scatter.1

commit v4 on v3

--- a/solution.py
+++ b/solution.py
@@ -173,18 +173,18 @@
     act = jnp.dot(normed, w_mlp[0], preferred_element_type=f32)
     hidden = jax.nn.gelu(act, approximate=False).astype(bf16)
     partial_out = times_transposed(hidden, w_mlp[1])
-    mixed = flat + lax.psum(partial_out.astype(bf16), ("grp", "tp")).astype(f32)
-    feat = norm_rows(mixed).astype(bf16)
+    share = rows // count_tp
+    out = summed_piece(partial_out.astype(bf16).reshape(count_tp, share, width), "tp").astype(bf16)
+    out = out.astype(f32) + across(out).astype(f32)
+    own_mixed = lax.dynamic_slice_in_dim(flat, column * share, share, 0) + out
+    feat = joined_pieces(norm_rows(own_mixed).astype(bf16), "tp").reshape(rows, width)
     pred_d = jnp.dot(feat, w_dino, preferred_element_type=f32)
     pred_s = jnp.dot(feat, w_sig, preferred_element_type=f32)
     diff_d = ((pred_d - target[:, :cols_d]) * scale).astype(bf16)
     diff_s = ((pred_s - target[:, cols_d:]) * scale).astype(bf16)
 
     dfeat = times_transposed(diff_d, w_dino) + times_transposed(diff_s, w_sig)
-    dfeat = summed_piece(dfeat.astype(bf16).reshape(count_tp, rows // count_tp, width), "tp")
-    own_mixed = lax.dynamic_slice_in_dim(
-        mixed, column * (rows // count_tp), rows // count_tp, 0
-    )
+    dfeat = summed_piece(dfeat.astype(bf16).reshape(count_tp, share, width), "tp")
     dmixed = joined_pieces(norm_back(own_mixed, dfeat).astype(bf16), "tp").reshape(rows, width)
     own_feat = lax.dynamic_slice_in_dim(feat, group * half, half, 1)
     grad_heads = over_rows(own_feat, jnp.concatenate([diff_d, diff_s], axis=1)).astype(bf16)

time: 470 us -> 432 us (0.919)
  waiting for transfers between devices: 278 us -> 224 us
  starting transfers between devices: 81.8 us -> 91.9 us
  other arithmetic: 20.1 us -> 25 us
    psum x1 -> x0, waiting for transfers between devices: 50.6 us -> none  [body(): mixed = flat + lax.psum(partial_out.astype(bf16), ('grp', 'tp')).astype(f32)]
    ppermute x15, waiting for transfers between devices: 117 us -> 96.8 us  [gathered_rows(): lax.ppermute(down[-1], 'dp', [(i, i - 1) for i in range(1, count - step +...]
    ppermute x15, waiting for transfers between devices: 9.97 us -> 26.7 us  [gathered_rows(): lax.ppermute(up[-1], 'dp', [(i, i + 1) for i in range(step - 1, count - 1)])]
    unnamed x87 -> x100, local copies, waits for them, and re-layouts: 33.2 us -> 37.3 us
    ppermute x9 -> x12, starting transfers between devices: 10.3 us -> 13.3 us  [summed_piece(): total = total + lax.ppermute(piece, axis, pairs).astype(jnp.float32)]
    ppermute x9 -> x12, waiting for transfers between devices: 23.6 us -> 23 us  [summed_piece(): total = total + lax.ppermute(piece, axis, pairs).astype(jnp.float32)]
  transfers between devices with their start and end apart: 47 -> 53, of which waited for: 16 -> 24; matrix products, arithmetic and copies ran while one was open for 15% -> 16% of each run, Pallas kernels for 0% -> 0%
where the time goes in v4:
time: 432 us; the launch traced here: 430 us
  waiting for transfers between devices  224 us (52%)
  starting transfers between devices  91.9 us (21%)
  local copies, waits for them, and re-layouts  52.9 us (12%)
  other arithmetic  25 us (6%)
  matrix products  20.6 us (5%)
  between operations  15.2 us (4%)
    ppermute x15, waiting for transfers between devices, gathered_rows(): lax.ppermute(down[-1], 'dp', [(i, i - 1) for i in range(1, count - step +...  96.8 us
    reduce_scatter x1, waiting for transfers between devices, body(): sum_mlp = lax.psum_scatter(grad_mlp, 'dp', scatter_dimension=1, tiled=True)  64.3 us
    ppermute x15, starting transfers between devices, gathered_rows(): lax.ppermute(up[-1], 'dp', [(i, i + 1) for i in range(step - 1, count - 1)])  41.5 us
    unnamed x100, local copies, waits for them, and re-layouts  37.3 us
    ppermute x15, waiting for transfers between devices, gathered_rows(): lax.ppermute(up[-1], 'dp', [(i, i + 1) for i in range(step - 1, count - 1)])  26.7 us
    ppermute x12, waiting for transfers between devices, summed_piece(): total = total + lax.ppermute(piece, axis, pairs).astype(jnp.float32)  23 us
    ppermute x15, starting transfers between devices, gathered_rows(): lax.ppermute(down[-1], 'dp', [(i, i - 1) for i in range(1, count - step +...  19.3 us
    ppermute x12, starting transfers between devices, summed_piece(): total = total + lax.ppermute(piece, axis, pairs).astype(jnp.float32)  13.3 us
  transfers between devices with their start and end apart: 53, of which 24 were waited for; matrix products, arithmetic and copies ran while one was open for 16% of the time, Pallas kernels for 0%

profile of v4, /device:TPU:0, one launch (start us, length us, event | category | flops | bytes accessed | tf_op | source)
XLA Modules:
  0.0 429.9 jit_solution(4715988953288605897)
XLA Ops:
  7.2 1.6 slice_select_fusion.1
  8.8 6.0 %collective-permute-start = (bf16[2,320,640]{2,1,0:T(8,128)(2,1)S(1)}, bf16[2,320,640]{2,1,0:T(8,128)(2,1)}, u32[]{:S(2)}, u32[]{:S(2)}) collective-permute-start(bf16[2,320,640]{2,1,0:T(8,128)(2,1)S(1)} %slice_select_fusion.1), channel_id=1, source_target_pairs={{0,4},{4,8},{8,12},{1,5},{5,9},{9,13},{2,6},{6,10},{10,14},{3,7},{... | collective-permute-start | bytes 2457608 | tf_op jit(solution)/shard_map/ppermute | solution.py:50
  18.4 13.0 %collective-permute-done = bf16[2,320,640]{2,1,0:T(8,128)(2,1)} collective-permute-done((bf16[2,320,640]{2,1,0:T(8,128)(2,1)S(1)}, bf16[2,320,640]{2,1,0:T(8,128)(2,1)}, u32[]{:S(2)}, u32[]{:S(2)}) %collective-permute-start) | collective-permute-done | bytes 819232 | tf_op jit(solution)/shard_map/ppermute | solution.py:50
  31.4 1.6 collective-permute-start.1
  32.9 3.6 collective-permute-done.2
  37.8 1.8 slice_select_fusion
  40.8 16.9 %collective-permute-done.3 = bf16[2,320,640]{2,1,0:T(8,128)(2,1)} collective-permute-done((bf16[2,320,640]{2,1,0:T(8,128)(2,1)}, bf16[2,320,640]{2,1,0:T(8,128)(2,1)}, u32[]{:S(2)}, u32[]{:S(2)}) %collective-permute-start.3) | collective-permute-done | bytes 819232 | tf_op jit(solution)/shard_map/ppermute | solution.py:52
  61.2 1.4 constant_dynamic-update-slice_fusion.5
  66.7 13.2 %collective-permute-done.5 = bf16[2,320,640]{2,1,0:T(8,128)(2,1)S(1)} collective-permute-done((bf16[2,320,640]{2,1,0:T(8,128)(2,1)}, bf16[2,320,640]{2,1,0:T(8,128)(2,1)S(1)}, u32[]{:S(2)}, u32[]{:S(2)}) %collective-permute-start.5) | collective-permute-done | bytes 819232 | tf_op jit(solution)/shard_map/ppermute | solution.py:52
  80.1 2.8 fusion.27
  85.2 1.5 collective-permute-start.7
  86.7 1.4 collective-permute-start.8
  88.7 2.5 collective-permute-start.25
  93.1 1.4 collective-permute-done.8
  95.7 1.6 collective-permute-start.9
  99.8 4.2 collective-permute-start.13
  105.3 2.2 collective-permute-done.25
  107.5 1.5 collective-permute-start.26
  109.0 3.8 collective-permute-done.28
  117.0 1.6 collective-permute-done.10
  119.1 11.6 %collective-permute-done.13 = bf16[3,384,512]{2,1,0:T(8,128)(2,1)} collective-permute-done((bf16[3,384,512]{2,1,0:T(8,128)(2,1)S(1)}, bf16[3,384,512]{2,1,0:T(8,128)(2,1)}, u32[]{:S(2)}, u32[]{:S(2)}) %collective-permute-start.13) | collective-permute-done | bytes 1179680 | tf_op jit(solution)/shard_map/ppermute | solution.py:50
  130.7 7.3 %collective-permute-done.15 = bf16[3,384,512]{2,1,0:T(8,128)(2,1)} collective-permute-done((bf16[3,384,512]{2,1,0:T(8,128)(2,1)S(1)}, bf16[3,384,512]{2,1,0:T(8,128)(2,1)}, u32[]{:S(2)}, u32[]{:S(2)}) %collective-permute-start.15) | collective-permute-done | bytes 1179680 | tf_op jit(solution)/shard_map/ppermute | solution.py:52
  138.0 1.7 collective-permute-start.14
  141.0 11.9 %collective-permute-done.29 = bf16[2,288,564]{2,1,0:T(8,128)(2,1)} collective-permute-done((bf16[2,288,564]{2,1,0:T(8,128)(2,1)}, bf16[2,288,564]{2,1,0:T(8,128)(2,1)}, u32[]{:S(2)}, u32[]{:S(2)}) %collective-permute-start.29) | collective-permute-done | bytes 649760 | tf_op jit(solution)/shard_map/ppermute | solution.py:52
  156.8 23.2 %collective-permute-done.16 = bf16[3,384,512]{2,1,0:T(8,128)(2,1)} collective-permute-done((bf16[3,384,512]{2,1,0:T(8,128)(2,1)}, bf16[3,384,512]{2,1,0:T(8,128)(2,1)}, u32[]{:S(2)}, u32[]{:S(2)}) %collective-permute-start.16) | collective-permute-done | bytes 1179680 | tf_op jit(solution)/shard_map/ppermute | solution.py:52
  180.0 1.7 collective-permute-start.23
  186.8 5.7 %collective-permute-done.30 = bf16[2,288,564]{2,1,0:T(8,128)(2,1)S(1)} collective-permute-done((bf16[2,288,564]{2,1,0:T(8,128)(2,1)}, bf16[2,288,564]{2,1,0:T(8,128)(2,1)S(1)}, u32[]{:S(2)}, u32[]{:S(2)}) %collective-permute-start.30) | collective-permute-done | bytes 649760 | tf_op jit(solution)/shard_map/ppermute | solution.py:52
  195.0 3.8 convolution_convert_fusion.2
  198.8 5.2 %collective-permute-start.35 = (bf16[320,288]{0,1:T(8,128)(2,1)}, bf16[320,288]{0,1:T(8,128)(2,1)}, u32[]{:S(2)}, u32[]{:S(2)}) collective-permute-start(bf16[320,288]{0,1:T(8,128)(2,1)} %param.16), channel_id=1, source_target_pairs={{0,4},{4,8},{8,12},{1,5},{5,9},{9,13},{2,6},{6,10},{10,14},{3,7},{... | collective-permute-start | bytes 552968 | tf_op jit(solution)/shard_map/ppermute | solution.py:50
  205.4 11.0 %collective-permute-start.17 = (bf16[320,384]{1,0:T(8,128)(2,1)}, bf16[320,384]{1,0:T(8,128)(2,1)}, u32[]{:S(2)}, u32[]{:S(2)}) collective-permute-start(bf16[320,384]{1,0:T(8,128)(2,1)} %param.15), channel_id=1, source_target_pairs={{0,4},{4,8},{8,12},{1,5},{5,9},{9,13},{2,6},{6,10},{10,14},{3,7},{... | collective-permute-start | bytes 737288 | tf_op jit(solution)/shard_map/ppermute | solution.py:50
  218.6 8.6 %collective-permute-done.38 = bf16[320,288]{0,1:T(8,128)(2,1)} collective-permute-done((bf16[320,288]{0,1:T(8,128)(2,1)}, bf16[320,288]{0,1:T(8,128)(2,1)}, u32[]{:S(2)}, u32[]{:S(2)}) %collective-permute-start.38) | collective-permute-done | bytes 184352 | tf_op jit(solution)/shard_map/ppermute | solution.py:52
  229.8 1.4 collective-permute-start.18
  238.0 1.4 constant_dynamic-update-slice_fusion.14
  239.5 3.2 copy-done.14
  244.1 3.2 convolution_convert_fusion.3
  248.8 2.2 collective-permute-start.32
  251.1 1.4 collective-permute-start.33
  254.5 5.0 %collective-permute-done.31 = bf16[256,672]{1,0:T(8,128)(2,1)S(1)} collective-permute-done((bf16[256,672]{1,0:T(8,128)(2,1)S(1)}, bf16[256,672]{1,0:T(8,128)(2,1)S(1)}, u32[]{:S(2)}, u32[]{:S(2)}) %collective-permute-start.31) | collective-permute-done | bytes 344096 | tf_op jit(solution)/shard_map/ppermute | solution.py:74
  262.4 6.0 %collective-permute-done.33 = bf16[256,672]{1,0:T(8,128)(2,1)S(1)} collective-permute-done((bf16[256,672]{1,0:T(8,128)(2,1)S(1)}, bf16[256,672]{1,0:T(8,128)(2,1)S(1)}, u32[]{:S(2)}, u32[]{:S(2)}) %collective-permute-start.33) | collective-permute-done | bytes 344096 | tf_op jit(solution)/shard_map/ppermute | solution.py:74
  268.6 1.6 collective-permute-start.34
  272.2 2.6 collective-permute-done.40
  274.8 2.6 concatenate.45
  277.4 1.7 constant_dynamic-update-slice_fusion.13
  279.1 1.7 constant_dynamic-update-slice_fusion.12
  283.3 1.8 broadcast_select_fusion
  285.1 9.0 %all-to-all-start = ((bf16[4,64,672]{2,1,0:T(8,128)(2,1)}), bf16[4,64,672]{2,1,0:T(8,128)(2,1)S(1)}, u32[]{:S(2)}, u32[]{:S(2)}) async-start(bf16[4,64,672]{2,1,0:T(8,128)(2,1)} %broadcast_select_fusion), calls=%async_computation | async-start | bytes 786432 | tf_op jit(solution)/shard_map/all_to_all | solution.py:168
  294.1 1.7 constant_dynamic-update-slice_fusion.11
  295.7 1.7 constant_dynamic-update-slice_fusion.10
  297.4 1.7 constant_dynamic-update-slice_fusion.9
  299.1 1.7 constant_dynamic-update-slice_fusion.8
  300.8 1.7 constant_dynamic-update-slice_fusion.7
  302.4 3.8 all-to-all-done
  306.3 1.7 fusion.19
  310.8 1.7 collective-permute-start.43
  314.1 2.7 collective-permute-start.48
  317.0 2.2 collective-permute-start.49
  321.4 2.9 collective-permute-start.45
  324.9 9.6 %collective-permute-done.48 = bf16[160,672]{1,0:T(8,128)(2,1)S(1)} collective-permute-done((bf16[160,672]{1,0:T(8,128)(2,1)S(1)}, bf16[160,672]{1,0:T(8,128)(2,1)S(1)}, u32[]{:S(2)}, u32[]{:S(2)}) %collective-permute-start.48) | collective-permute-done | bytes 215072 | tf_op jit(solution)/shard_map/ppermute | solution.py:74
  337.1 4.1 convolution_convert_fusion.1
  341.2 1.6 copy.18
  342.9 2.0 pad_maximum_fusion
  345.0 64.3 %reduce-scatter.2.cloned.1.call-done = bf16[2,320,640]{2,1,0:T(8,128)(2,1)} async-done(((bf16[2,1280,640]{2,1,0:T(8,128)(2,1)}), bf16[2,320,640]{2,1,0:T(8,128)(2,1)}) %reduce-scatter.2.cloned.1.call-update) | async-done | bytes 819216 | tf_op jit(solution)/shard_map/reduce_scatter | solution.py:202
  410.5 1.5 collective-permute-start.50
  413.5 8.1 %collective-permute-done.50 = bf16[2,160,640]{2,1,0:T(8,128)(2,1)S(1)} collective-permute-done((bf16[2,160,640]{2,1,0:T(8,128)(2,1)S(1)}, bf16[2,160,640]{2,1,0:T(8,128)(2,1)S(1)}, u32[]{:S(2)}, u32[]{:S(2)}) %collective-permute-start.50) | collective-permute-done | bytes 409632 | tf_op jit(solution)/shard_map/ppermute | solution.py:91
  (226 shorter events, 80.4 us)
Async XLA Ops:
  7.2 8.9 %copy-start = (bf16[4,64,1536]{2,1,0:T(8,128)(2,1)S(1)}, bf16[4,64,1536]{2,1,0:T(8,128)(2,1)}, u32[]{:S(2)}) copy-start(bf16[4,64,1536]{2,1,0:T(8,128)(2,1)} %param.9) | copy-start | bytes 2359300
  7.2 9.5 %copy-start.3 = (bf16[1,256,1280]{2,1,0:T(8,128)(2,1)S(1)}, bf16[1,256,1280]{2,1,0:T(8,128)(2,1)}, u32[]{:S(2)}) copy-start(bf16[1,256,1280]{2,1,0:T(8,128)(2,1)} %param.11) | copy-start | bytes 1966084
  8.8 8.6 %copy-start.10 = (bf16[2,288,1076]{2,1,0:T(8,128)(2,1)S(1)}, bf16[2,288,1076]{2,1,0:T(8,128)(2,1)}, u32[]{:S(2)}) copy-start(bf16[2,288,1076]{2,1,0:T(8,128)(2,1)} %param.13) | copy-start | bytes 3718660
  8.8 22.6 %collective-permute-start = (bf16[2,320,640]{2,1,0:T(8,128)(2,1)S(1)}, bf16[2,320,640]{2,1,0:T(8,128)(2,1)}, u32[]{:S(2)}, u32[]{:S(2)}) collective-permute-start(bf16[2,320,640]{2,1,0:T(8,128)(2,1)S(1)} %slice_select_fusion.1), channel_id=1, source_target_pairs={{0,4},{4,8},{8,12},{1,5},{5,9},{9,13},{2,6},{6,10},{10,14},{3,7},{... | collective-permute-start | bytes 2457608 | tf_op jit(solution)/shard_map/ppermute | solution.py:50
  14.8 21.7 %collective-permute-start.2 = (bf16[2,320,640]{2,1,0:T(8,128)(2,1)S(1)}, bf16[2,320,640]{2,1,0:T(8,128)(2,1)}, u32[]{:S(2)}, u32[]{:S(2)}) collective-permute-start(bf16[2,320,640]{2,1,0:T(8,128)(2,1)S(1)} %slice_select_fusion.1), channel_id=1, source_target_pairs={{4,0},{8,4},{12,8},{5,1},{9,5},{13,9},{6,2},{10,6},{14,10},{7,3},{... | collective-permute-start | bytes 2457608 | tf_op jit(solution)/shard_map/ppermute | solution.py:52
  16.8 21.0 %copy-start.30 = (s32[4]{0:T(128)S(1)}, s32[4]{0:T(128)}, u32[]{:S(2)}) copy-start(s32[4]{0:T(128)} %param.17) | copy-start | bytes 52
  17.2 62.9 %copy-start.27 = (f32[256]{0:T(256)}, f32[256]{0:T(256)S(1)}, u32[]{:S(2)}) copy-start(f32[256]{0:T(256)S(1)} %add_rsqrt_fusion.2) | copy-start | bytes 3076
  31.4 9.4 %collective-permute-start.1 = (bf16[2,320,640]{2,1,0:T(8,128)(2,1)}, bf16[2,320,640]{2,1,0:T(8,128)(2,1)}, u32[]{:S(2)}, u32[]{:S(2)}) collective-permute-start(bf16[2,320,640]{2,1,0:T(8,128)(2,1)} %collective-permute-done), channel_id=1, source_target_pairs={{4,8},{8,12},{5,9},{9,13},{6,10},{10,14},{7,11},{11,15},{20,24},{2... | collective-permute-start | bytes 2457608 | tf_op jit(solution)/shard_map/ppermute | solution.py:50
  36.5 21.1 %collective-permute-start.3 = (bf16[2,320,640]{2,1,0:T(8,128)(2,1)}, bf16[2,320,640]{2,1,0:T(8,128)(2,1)}, u32[]{:S(2)}, u32[]{:S(2)}) collective-permute-start(bf16[2,320,640]{2,1,0:T(8,128)(2,1)} %collective-permute-done.2), channel_id=1, source_target_pairs={{4,0},{8,4},{5,1},{9,5},{6,2},{10,6},{7,3},{11,7},{20,16},{24,20},... | collective-permute-start | bytes 2457608 | tf_op jit(solution)/shard_map/ppermute | solution.py:52
  57.6 3.4 collective-permute-start.4
  59.8 20.1 %collective-permute-start.5 = (bf16[2,320,640]{2,1,0:T(8,128)(2,1)}, bf16[2,320,640]{2,1,0:T(8,128)(2,1)S(1)}, u32[]{:S(2)}, u32[]{:S(2)}) collective-permute-start(bf16[2,320,640]{2,1,0:T(8,128)(2,1)} %collective-permute-done.3), channel_id=1, source_target_pairs={{4,0},{5,1},{6,2},{7,3},{20,16},{21,17},{22,18},{23,19}} | collective-permute-start | bytes 2457608 | tf_op jit(solution)/shard_map/ppermute | solution.py:52
  85.2 7.2 %collective-permute-start.6 = (bf16[64,1280]{1,0:T(8,128)(2,1)}, bf16[64,1280]{1,0:T(8,128)(2,1)S(1)}, u32[]{:S(2)}, u32[]{:S(2)}) collective-permute-start(bf16[64,1280]{1,0:T(8,128)(2,1)} %get-tuple-element.43), channel_id=1, source_target_pairs={{0,1},{1,2},{2,3},{3,0},{4,5},{5,6},{6,7},{7,4},{8,9},{9,10},{10,1... | collective-permute-start | bytes 491528 | tf_op jit(solution)/shard_map/ppermute | solution.py:74
  85.2 7.3 %collective-permute-start.7 = (bf16[64,1280]{1,0:T(8,128)(2,1)}, bf16[64,1280]{1,0:T(8,128)(2,1)S(1)}, u32[]{:S(2)}, u32[]{:S(2)}) collective-permute-start(bf16[64,1280]{1,0:T(8,128)(2,1)} %get-tuple-element.45), channel_id=1, source_target_pairs={{0,2},{1,3},{2,0},{3,1},{4,6},{5,7},{6,4},{7,5},{8,10},{9,11},{10,... | collective-permute-start | bytes 491528 | tf_op jit(solution)/shard_map/ppermute | solution.py:74
  86.7 7.8 %collective-permute-start.8 = (bf16[64,1280]{1,0:T(8,128)(2,1)}, bf16[64,1280]{1,0:T(8,128)(2,1)}, u32[]{:S(2)}, u32[]{:S(2)}) collective-permute-start(bf16[64,1280]{1,0:T(8,128)(2,1)} %get-tuple-element.44), channel_id=1, source_target_pairs={{0,3},{1,0},{2,1},{3,2},{4,7},{5,4},{6,5},{7,6},{8,11},{9,8},{10,9... | collective-permute-start | bytes 491528 | tf_op jit(solution)/shard_map/ppermute | solution.py:74
  88.7 18.8 %collective-permute-start.25 = (bf16[2,288,564]{2,1,0:T(8,128)(2,1)}, bf16[2,288,564]{2,1,0:T(8,128)(2,1)}, u32[]{:S(2)}, u32[]{:S(2)}) collective-permute-start(bf16[2,288,564]{2,1,0:T(8,128)(2,1)} %slice_select_fusion.2), channel_id=1, source_target_pairs={{0,4},{4,8},{8,12},{1,5},{5,9},{9,13},{2,6},{6,10},{10,14},{3,7},{... | collective-permute-start | bytes 1949192 | tf_op jit(solution)/shard_map/ppermute | solution.py:50
  91.1 21.6 %collective-permute-start.28 = (bf16[2,288,564]{2,1,0:T(8,128)(2,1)}, bf16[2,288,564]{2,1,0:T(8,128)(2,1)}, u32[]{:S(2)}, u32[]{:S(2)}) collective-permute-start(bf16[2,288,564]{2,1,0:T(8,128)(2,1)} %slice_select_fusion.2), channel_id=1, source_target_pairs={{4,0},{8,4},{12,8},{5,1},{9,5},{13,9},{6,2},{10,6},{14,10},{7,3},{... | collective-permute-start | bytes 1949192 | tf_op jit(solution)/shard_map/ppermute | solution.py:52
  95.7 18.4 %copy-start.20 = (bf16[64,1280]{1,0:T(8,128)(2,1)}, bf16[64,1280]{1,0:T(8,128)(2,1)S(1)}, u32[]{:S(2)}) copy-start(bf16[64,1280]{1,0:T(8,128)(2,1)S(1)} %fusion.73) | copy-start | bytes 491524
  95.7 18.4 %collective-permute-start.9 = (bf16[64,1280]{1,0:T(8,128)(2,1)S(1)}, bf16[64,1280]{1,0:T(8,128)(2,1)}, u32[]{:S(2)}, u32[]{:S(2)}) collective-permute-start(bf16[64,1280]{1,0:T(8,128)(2,1)S(1)} %fusion.73), channel_id=1, source_target_pairs={{0,16},{16,0},{1,17},{17,1},{2,18},{18,2},{3,19},{19,3},{4,20},{20... | collective-permute-start | bytes 491528 | tf_op jit(solution)/shard_map/ppermute | solution.py:91
  99.8 30.9 %collective-permute-start.13 = (bf16[3,384,512]{2,1,0:T(8,128)(2,1)S(1)}, bf16[3,384,512]{2,1,0:T(8,128)(2,1)}, u32[]{:S(2)}, u32[]{:S(2)}) collective-permute-start(bf16[3,384,512]{2,1,0:T(8,128)(2,1)S(1)} %slice_select_fusion), channel_id=1, source_target_pairs={{0,4},{4,8},{8,12},{1,5},{5,9},{9,13},{2,6},{6,10},{10,14},{3,7},{... | collective-permute-start | bytes 3538952 | tf_op jit(solution)/shard_map/ppermute | solution.py:50
  104.0 34.0 %collective-permute-start.15 = (bf16[3,384,512]{2,1,0:T(8,128)(2,1)S(1)}, bf16[3,384,512]{2,1,0:T(8,128)(2,1)}, u32[]{:S(2)}, u32[]{:S(2)}) collective-permute-start(bf16[3,384,512]{2,1,0:T(8,128)(2,1)S(1)} %slice_select_fusion), channel_id=1, source_target_pairs={{4,0},{8,4},{12,8},{5,1},{9,5},{13,9},{6,2},{10,6},{14,10},{7,3},{... | collective-permute-start | bytes 3538952 | tf_op jit(solution)/shard_map/ppermute | solution.py:52
  107.5 32.3 %collective-permute-start.26 = (bf16[2,288,564]{2,1,0:T(8,128)(2,1)}, bf16[2,288,564]{2,1,0:T(8,128)(2,1)}, u32[]{:S(2)}, u32[]{:S(2)}) collective-permute-start(bf16[2,288,564]{2,1,0:T(8,128)(2,1)} %collective-permute-done.25), channel_id=1, source_target_pairs={{4,8},{8,12},{5,9},{9,13},{6,10},{10,14},{7,11},{11,15},{20,24},{2... | collective-permute-start | bytes 1949192 | tf_op jit(solution)/shard_map/ppermute | solution.py:50
  112.8 40.2 %collective-permute-start.29 = (bf16[2,288,564]{2,1,0:T(8,128)(2,1)}, bf16[2,288,564]{2,1,0:T(8,128)(2,1)}, u32[]{:S(2)}, u32[]{:S(2)}) collective-permute-start(bf16[2,288,564]{2,1,0:T(8,128)(2,1)} %collective-permute-done.28), channel_id=1, source_target_pairs={{4,0},{8,4},{5,1},{9,5},{6,2},{10,6},{7,3},{11,7},{20,16},{24,20},... | collective-permute-start | bytes 1949192 | tf_op jit(solution)/shard_map/ppermute | solution.py:52
  115.7 2.9 collective-permute-start.10
  118.6 35.1 %collective-permute-start.11 = (bf16[64,1280]{1,0:T(8,128)(2,1)S(1)}, bf16[64,1280]{1,0:T(8,128)(2,1)S(1)}, u32[]{:S(2)}, u32[]{:S(2)}) collective-permute-start(bf16[64,1280]{1,0:T(8,128)(2,1)S(1)} %fusion.87), channel_id=1, source_target_pairs={{0,2},{1,3},{2,0},{3,1},{4,6},{5,7},{6,4},{7,5},{8,10},{9,11},{10,... | collective-permute-start | bytes 491528 | tf_op jit(solution)/shard_map/ppermute | solution.py:84
  130.7 24.3 %collective-permute-start.12 = (bf16[64,1280]{1,0:T(8,128)(2,1)S(1)}, bf16[64,1280]{1,0:T(8,128)(2,1)S(1)}, u32[]{:S(2)}, u32[]{:S(2)}) collective-permute-start(bf16[64,1280]{1,0:T(8,128)(2,1)S(1)} %fusion.87), channel_id=1, source_target_pairs={{0,1},{1,2},{2,3},{3,0},{4,5},{5,6},{6,7},{7,4},{8,9},{9,10},{10,1... | collective-permute-start | bytes 491528 | tf_op jit(solution)/shard_map/ppermute | solution.py:84
  138.0 18.7 %collective-permute-start.14 = (bf16[3,384,512]{2,1,0:T(8,128)(2,1)}, bf16[3,384,512]{2,1,0:T(8,128)(2,1)}, u32[]{:S(2)}, u32[]{:S(2)}) collective-permute-start(bf16[3,384,512]{2,1,0:T(8,128)(2,1)} %collective-permute-done.13), channel_id=1, source_target_pairs={{4,8},{8,12},{5,9},{9,13},{6,10},{10,14},{7,11},{11,15},{20,24},{2... | collective-permute-start | bytes 3538952 | tf_op jit(solution)/shard_map/ppermute | solution.py:50
  139.7 40.3 %collective-permute-start.16 = (bf16[3,384,512]{2,1,0:T(8,128)(2,1)}, bf16[3,384,512]{2,1,0:T(8,128)(2,1)}, u32[]{:S(2)}, u32[]{:S(2)}) collective-permute-start(bf16[3,384,512]{2,1,0:T(8,128)(2,1)} %collective-permute-done.15), channel_id=1, source_target_pairs={{4,0},{8,4},{5,1},{9,5},{6,2},{10,6},{7,3},{11,7},{20,16},{24,20},... | collective-permute-start | bytes 3538952 | tf_op jit(solution)/shard_map/ppermute | solution.py:52
  153.0 3.7 collective-permute-start.27
  153.7 38.9 %collective-permute-start.30 = (bf16[2,288,564]{2,1,0:T(8,128)(2,1)}, bf16[2,288,564]{2,1,0:T(8,128)(2,1)S(1)}, u32[]{:S(2)}, u32[]{:S(2)}) collective-permute-start(bf16[2,288,564]{2,1,0:T(8,128)(2,1)} %collective-permute-done.29), channel_id=1, source_target_pairs={{4,0},{5,1},{6,2},{7,3},{20,16},{21,17},{22,18},{23,19}} | collective-permute-start | bytes 1949192 | tf_op jit(solution)/shard_map/ppermute | solution.py:52
  156.8 27.4 %copy-start.6 = (bf16[2,288,564]{2,1,0:T(8,128)(2,1)S(1)}, bf16[2,288,564]{2,1,0:T(8,128)(2,1)}, u32[]{:S(2)}) copy-start(bf16[2,288,564]{2,1,0:T(8,128)(2,1)} %slice_select_fusion.2) | copy-start | bytes 1949188
  180.0 49.8 %collective-permute-start.23 = (bf16[3,384,512]{2,1,0:T(8,128)(2,1)}, bf16[3,384,512]{2,1,0:T(8,128)(2,1)}, u32[]{:S(2)}, u32[]{:S(2)}) collective-permute-start(bf16[3,384,512]{2,1,0:T(8,128)(2,1)} %collective-permute-done.14), channel_id=1, source_target_pairs={{8,12},{9,13},{10,14},{11,15},{24,28},{25,29},{26,30},{27,31}} | collective-permute-start | bytes 3538952 | tf_op jit(solution)/shard_map/ppermute | solution.py:50
  185.5 9.5 %copy-start.21 = (bf16[4,64,1152]{2,1,0:T(8,128)(2,1)S(1)}, bf16[4,64,1152]{2,1,0:T(8,128)(2,1)}, u32[]{:S(2)}) copy-start(bf16[4,64,1152]{2,1,0:T(8,128)(2,1)} %fusion.17) | copy-start | bytes 1769476
  185.5 9.5 %copy-start.31 = (pred[564]{0:T(1024)(128)(4,1)S(1)}, pred[564]{0:T(1024)(128)(4,1)}, u32[]{:S(2)}) copy-start(pred[564]{0:T(1024)(128)(4,1)} %fusion.104) | copy-start | bytes 1696
  192.7 45.3 %collective-permute-start.24 = (bf16[3,384,512]{2,1,0:T(8,128)(2,1)}, bf16[3,384,512]{2,1,0:T(8,128)(2,1)}, u32[]{:S(2)}, u32[]{:S(2)}) collective-permute-start(bf16[3,384,512]{2,1,0:T(8,128)(2,1)} %collective-permute-done.16), channel_id=1, source_target_pairs={{4,0},{5,1},{6,2},{7,3},{20,16},{21,17},{22,18},{23,19}} | collective-permute-start | bytes 3538952 | tf_op jit(solution)/shard_map/ppermute | solution.py:52
  198.8 18.4 %collective-permute-start.35 = (bf16[320,288]{0,1:T(8,128)(2,1)}, bf16[320,288]{0,1:T(8,128)(2,1)}, u32[]{:S(2)}, u32[]{:S(2)}) collective-permute-start(bf16[320,288]{0,1:T(8,128)(2,1)} %param.16), channel_id=1, source_target_pairs={{0,4},{4,8},{8,12},{1,5},{5,9},{9,13},{2,6},{6,10},{10,14},{3,7},{... | collective-permute-start | bytes 552968 | tf_op jit(solution)/shard_map/ppermute | solution.py:50
  204.1 23.1 %collective-permute-start.38 = (bf16[320,288]{0,1:T(8,128)(2,1)}, bf16[320,288]{0,1:T(8,128)(2,1)}, u32[]{:S(2)}, u32[]{:S(2)}) collective-permute-start(bf16[320,288]{0,1:T(8,128)(2,1)} %param.16), channel_id=1, source_target_pairs={{4,0},{8,4},{12,8},{5,1},{9,5},{13,9},{6,2},{10,6},{14,10},{7,3},{... | collective-permute-start | bytes 552968 | tf_op jit(solution)/shard_map/ppermute | solution.py:52
  205.4 23.1 %collective-permute-start.17 = (bf16[320,384]{1,0:T(8,128)(2,1)}, bf16[320,384]{1,0:T(8,128)(2,1)}, u32[]{:S(2)}, u32[]{:S(2)}) collective-permute-start(bf16[320,384]{1,0:T(8,128)(2,1)} %param.15), channel_id=1, source_target_pairs={{0,4},{4,8},{8,12},{1,5},{5,9},{9,13},{2,6},{6,10},{10,14},{3,7},{... | collective-permute-start | bytes 737288 | tf_op jit(solution)/shard_map/ppermute | solution.py:50
  217.3 31.6 %collective-permute-start.20 = (bf16[320,384]{1,0:T(8,128)(2,1)}, bf16[320,384]{1,0:T(8,128)(2,1)}, u32[]{:S(2)}, u32[]{:S(2)}) collective-permute-start(bf16[320,384]{1,0:T(8,128)(2,1)} %param.15), channel_id=1, source_target_pairs={{4,0},{8,4},{12,8},{5,1},{9,5},{13,9},{6,2},{10,6},{14,10},{7,3},{... | collective-permute-start | bytes 737288 | tf_op jit(solution)/shard_map/ppermute | solution.py:52
  227.1 23.9 %collective-permute-start.36 = (bf16[320,288]{0,1:T(8,128)(2,1)}, bf16[320,288]{0,1:T(8,128)(2,1)}, u32[]{:S(2)}, u32[]{:S(2)}) collective-permute-start(bf16[320,288]{0,1:T(8,128)(2,1)} %collective-permute-done.35), channel_id=1, source_target_pairs={{4,8},{8,12},{5,9},{9,13},{6,10},{10,14},{7,11},{11,15},{20,24},{2... | collective-permute-start | bytes 552968 | tf_op jit(solution)/shard_map/ppermute | solution.py:50
  228.5 24.0 %collective-permute-start.39 = (bf16[320,288]{0,1:T(8,128)(2,1)}, bf16[320,288]{0,1:T(8,128)(2,1)}, u32[]{:S(2)}, u32[]{:S(2)}) collective-permute-start(bf16[320,288]{0,1:T(8,128)(2,1)} %collective-permute-done.38), channel_id=1, source_target_pairs={{4,0},{8,4},{5,1},{9,5},{6,2},{10,6},{7,3},{11,7},{20,16},{24,20},... | collective-permute-start | bytes 552968 | tf_op jit(solution)/shard_map/ppermute | solution.py:52
  229.8 24.0 %collective-permute-start.18 = (bf16[320,384]{1,0:T(8,128)(2,1)}, bf16[320,384]{1,0:T(8,128)(2,1)}, u32[]{:S(2)}, u32[]{:S(2)}) collective-permute-start(bf16[320,384]{1,0:T(8,128)(2,1)} %collective-permute-done.17), channel_id=1, source_target_pairs={{4,8},{8,12},{5,9},{9,13},{6,10},{10,14},{7,11},{11,15},{20,24},{2... | collective-permute-start | bytes 737288 | tf_op jit(solution)/shard_map/ppermute | solution.py:50
  248.8 10.7 %collective-permute-start.31 = (bf16[256,672]{1,0:T(8,128)(2,1)S(1)}, bf16[256,672]{1,0:T(8,128)(2,1)S(1)}, u32[]{:S(2)}, u32[]{:S(2)}) collective-permute-start(bf16[256,672]{1,0:T(8,128)(2,1)S(1)} %get-tuple-element.28), channel_id=1, source_target_pairs={{0,1},{1,2},{2,3},{3,0},{4,5},{5,6},{6,7},{7,4},{8,9},{9,10},{10,1... | collective-permute-start | bytes 1032200 | tf_op jit(solution)/shard_map/ppermute | solution.py:74
  248.8 12.2 %collective-permute-start.32 = (bf16[256,672]{1,0:T(8,128)(2,1)S(1)}, bf16[256,672]{1,0:T(8,128)(2,1)S(1)}, u32[]{:S(2)}, u32[]{:S(2)}) collective-permute-start(bf16[256,672]{1,0:T(8,128)(2,1)S(1)} %get-tuple-element.30), channel_id=1, source_target_pairs={{0,2},{1,3},{2,0},{3,1},{4,6},{5,7},{6,4},{7,5},{8,10},{9,11},{10,... | collective-permute-start | bytes 1032200 | tf_op jit(solution)/shard_map/ppermute | solution.py:74
  251.1 17.3 %collective-permute-start.33 = (bf16[256,672]{1,0:T(8,128)(2,1)S(1)}, bf16[256,672]{1,0:T(8,128)(2,1)S(1)}, u32[]{:S(2)}, u32[]{:S(2)}) collective-permute-start(bf16[256,672]{1,0:T(8,128)(2,1)S(1)} %get-tuple-element.29), channel_id=1, source_target_pairs={{0,3},{1,0},{2,1},{3,2},{4,7},{5,4},{6,5},{7,6},{8,11},{9,8},{10,9... | collective-permute-start | bytes 1032200 | tf_op jit(solution)/shard_map/ppermute | solution.py:74
  252.5 17.7 %collective-permute-start.21 = (bf16[320,384]{1,0:T(8,128)(2,1)}, bf16[320,384]{1,0:T(8,128)(2,1)}, u32[]{:S(2)}, u32[]{:S(2)}) collective-permute-start(bf16[320,384]{1,0:T(8,128)(2,1)} %collective-permute-done.20), channel_id=1, source_target_pairs={{4,0},{8,4},{5,1},{9,5},{6,2},{10,6},{7,3},{11,7},{20,16},{24,20},... | collective-permute-start | bytes 737288 | tf_op jit(solution)/shard_map/ppermute | solution.py:52
  253.8 17.7 %collective-permute-start.37 = (bf16[320,288]{0,1:T(8,128)(2,1)}, bf16[320,288]{0,1:T(8,128)(2,1)S(1)}, u32[]{:S(2)}, u32[]{:S(2)}) collective-permute-start(bf16[320,288]{0,1:T(8,128)(2,1)} %collective-permute-done.36), channel_id=1, source_target_pairs={{8,12},{9,13},{10,14},{11,15},{24,28},{25,29},{26,30},{27,31}} | collective-permute-start | bytes 552968 | tf_op jit(solution)/shard_map/ppermute | solution.py:50
  259.5 15.3 %collective-permute-start.40 = (bf16[320,288]{0,1:T(8,128)(2,1)}, bf16[320,288]{0,1:T(8,128)(2,1)}, u32[]{:S(2)}, u32[]{:S(2)}) collective-permute-start(bf16[320,288]{0,1:T(8,128)(2,1)} %collective-permute-done.39), channel_id=1, source_target_pairs={{4,0},{5,1},{6,2},{7,3},{20,16},{21,17},{22,18},{23,19}} | collective-permute-start | bytes 552968 | tf_op jit(solution)/shard_map/ppermute | solution.py:52
  261.0 16.4 %collective-permute-start.19 = (bf16[320,384]{1,0:T(8,128)(2,1)}, bf16[320,384]{1,0:T(8,128)(2,1)}, u32[]{:S(2)}, u32[]{:S(2)}) collective-permute-start(bf16[320,384]{1,0:T(8,128)(2,1)} %collective-permute-done.18), channel_id=1, source_target_pairs={{8,12},{9,13},{10,14},{11,15},{24,28},{25,29},{26,30},{27,31}} | collective-permute-start | bytes 737288 | tf_op jit(solution)/shard_map/ppermute | solution.py:50
  268.6 12.2 %collective-permute-start.34 = (bf16[256,672]{1,0:T(8,128)(2,1)S(1)}, bf16[256,672]{1,0:T(8,128)(2,1)}, u32[]{:S(2)}, u32[]{:S(2)}) collective-permute-start(bf16[256,672]{1,0:T(8,128)(2,1)S(1)} %fusion.24), channel_id=1, source_target_pairs={{0,16},{16,0},{1,17},{17,1},{2,18},{18,2},{3,19},{19,3},{4,20},{20... | collective-permute-start | bytes 1032200 | tf_op jit(solution)/shard_map/ppermute | solution.py:91
  270.2 30.6 %collective-permute-start.22 = (bf16[320,384]{1,0:T(8,128)(2,1)}, bf16[320,384]{1,0:T(8,128)(2,1)}, u32[]{:S(2)}, u32[]{:S(2)}) collective-permute-start(bf16[320,384]{1,0:T(8,128)(2,1)} %collective-permute-done.21), channel_id=1, source_target_pairs={{4,0},{5,1},{6,2},{7,3},{20,16},{21,17},{22,18},{23,19}} | collective-permute-start | bytes 737288 | tf_op jit(solution)/shard_map/ppermute | solution.py:52
  285.1 21.1 %all-to-all-start = ((bf16[4,64,672]{2,1,0:T(8,128)(2,1)}), bf16[4,64,672]{2,1,0:T(8,128)(2,1)S(1)}, u32[]{:S(2)}, u32[]{:S(2)}) async-start(bf16[4,64,672]{2,1,0:T(8,128)(2,1)} %broadcast_select_fusion), calls=%async_computation | async-start | bytes 786432 | tf_op jit(solution)/shard_map/all_to_all | solution.py:168
  294.1 115.2 %reduce-scatter.2.cloned.1.call-start = ((), (), s32[]{:S(2)}) async-start(), calls=%async_computation.2 | async-start | bytes 4096000 | tf_op jit(solution)/shard_map/reduce_scatter | solution.py:202
  310.8 6.3 %collective-permute-start.41 = (bf16[64,1280]{1,0:T(8,128)(2,1)}, bf16[64,1280]{1,0:T(8,128)(2,1)}, u32[]{:S(2)}, u32[]{:S(2)}) collective-permute-start(bf16[64,1280]{1,0:T(8,128)(2,1)} %get-tuple-element.40), channel_id=1, source_target_pairs={{0,1},{1,2},{2,3},{3,0},{4,5},{5,6},{6,7},{7,4},{8,9},{9,10},{10,1... | collective-permute-start | bytes 491528 | tf_op jit(solution)/shard_map/ppermute | solution.py:74
  310.8 8.4 %collective-permute-start.42 = (bf16[64,1280]{1,0:T(8,128)(2,1)}, bf16[64,1280]{1,0:T(8,128)(2,1)}, u32[]{:S(2)}, u32[]{:S(2)}) collective-permute-start(bf16[64,1280]{1,0:T(8,128)(2,1)} %get-tuple-element.42), channel_id=1, source_target_pairs={{0,2},{1,3},{2,0},{3,1},{4,6},{5,7},{6,4},{7,5},{8,10},{9,11},{10,... | collective-permute-start | bytes 491528 | tf_op jit(solution)/shard_map/ppermute | solution.py:74
  310.8 8.4 %collective-permute-start.43 = (bf16[64,1280]{1,0:T(8,128)(2,1)}, bf16[64,1280]{1,0:T(8,128)(2,1)}, u32[]{:S(2)}, u32[]{:S(2)}) collective-permute-start(bf16[64,1280]{1,0:T(8,128)(2,1)} %get-tuple-element.41), channel_id=1, source_target_pairs={{0,3},{1,0},{2,1},{3,2},{4,7},{5,4},{6,5},{7,6},{8,11},{9,8},{10,9... | collective-permute-start | bytes 491528 | tf_op jit(solution)/shard_map/ppermute | solution.py:74
  314.1 10.8 %collective-permute-start.47 = (bf16[160,672]{1,0:T(8,128)(2,1)S(1)}, bf16[160,672]{1,0:T(8,128)(2,1)S(1)}, u32[]{:S(2)}, u32[]{:S(2)}) collective-permute-start(bf16[160,672]{1,0:T(8,128)(2,1)S(1)} %get-tuple-element.33), channel_id=1, source_target_pairs={{0,4},{4,8},{8,12},{12,0},{1,5},{5,9},{9,13},{13,1},{2,6},{6,10},{... | collective-permute-start | bytes 645128 | tf_op jit(solution)/shard_map/ppermute | solution.py:74
  314.1 20.3 %collective-permute-start.48 = (bf16[160,672]{1,0:T(8,128)(2,1)S(1)}, bf16[160,672]{1,0:T(8,128)(2,1)S(1)}, u32[]{:S(2)}, u32[]{:S(2)}) collective-permute-start(bf16[160,672]{1,0:T(8,128)(2,1)S(1)} %get-tuple-element.35), channel_id=1, source_target_pairs={{0,8},{4,12},{8,0},{12,4},{1,9},{5,13},{9,1},{13,5},{2,10},{6,14},... | collective-permute-start | bytes 645128 | tf_op jit(solution)/shard_map/ppermute | solution.py:74
  317.0 17.5 %collective-permute-start.49 = (bf16[160,672]{1,0:T(8,128)(2,1)S(1)}, bf16[160,672]{1,0:T(8,128)(2,1)S(1)}, u32[]{:S(2)}, u32[]{:S(2)}) collective-permute-start(bf16[160,672]{1,0:T(8,128)(2,1)S(1)} %get-tuple-element.34), channel_id=1, source_target_pairs={{0,12},{4,0},{8,4},{12,8},{1,13},{5,1},{9,5},{13,9},{2,14},{6,2},{... | collective-permute-start | bytes 645128 | tf_op jit(solution)/shard_map/ppermute | solution.py:74
  320.7 14.7 %collective-permute-start.44 = (bf16[64,1280]{1,0:T(8,128)(2,1)S(1)}, bf16[64,1280]{1,0:T(8,128)(2,1)S(1)}, u32[]{:S(2)}, u32[]{:S(2)}) collective-permute-start(bf16[64,1280]{1,0:T(8,128)(2,1)S(1)} %multiply_convert_fusion.4), channel_id=1, source_target_pairs={{0,3},{1,0},{2,1},{3,2},{4,7},{5,4},{6,5},{7,6},{8,11},{9,8},{10,9... | collective-permute-start | bytes 491528 | tf_op jit(solution)/shard_map/ppermute | solution.py:84
  321.4 14.0 %collective-permute-start.45 = (bf16[64,1280]{1,0:T(8,128)(2,1)S(1)}, bf16[64,1280]{1,0:T(8,128)(2,1)S(1)}, u32[]{:S(2)}, u32[]{:S(2)}) collective-permute-start(bf16[64,1280]{1,0:T(8,128)(2,1)S(1)} %multiply_convert_fusion.4), channel_id=1, source_target_pairs={{0,2},{1,3},{2,0},{3,1},{4,6},{5,7},{6,4},{7,5},{8,10},{9,11},{10,... | collective-permute-start | bytes 491528 | tf_op jit(solution)/shard_map/ppermute | solution.py:84
  324.9 10.6 %collective-permute-start.46 = (bf16[64,1280]{1,0:T(8,128)(2,1)S(1)}, bf16[64,1280]{1,0:T(8,128)(2,1)S(1)}, u32[]{:S(2)}, u32[]{:S(2)}) collective-permute-start(bf16[64,1280]{1,0:T(8,128)(2,1)S(1)} %multiply_convert_fusion.4), channel_id=1, source_target_pairs={{0,1},{1,2},{2,3},{3,0},{4,5},{5,6},{6,7},{7,4},{8,9},{9,10},{10,1... | collective-permute-start | bytes 491528 | tf_op jit(solution)/shard_map/ppermute | solution.py:84
  345.0 67.1 %copy-start.9 = (f32[160,672]{1,0:T(8,128)S(1)}, f32[160,672]{1,0:T(8,128)}, u32[]{:S(2)}) copy-start(f32[160,672]{1,0:T(8,128)} %fusion.63) | copy-start | bytes 1290244
  409.3 12.4 %copy-start.4 = (bf16[2,320,640]{2,1,0:T(8,128)(2,1)S(1)}, bf16[2,320,640]{2,1,0:T(8,128)(2,1)}, u32[]{:S(2)}) copy-start(bf16[2,320,640]{2,1,0:T(8,128)(2,1)} %reduce-scatter.2.cloned.1.call-done) | copy-start | bytes 2457604
  410.5 11.1 %collective-permute-start.50 = (bf16[2,160,640]{2,1,0:T(8,128)(2,1)S(1)}, bf16[2,160,640]{2,1,0:T(8,128)(2,1)S(1)}, u32[]{:S(2)}, u32[]{:S(2)}) collective-permute-start(bf16[2,160,640]{2,1,0:T(8,128)(2,1)S(1)} %fusion.64), channel_id=1, source_target_pairs={{0,16},{16,0},{1,17},{17,1},{2,18},{18,2},{3,19},{19,3},{4,20},{20... | collective-permute-start | bytes 1228808 | tf_op jit(solution)/shard_map/ppermute | solution.py:91
  (22 other events, 58.9 us)
Sparse Core Ops, SparseCore 0:
  345.1 64.1 reduce-scatter.1

commit v5 on v4

--- a/solution.py
+++ b/solution.py
@@ -125,9 +125,9 @@
     own_student = own_units(student_mlp, group, units)
     w_mlp, own_dino, own_siglip = gathered_rows(own_student, 1, (own_dino, own_siglip))
     siglip_full, = gathered_rows(own_siglip, 1)
-    dino_full, own_hd, own_hs = gathered_rows(own_dino, 1, (dino_head, siglip_head))
-    w_dino, = gathered_rows(own_hd, 0)
-    w_sig, = gathered_rows(own_hs, 0)
+    own_heads = jnp.concatenate([dino_head, siglip_head], axis=1)
+    dino_full, own_heads = gathered_rows(own_dino, 1, (own_heads,))
+    w_heads, = gathered_rows(own_heads, 0)
 
     def once(hidden, low):
         place = lax.broadcasted_iota(jnp.int32, hidden.shape, 1)
@@ -178,16 +178,14 @@
     out = out.astype(f32) + across(out).astype(f32)
     own_mixed = lax.dynamic_slice_in_dim(flat, column * share, share, 0) + out
     feat = joined_pieces(norm_rows(own_mixed).astype(bf16), "tp").reshape(rows, width)
-    pred_d = jnp.dot(feat, w_dino, preferred_element_type=f32)
-    pred_s = jnp.dot(feat, w_sig, preferred_element_type=f32)
-    diff_d = ((pred_d - target[:, :cols_d]) * scale).astype(bf16)
-    diff_s = ((pred_s - target[:, cols_d:]) * scale).astype(bf16)
-
-    dfeat = times_transposed(diff_d, w_dino) + times_transposed(diff_s, w_sig)
+    pred = jnp.dot(feat, w_heads, preferred_element_type=f32)
+    diff = ((pred - target) * scale).astype(bf16)
+
+    dfeat = times_transposed(diff, w_heads)
     dfeat = summed_piece(dfeat.astype(bf16).reshape(count_tp, share, width), "tp")
     dmixed = joined_pieces(norm_back(own_mixed, dfeat).astype(bf16), "tp").reshape(rows, width)
     own_feat = lax.dynamic_slice_in_dim(feat, group * half, half, 1)
-    grad_heads = over_rows(own_feat, jnp.concatenate([diff_d, diff_s], axis=1)).astype(bf16)
+    grad_heads = over_rows(own_feat, diff).astype(bf16)
     sum_heads = summed_piece(grad_heads.reshape(count_dp, block, cols_d + cols_s), "dp")
     grad_down = over_rows(dmixed, hidden).astype(bf16)
     dhidden = jnp.dot(dmixed, w_mlp[1], preferred_element_type=f32)

time: 432 us -> 423 us (0.979)
  waiting for transfers between devices: 224 us -> 249 us
  starting transfers between devices: 91.9 us -> 69 us
  local copies, waits for them, and re-layouts: 52.9 us -> 47 us
    ppermute x12, waiting for transfers between devices: 23 us -> 38.9 us  [summed_piece(): total = total + lax.ppermute(piece, axis, pairs).astype(jnp.float32)]
    ppermute x15 -> x12, starting transfers between devices: 41.5 us -> 27.4 us  [gathered_rows(): lax.ppermute(up[-1], 'dp', [(i, i + 1) for i in range(step - 1, count - 1)])]
    ppermute x15 -> x12, waiting for transfers between devices: 96.8 us -> 105 us  [gathered_rows(): lax.ppermute(down[-1], 'dp', [(i, i - 1) for i in range(1, count - step +...]
    ppermute x12, starting transfers between devices: 13.3 us -> 8 us  [summed_piece(): total = total + lax.ppermute(piece, axis, pairs).astype(jnp.float32)]
    unnamed x100 -> x93, local copies, waits for them, and re-layouts: 37.3 us -> 33 us
    ppermute x15 -> x12, starting transfers between devices: 19.3 us -> 15.4 us  [gathered_rows(): lax.ppermute(down[-1], 'dp', [(i, i - 1) for i in range(1, count - step +...]
    ppermute x15 -> x12, waiting for transfers between devices: 26.7 us -> 30.4 us  [gathered_rows(): lax.ppermute(up[-1], 'dp', [(i, i + 1) for i in range(step - 1, count - 1)])]
    dot_general x5 -> x4, matrix products: 8.82 us -> 9.37 us  [times_transposed(): lax.dot_general(left, right, (((1,), (1,)), ((), ())), preferred_element_...]
  transfers between devices with their start and end apart: 53 -> 47, of which waited for: 24 -> 24; matrix products, arithmetic and copies ran while one was open for 16% -> 14% of each run, Pallas kernels for 0% -> 0%
where the time goes in v5:
time: 423 us; the launch traced here: 421 us
  waiting for transfers between devices  249 us (59%)
  starting transfers between devices  69 us (16%)
  local copies, waits for them, and re-layouts  47 us (11%)
  other arithmetic  20.9 us (5%)
  matrix products  20.5 us (5%)
  between operations  15.1 us (4%)
    ppermute x12, waiting for transfers between devices, gathered_rows(): lax.ppermute(down[-1], 'dp', [(i, i - 1) for i in range(1, count - step +...  105 us
    reduce_scatter x1, waiting for transfers between devices, body(): sum_mlp = lax.psum_scatter(grad_mlp, 'dp', scatter_dimension=1, tiled=True)  62.4 us
    ppermute x12, waiting for transfers between devices, summed_piece(): total = total + lax.ppermute(piece, axis, pairs).astype(jnp.float32)  38.9 us
    unnamed x93, local copies, waits for them, and re-layouts  33 us
    ppermute x12, waiting for transfers between devices, gathered_rows(): lax.ppermute(up[-1], 'dp', [(i, i + 1) for i in range(step - 1, count - 1)])  30.4 us
    ppermute x12, starting transfers between devices, gathered_rows(): lax.ppermute(up[-1], 'dp', [(i, i + 1) for i in range(step - 1, count - 1)])  27.4 us
    ppermute x12, starting transfers between devices, gathered_rows(): lax.ppermute(down[-1], 'dp', [(i, i - 1) for i in range(1, count - step +...  15.4 us
    all_to_all x1, starting transfers between devices, body(): lax.all_to_all(arranged, 'dp', split_axis=0, concat_axis=1, tiled=True)  12.2 us
  transfers between devices with their start and end apart: 47, of which 24 were waited for; matrix products, arithmetic and copies ran while one was open for 14% of the time, Pallas kernels for 0%

profile of v5, /device:TPU:0, one launch (start us, length us, event | category | flops | bytes accessed | tf_op | source)
XLA Modules:
  0.0 421.2 jit_solution(17521932117278425228)
XLA Ops:
  7.2 1.6 slice_select_fusion.1
  8.8 6.0 %collective-permute-start = (bf16[2,320,640]{2,1,0:T(8,128)(2,1)S(1)}, bf16[2,320,640]{2,1,0:T(8,128)(2,1)}, u32[]{:S(2)}, u32[]{:S(2)}) collective-permute-start(bf16[2,320,640]{2,1,0:T(8,128)(2,1)S(1)} %slice_select_fusion.1), channel_id=1, source_target_pairs={{0,4},{4,8},{8,12},{1,5},{5,9},{9,13},{2,6},{6,10},{10,14},{3,7},{... | collective-permute-start | bytes 2457608 | tf_op jit(solution)/shard_map/ppermute | solution.py:50
  18.3 13.0 %collective-permute-done = bf16[2,320,640]{2,1,0:T(8,128)(2,1)} collective-permute-done((bf16[2,320,640]{2,1,0:T(8,128)(2,1)S(1)}, bf16[2,320,640]{2,1,0:T(8,128)(2,1)}, u32[]{:S(2)}, u32[]{:S(2)}) %collective-permute-start) | collective-permute-done | bytes 819232 | tf_op jit(solution)/shard_map/ppermute | solution.py:50
  31.4 1.6 collective-permute-start.1
  32.9 3.6 collective-permute-done.2
  38.3 1.7 slice_select_fusion
  41.2 16.5 %collective-permute-done.3 = bf16[2,320,640]{2,1,0:T(8,128)(2,1)} collective-permute-done((bf16[2,320,640]{2,1,0:T(8,128)(2,1)}, bf16[2,320,640]{2,1,0:T(8,128)(2,1)}, u32[]{:S(2)}, u32[]{:S(2)}) %collective-permute-start.3) | collective-permute-done | bytes 819232 | tf_op jit(solution)/shard_map/ppermute | solution.py:52
  61.3 1.4 constant_dynamic-update-slice_fusion.5
  66.8 13.2 %collective-permute-done.5 = bf16[2,320,640]{2,1,0:T(8,128)(2,1)S(1)} collective-permute-done((bf16[2,320,640]{2,1,0:T(8,128)(2,1)}, bf16[2,320,640]{2,1,0:T(8,128)(2,1)S(1)}, u32[]{:S(2)}, u32[]{:S(2)}) %collective-permute-start.5) | collective-permute-done | bytes 819232 | tf_op jit(solution)/shard_map/ppermute | solution.py:52
  80.1 2.8 fusion.32
  85.2 1.5 collective-permute-start.7
  87.8 2.4 collective-permute-start.25
  91.5 4.0 collective-permute-done.7
  96.8 1.6 collective-permute-start.9
  100.2 2.6 collective-permute-start.13
  104.1 2.3 collective-permute-done.25
  106.4 1.5 collective-permute-start.26
  107.9 3.8 collective-permute-done.28
  116.2 1.6 collective-permute-done.10
  117.8 13.3 %collective-permute-done.13 = bf16[3,384,512]{2,1,0:T(8,128)(2,1)} collective-permute-done((bf16[3,384,512]{2,1,0:T(8,128)(2,1)S(1)}, bf16[3,384,512]{2,1,0:T(8,128)(2,1)}, u32[]{:S(2)}, u32[]{:S(2)}) %collective-permute-start.13) | collective-permute-done | bytes 1179680 | tf_op jit(solution)/shard_map/ppermute | solution.py:50
  131.1 5.9 %collective-permute-done.15 = bf16[3,384,512]{2,1,0:T(8,128)(2,1)} collective-permute-done((bf16[3,384,512]{2,1,0:T(8,128)(2,1)S(1)}, bf16[3,384,512]{2,1,0:T(8,128)(2,1)}, u32[]{:S(2)}, u32[]{:S(2)}) %collective-permute-start.15) | collective-permute-done | bytes 1179680 | tf_op jit(solution)/shard_map/ppermute | solution.py:52
  137.0 1.7 collective-permute-start.14
  140.0 12.0 %collective-permute-done.29 = bf16[2,288,564]{2,1,0:T(8,128)(2,1)} collective-permute-done((bf16[2,288,564]{2,1,0:T(8,128)(2,1)}, bf16[2,288,564]{2,1,0:T(8,128)(2,1)}, u32[]{:S(2)}, u32[]{:S(2)}) %collective-permute-start.29) | collective-permute-done | bytes 649760 | tf_op jit(solution)/shard_map/ppermute | solution.py:52
  155.4 23.5 %collective-permute-done.16 = bf16[3,384,512]{2,1,0:T(8,128)(2,1)} collective-permute-done((bf16[3,384,512]{2,1,0:T(8,128)(2,1)}, bf16[3,384,512]{2,1,0:T(8,128)(2,1)}, u32[]{:S(2)}, u32[]{:S(2)}) %collective-permute-start.16) | collective-permute-done | bytes 1179680 | tf_op jit(solution)/shard_map/ppermute | solution.py:52
  178.9 1.7 collective-permute-start.23
  185.6 7.4 %collective-permute-done.30 = bf16[2,288,564]{2,1,0:T(8,128)(2,1)S(1)} collective-permute-done((bf16[2,288,564]{2,1,0:T(8,128)(2,1)}, bf16[2,288,564]{2,1,0:T(8,128)(2,1)S(1)}, u32[]{:S(2)}, u32[]{:S(2)}) %collective-permute-start.30) | collective-permute-done | bytes 649760 | tf_op jit(solution)/shard_map/ppermute | solution.py:52
  194.4 6.4 %collective-permute-start.17 = (bf16[320,672]{1,0:T(8,128)(2,1)S(1)}, bf16[320,672]{1,0:T(8,128)(2,1)}, u32[]{:S(2)}, u32[]{:S(2)}) collective-permute-start(bf16[320,672]{1,0:T(8,128)(2,1)S(1)} %pad_maximum_fusion.3), channel_id=1, source_target_pairs={{0,4},{4,8},{8,12},{1,5},{5,9},{9,13},{2,6},{6,10},{10,14},{3,7},{... | collective-permute-start | bytes 1290248 | tf_op jit(solution)/shard_map/ppermute | solution.py:50
  200.8 4.0 convolution_convert_fusion.3
  207.1 1.8 collective-permute-done.17
  208.9 1.5 collective-permute-start.18
  210.4 1.3 constant_dynamic-update-slice_fusion.20
  211.7 1.3 constant_dynamic-update-slice_fusion.19
  213.1 1.3 constant_dynamic-update-slice_fusion.18
  214.5 1.3 constant_dynamic-update-slice_fusion.16
  215.9 1.3 constant_dynamic-update-slice_fusion.15
  217.2 7.0 %collective-permute-done.24 = bf16[3,384,512]{2,1,0:T(8,128)(2,1)} collective-permute-done((bf16[3,384,512]{2,1,0:T(8,128)(2,1)}, bf16[3,384,512]{2,1,0:T(8,128)(2,1)}, u32[]{:S(2)}, u32[]{:S(2)}) %collective-permute-start.24) | collective-permute-done | bytes 1179680 | tf_op jit(solution)/shard_map/ppermute | solution.py:52
  224.2 1.3 constant_dynamic-update-slice_fusion.14
  225.6 3.3 copy-done.13
  229.4 3.9 convolution_convert_fusion.4
  233.4 1.4 fusion.118
  235.4 1.7 collective-permute-start.32
  237.3 1.3 collective-permute-start.21
  239.3 4.4 %collective-permute-done.33 = bf16[256,672]{1,0:T(8,128)(2,1)S(1)} collective-permute-done((bf16[256,672]{1,0:T(8,128)(2,1)S(1)}, bf16[256,672]{1,0:T(8,128)(2,1)S(1)}, u32[]{:S(2)}, u32[]{:S(2)}) %collective-permute-start.33) | collective-permute-done | bytes 344096 | tf_op jit(solution)/shard_map/ppermute | solution.py:74
  243.7 11.7 %collective-permute-done.32 = bf16[256,672]{1,0:T(8,128)(2,1)S(1)} collective-permute-done((bf16[256,672]{1,0:T(8,128)(2,1)S(1)}, bf16[256,672]{1,0:T(8,128)(2,1)S(1)}, u32[]{:S(2)}, u32[]{:S(2)}) %collective-permute-start.32) | collective-permute-done | bytes 344096 | tf_op jit(solution)/shard_map/ppermute | solution.py:74
  255.5 1.6 collective-permute-start.34
  257.2 12.3 %collective-permute-done.21 = bf16[320,672]{1,0:T(8,128)(2,1)S(1)} collective-permute-done((bf16[320,672]{1,0:T(8,128)(2,1)}, bf16[320,672]{1,0:T(8,128)(2,1)S(1)}, u32[]{:S(2)}, u32[]{:S(2)}) %collective-permute-start.21) | collective-permute-done | bytes 430112 | tf_op jit(solution)/shard_map/ppermute | solution.py:52
  271.6 1.8 constant_dynamic-update-slice_fusion.12
  275.1 12.2 %all-to-all-start = ((bf16[4,64,672]{2,1,0:T(8,128)(2,1)}), bf16[4,64,672]{2,1,0:T(8,128)(2,1)S(1)}, u32[]{:S(2)}, u32[]{:S(2)}) async-start(bf16[4,64,672]{2,1,0:T(8,128)(2,1)} %broadcast_select_fusion), calls=%async_computation | async-start | bytes 786432 | tf_op jit(solution)/shard_map/all_to_all | solution.py:168
  287.3 1.9 constant_dynamic-update-slice_fusion.11
  290.0 1.9 constant_dynamic-update-slice_fusion.9
  292.7 1.8 constant_dynamic-update-slice_fusion.7
  294.6 2.1 all-to-all-done
  297.0 2.5 fusion.21
  301.1 1.7 collective-permute-start.36
  304.5 1.5 collective-permute-start.43
  307.0 4.6 %collective-permute-done.36 = bf16[64,1280]{1,0:T(8,128)(2,1)} collective-permute-done((bf16[64,1280]{1,0:T(8,128)(2,1)}, bf16[64,1280]{1,0:T(8,128)(2,1)}, u32[]{:S(2)}, u32[]{:S(2)}) %collective-permute-start.36) | collective-permute-done | bytes 163872 | tf_op jit(solution)/shard_map/ppermute | solution.py:74
  311.6 1.3 fusion.115
  313.8 14.1 %collective-permute-done.42 = bf16[160,672]{1,0:T(8,128)(2,1)S(1)} collective-permute-done((bf16[160,672]{1,0:T(8,128)(2,1)S(1)}, bf16[160,672]{1,0:T(8,128)(2,1)S(1)}, u32[]{:S(2)}, u32[]{:S(2)}) %collective-permute-start.42) | collective-permute-done | bytes 215072 | tf_op jit(solution)/shard_map/ppermute | solution.py:74
  330.5 4.1 convolution_convert_fusion.1
  334.5 1.6 copy.20
  336.1 2.0 pad_maximum_fusion
  338.1 62.4 %reduce-scatter.2.cloned.1.call-done = bf16[2,320,640]{2,1,0:T(8,128)(2,1)} async-done(((bf16[2,1280,640]{2,1,0:T(8,128)(2,1)}), bf16[2,320,640]{2,1,0:T(8,128)(2,1)}) %reduce-scatter.2.cloned.1.call-update) | async-done | bytes 819216 | tf_op jit(solution)/shard_map/reduce_scatter | solution.py:200
  401.8 1.5 collective-permute-start.44
  404.7 8.2 %collective-permute-done.44 = bf16[2,160,640]{2,1,0:T(8,128)(2,1)S(1)} collective-permute-done((bf16[2,160,640]{2,1,0:T(8,128)(2,1)S(1)}, bf16[2,160,640]{2,1,0:T(8,128)(2,1)S(1)}, u32[]{:S(2)}, u32[]{:S(2)}) %collective-permute-start.44) | collective-permute-done | bytes 409632 | tf_op jit(solution)/shard_map/ppermute | solution.py:91
  (206 shorter events, 60.6 us)
Async XLA Ops:
  7.2 8.9 %copy-start.3 = (bf16[1,256,1280]{2,1,0:T(8,128)(2,1)S(1)}, bf16[1,256,1280]{2,1,0:T(8,128)(2,1)}, u32[]{:S(2)}) copy-start(bf16[1,256,1280]{2,1,0:T(8,128)(2,1)} %param.11) | copy-start | bytes 1966084
  7.2 9.4 %copy-start.1 = (bf16[4,64,1152]{2,1,0:T(8,128)(2,1)S(1)}, bf16[4,64,1152]{2,1,0:T(8,128)(2,1)}, u32[]{:S(2)}) copy-start(bf16[4,64,1152]{2,1,0:T(8,128)(2,1)} %param.10) | copy-start | bytes 1769476
  8.8 8.3 %copy-start.28 = (s32[4]{0:T(128)S(1)}, s32[4]{0:T(128)}, u32[]{:S(2)}) copy-start(s32[4]{0:T(128)} %param.17) | copy-start | bytes 52
  8.8 8.3 %copy-start = (bf16[4,64,1536]{2,1,0:T(8,128)(2,1)S(1)}, bf16[4,64,1536]{2,1,0:T(8,128)(2,1)}, u32[]{:S(2)}) copy-start(bf16[4,64,1536]{2,1,0:T(8,128)(2,1)} %param.9) | copy-start | bytes 2359300
  8.8 8.5 %copy-start.9 = (bf16[2,288,1076]{2,1,0:T(8,128)(2,1)S(1)}, bf16[2,288,1076]{2,1,0:T(8,128)(2,1)}, u32[]{:S(2)}) copy-start(bf16[2,288,1076]{2,1,0:T(8,128)(2,1)} %param.13) | copy-start | bytes 3718660
  8.8 22.6 %collective-permute-start = (bf16[2,320,640]{2,1,0:T(8,128)(2,1)S(1)}, bf16[2,320,640]{2,1,0:T(8,128)(2,1)}, u32[]{:S(2)}, u32[]{:S(2)}) collective-permute-start(bf16[2,320,640]{2,1,0:T(8,128)(2,1)S(1)} %slice_select_fusion.1), channel_id=1, source_target_pairs={{0,4},{4,8},{8,12},{1,5},{5,9},{9,13},{2,6},{6,10},{10,14},{3,7},{... | collective-permute-start | bytes 2457608 | tf_op jit(solution)/shard_map/ppermute | solution.py:50
  14.8 21.7 %collective-permute-start.2 = (bf16[2,320,640]{2,1,0:T(8,128)(2,1)S(1)}, bf16[2,320,640]{2,1,0:T(8,128)(2,1)}, u32[]{:S(2)}, u32[]{:S(2)}) collective-permute-start(bf16[2,320,640]{2,1,0:T(8,128)(2,1)S(1)} %slice_select_fusion.1), channel_id=1, source_target_pairs={{4,0},{8,4},{12,8},{5,1},{9,5},{13,9},{6,2},{10,6},{14,10},{7,3},{... | collective-permute-start | bytes 2457608 | tf_op jit(solution)/shard_map/ppermute | solution.py:52
  16.6 63.5 %copy-start.25 = (f32[256]{0:T(256)}, f32[256]{0:T(256)S(1)}, u32[]{:S(2)}) copy-start(f32[256]{0:T(256)S(1)} %add_rsqrt_fusion.2) | copy-start | bytes 3076
  31.4 9.8 %collective-permute-start.1 = (bf16[2,320,640]{2,1,0:T(8,128)(2,1)}, bf16[2,320,640]{2,1,0:T(8,128)(2,1)}, u32[]{:S(2)}, u32[]{:S(2)}) collective-permute-start(bf16[2,320,640]{2,1,0:T(8,128)(2,1)} %collective-permute-done), channel_id=1, source_target_pairs={{4,8},{8,12},{5,9},{9,13},{6,10},{10,14},{7,11},{11,15},{20,24},{2... | collective-permute-start | bytes 2457608 | tf_op jit(solution)/shard_map/ppermute | solution.py:50
  36.5 21.1 %collective-permute-start.3 = (bf16[2,320,640]{2,1,0:T(8,128)(2,1)}, bf16[2,320,640]{2,1,0:T(8,128)(2,1)}, u32[]{:S(2)}, u32[]{:S(2)}) collective-permute-start(bf16[2,320,640]{2,1,0:T(8,128)(2,1)} %collective-permute-done.2), channel_id=1, source_target_pairs={{4,0},{8,4},{5,1},{9,5},{6,2},{10,6},{7,3},{11,7},{20,16},{24,20},... | collective-permute-start | bytes 2457608 | tf_op jit(solution)/shard_map/ppermute | solution.py:52
  57.6 3.5 collective-permute-start.4
  59.9 20.1 %collective-permute-start.5 = (bf16[2,320,640]{2,1,0:T(8,128)(2,1)}, bf16[2,320,640]{2,1,0:T(8,128)(2,1)S(1)}, u32[]{:S(2)}, u32[]{:S(2)}) collective-permute-start(bf16[2,320,640]{2,1,0:T(8,128)(2,1)} %collective-permute-done.3), channel_id=1, source_target_pairs={{4,0},{5,1},{6,2},{7,3},{20,16},{21,17},{22,18},{23,19}} | collective-permute-start | bytes 2457608 | tf_op jit(solution)/shard_map/ppermute | solution.py:52
  61.3 2.7 copy-start.2
  80.1 2.8 copy-start.12
  85.2 6.3 %collective-permute-start.8 = (bf16[64,1280]{1,0:T(8,128)(2,1)}, bf16[64,1280]{1,0:T(8,128)(2,1)S(1)}, u32[]{:S(2)}, u32[]{:S(2)}) collective-permute-start(bf16[64,1280]{1,0:T(8,128)(2,1)} %get-tuple-element.42), channel_id=1, source_target_pairs={{0,3},{1,0},{2,1},{3,2},{4,7},{5,4},{6,5},{7,6},{8,11},{9,8},{10,9... | collective-permute-start | bytes 491528 | tf_op jit(solution)/shard_map/ppermute | solution.py:74
  85.2 10.3 %collective-permute-start.7 = (bf16[64,1280]{1,0:T(8,128)(2,1)}, bf16[64,1280]{1,0:T(8,128)(2,1)}, u32[]{:S(2)}, u32[]{:S(2)}) collective-permute-start(bf16[64,1280]{1,0:T(8,128)(2,1)} %get-tuple-element.43), channel_id=1, source_target_pairs={{0,2},{1,3},{2,0},{3,1},{4,6},{5,7},{6,4},{7,5},{8,10},{9,11},{10,... | collective-permute-start | bytes 491528 | tf_op jit(solution)/shard_map/ppermute | solution.py:74
  86.7 8.9 %collective-permute-start.6 = (bf16[64,1280]{1,0:T(8,128)(2,1)S(1)}, bf16[64,1280]{1,0:T(8,128)(2,1)}, u32[]{:S(2)}, u32[]{:S(2)}) collective-permute-start(bf16[64,1280]{1,0:T(8,128)(2,1)S(1)} %get-tuple-element.41), channel_id=1, source_target_pairs={{0,1},{1,2},{2,3},{3,0},{4,5},{5,6},{6,7},{7,4},{8,9},{9,10},{10,1... | collective-permute-start | bytes 491528 | tf_op jit(solution)/shard_map/ppermute | solution.py:74
  87.8 18.7 %collective-permute-start.25 = (bf16[2,288,564]{2,1,0:T(8,128)(2,1)}, bf16[2,288,564]{2,1,0:T(8,128)(2,1)}, u32[]{:S(2)}, u32[]{:S(2)}) collective-permute-start(bf16[2,288,564]{2,1,0:T(8,128)(2,1)} %slice_select_fusion.2), channel_id=1, source_target_pairs={{0,4},{4,8},{8,12},{1,5},{5,9},{9,13},{2,6},{6,10},{10,14},{3,7},{... | collective-permute-start | bytes 1949192 | tf_op jit(solution)/shard_map/ppermute | solution.py:50
  90.2 21.5 %collective-permute-start.28 = (bf16[2,288,564]{2,1,0:T(8,128)(2,1)}, bf16[2,288,564]{2,1,0:T(8,128)(2,1)}, u32[]{:S(2)}, u32[]{:S(2)}) collective-permute-start(bf16[2,288,564]{2,1,0:T(8,128)(2,1)} %slice_select_fusion.2), channel_id=1, source_target_pairs={{4,0},{8,4},{12,8},{5,1},{9,5},{13,9},{6,2},{10,6},{14,10},{7,3},{... | collective-permute-start | bytes 1949192 | tf_op jit(solution)/shard_map/ppermute | solution.py:52
  96.8 16.3 %collective-permute-start.9 = (bf16[64,1280]{1,0:T(8,128)(2,1)S(1)}, bf16[64,1280]{1,0:T(8,128)(2,1)S(1)}, u32[]{:S(2)}, u32[]{:S(2)}) collective-permute-start(bf16[64,1280]{1,0:T(8,128)(2,1)S(1)} %fusion.72), channel_id=1, source_target_pairs={{0,16},{16,0},{1,17},{17,1},{2,18},{18,2},{3,19},{19,3},{4,20},{20... | collective-permute-start | bytes 491528 | tf_op jit(solution)/shard_map/ppermute | solution.py:91
  99.5 16.7 %copy-start.23 = (bf16[320,384]{1,0:T(8,128)(2,1)S(1)}, bf16[320,384]{1,0:T(8,128)(2,1)}, u32[]{:S(2)}) copy-start(bf16[320,384]{1,0:T(8,128)(2,1)} %param.15) | copy-start | bytes 737284
  100.2 31.0 %collective-permute-start.13 = (bf16[3,384,512]{2,1,0:T(8,128)(2,1)S(1)}, bf16[3,384,512]{2,1,0:T(8,128)(2,1)}, u32[]{:S(2)}, u32[]{:S(2)}) collective-permute-start(bf16[3,384,512]{2,1,0:T(8,128)(2,1)S(1)} %slice_select_fusion), channel_id=1, source_target_pairs={{0,4},{4,8},{8,12},{1,5},{5,9},{9,13},{2,6},{6,10},{10,14},{3,7},{... | collective-permute-start | bytes 3538952 | tf_op jit(solution)/shard_map/ppermute | solution.py:50
  102.8 34.2 %collective-permute-start.15 = (bf16[3,384,512]{2,1,0:T(8,128)(2,1)S(1)}, bf16[3,384,512]{2,1,0:T(8,128)(2,1)}, u32[]{:S(2)}, u32[]{:S(2)}) collective-permute-start(bf16[3,384,512]{2,1,0:T(8,128)(2,1)S(1)} %slice_select_fusion), channel_id=1, source_target_pairs={{4,0},{8,4},{12,8},{5,1},{9,5},{13,9},{6,2},{10,6},{14,10},{7,3},{... | collective-permute-start | bytes 3538952 | tf_op jit(solution)/shard_map/ppermute | solution.py:52
  106.4 32.3 %collective-permute-start.26 = (bf16[2,288,564]{2,1,0:T(8,128)(2,1)}, bf16[2,288,564]{2,1,0:T(8,128)(2,1)}, u32[]{:S(2)}, u32[]{:S(2)}) collective-permute-start(bf16[2,288,564]{2,1,0:T(8,128)(2,1)} %collective-permute-done.25), channel_id=1, source_target_pairs={{4,8},{8,12},{5,9},{9,13},{6,10},{10,14},{7,11},{11,15},{20,24},{2... | collective-permute-start | bytes 1949192 | tf_op jit(solution)/shard_map/ppermute | solution.py:50
  111.7 40.3 %collective-permute-start.29 = (bf16[2,288,564]{2,1,0:T(8,128)(2,1)}, bf16[2,288,564]{2,1,0:T(8,128)(2,1)}, u32[]{:S(2)}, u32[]{:S(2)}) collective-permute-start(bf16[2,288,564]{2,1,0:T(8,128)(2,1)} %collective-permute-done.28), channel_id=1, source_target_pairs={{4,0},{8,4},{5,1},{9,5},{6,2},{10,6},{7,3},{11,7},{20,16},{24,20},... | collective-permute-start | bytes 1949192 | tf_op jit(solution)/shard_map/ppermute | solution.py:52
  114.5 3.3 collective-permute-start.10
  117.8 34.9 %collective-permute-start.11 = (bf16[64,1280]{1,0:T(8,128)(2,1)S(1)}, bf16[64,1280]{1,0:T(8,128)(2,1)S(1)}, u32[]{:S(2)}, u32[]{:S(2)}) collective-permute-start(bf16[64,1280]{1,0:T(8,128)(2,1)S(1)} %fusion.86), channel_id=1, source_target_pairs={{0,2},{1,3},{2,0},{3,1},{4,6},{5,7},{6,4},{7,5},{8,10},{9,11},{10,... | collective-permute-start | bytes 491528 | tf_op jit(solution)/shard_map/ppermute | solution.py:84
  131.1 22.9 %collective-permute-start.12 = (bf16[64,1280]{1,0:T(8,128)(2,1)S(1)}, bf16[64,1280]{1,0:T(8,128)(2,1)S(1)}, u32[]{:S(2)}, u32[]{:S(2)}) collective-permute-start(bf16[64,1280]{1,0:T(8,128)(2,1)S(1)} %fusion.86), channel_id=1, source_target_pairs={{0,1},{1,2},{2,3},{3,0},{4,5},{5,6},{6,7},{7,4},{8,9},{9,10},{10,1... | collective-permute-start | bytes 491528 | tf_op jit(solution)/shard_map/ppermute | solution.py:84
  137.0 18.3 %collective-permute-start.14 = (bf16[3,384,512]{2,1,0:T(8,128)(2,1)}, bf16[3,384,512]{2,1,0:T(8,128)(2,1)}, u32[]{:S(2)}, u32[]{:S(2)}) collective-permute-start(bf16[3,384,512]{2,1,0:T(8,128)(2,1)} %collective-permute-done.13), channel_id=1, source_target_pairs={{4,8},{8,12},{5,9},{9,13},{6,10},{10,14},{7,11},{11,15},{20,24},{2... | collective-permute-start | bytes 3538952 | tf_op jit(solution)/shard_map/ppermute | solution.py:50
  138.7 40.2 %collective-permute-start.16 = (bf16[3,384,512]{2,1,0:T(8,128)(2,1)}, bf16[3,384,512]{2,1,0:T(8,128)(2,1)}, u32[]{:S(2)}, u32[]{:S(2)}) collective-permute-start(bf16[3,384,512]{2,1,0:T(8,128)(2,1)} %collective-permute-done.15), channel_id=1, source_target_pairs={{4,0},{8,4},{5,1},{9,5},{6,2},{10,6},{7,3},{11,7},{20,16},{24,20},... | collective-permute-start | bytes 3538952 | tf_op jit(solution)/shard_map/ppermute | solution.py:52
  152.0 3.2 collective-permute-start.27
  152.7 40.3 %collective-permute-start.30 = (bf16[2,288,564]{2,1,0:T(8,128)(2,1)}, bf16[2,288,564]{2,1,0:T(8,128)(2,1)S(1)}, u32[]{:S(2)}, u32[]{:S(2)}) collective-permute-start(bf16[2,288,564]{2,1,0:T(8,128)(2,1)} %collective-permute-done.29), channel_id=1, source_target_pairs={{4,0},{5,1},{6,2},{7,3},{20,16},{21,17},{22,18},{23,19}} | collective-permute-start | bytes 1949192 | tf_op jit(solution)/shard_map/ppermute | solution.py:52
  154.1 27.7 %copy-start.19 = (bf16[64,1280]{1,0:T(8,128)(2,1)}, bf16[64,1280]{1,0:T(8,128)(2,1)S(1)}, u32[]{:S(2)}) copy-start(bf16[64,1280]{1,0:T(8,128)(2,1)S(1)} %collective-permute-done.12) | copy-start | bytes 491524
  155.3 27.7 %copy-start.6 = (bf16[2,288,564]{2,1,0:T(8,128)(2,1)S(1)}, bf16[2,288,564]{2,1,0:T(8,128)(2,1)}, u32[]{:S(2)}) copy-start(bf16[2,288,564]{2,1,0:T(8,128)(2,1)} %slice_select_fusion.2) | copy-start | bytes 1949188
  178.9 31.5 %collective-permute-start.23 = (bf16[3,384,512]{2,1,0:T(8,128)(2,1)}, bf16[3,384,512]{2,1,0:T(8,128)(2,1)}, u32[]{:S(2)}, u32[]{:S(2)}) collective-permute-start(bf16[3,384,512]{2,1,0:T(8,128)(2,1)} %collective-permute-done.14), channel_id=1, source_target_pairs={{8,12},{9,13},{10,14},{11,15},{24,28},{25,29},{26,30},{27,31}} | collective-permute-start | bytes 3538952 | tf_op jit(solution)/shard_map/ppermute | solution.py:50
  193.1 7.7 %copy-start.24 = (bf16[2,2016,564]{2,1,0:T(8,128)(2,1)}, bf16[2,2016,564]{2,1,0:T(8,128)(2,1)S(1)}, u32[]{:S(2)}) copy-start(bf16[2,2016,564]{2,1,0:T(8,128)(2,1)S(1)} %constant_dynamic-update-slice_fusion.21) | copy-start | bytes 13644292
  193.1 31.1 %collective-permute-start.24 = (bf16[3,384,512]{2,1,0:T(8,128)(2,1)}, bf16[3,384,512]{2,1,0:T(8,128)(2,1)}, u32[]{:S(2)}, u32[]{:S(2)}) collective-permute-start(bf16[3,384,512]{2,1,0:T(8,128)(2,1)} %collective-permute-done.16), channel_id=1, source_target_pairs={{4,0},{5,1},{6,2},{7,3},{20,16},{21,17},{22,18},{23,19}} | collective-permute-start | bytes 3538952 | tf_op jit(solution)/shard_map/ppermute | solution.py:52
  194.4 14.5 %collective-permute-start.17 = (bf16[320,672]{1,0:T(8,128)(2,1)S(1)}, bf16[320,672]{1,0:T(8,128)(2,1)}, u32[]{:S(2)}, u32[]{:S(2)}) collective-permute-start(bf16[320,672]{1,0:T(8,128)(2,1)S(1)} %pad_maximum_fusion.3), channel_id=1, source_target_pairs={{0,4},{4,8},{8,12},{1,5},{5,9},{9,13},{2,6},{6,10},{10,14},{3,7},{... | collective-permute-start | bytes 1290248 | tf_op jit(solution)/shard_map/ppermute | solution.py:50
  205.8 31.4 %collective-permute-start.20 = (bf16[320,672]{1,0:T(8,128)(2,1)S(1)}, bf16[320,672]{1,0:T(8,128)(2,1)}, u32[]{:S(2)}, u32[]{:S(2)}) collective-permute-start(bf16[320,672]{1,0:T(8,128)(2,1)S(1)} %pad_maximum_fusion.3), channel_id=1, source_target_pairs={{4,0},{8,4},{12,8},{5,1},{9,5},{13,9},{6,2},{10,6},{14,10},{7,3},{... | collective-permute-start | bytes 1290248 | tf_op jit(solution)/shard_map/ppermute | solution.py:52
  208.9 29.7 %collective-permute-start.18 = (bf16[320,672]{1,0:T(8,128)(2,1)}, bf16[320,672]{1,0:T(8,128)(2,1)}, u32[]{:S(2)}, u32[]{:S(2)}) collective-permute-start(bf16[320,672]{1,0:T(8,128)(2,1)} %collective-permute-done.17), channel_id=1, source_target_pairs={{4,8},{8,12},{5,9},{9,13},{6,10},{10,14},{7,11},{11,15},{20,24},{2... | collective-permute-start | bytes 1290248 | tf_op jit(solution)/shard_map/ppermute | solution.py:50
  217.2 11.6 %copy-start.5 = (bf16[4,64,1536]{2,1,0:T(8,128)(2,1)S(1)}, bf16[4,64,1536]{2,1,0:T(8,128)(2,1)}, u32[]{:S(2)}) copy-start(bf16[4,64,1536]{2,1,0:T(8,128)(2,1)} %fusion.7) | copy-start | bytes 2359300
  225.6 3.3 copy-start.13
  235.3 8.3 %collective-permute-start.33 = (bf16[256,672]{1,0:T(8,128)(2,1)S(1)}, bf16[256,672]{1,0:T(8,128)(2,1)S(1)}, u32[]{:S(2)}, u32[]{:S(2)}) collective-permute-start(bf16[256,672]{1,0:T(8,128)(2,1)S(1)} %get-tuple-element.27), channel_id=1, source_target_pairs={{0,3},{1,0},{2,1},{3,2},{4,7},{5,4},{6,5},{7,6},{8,11},{9,8},{10,9... | collective-permute-start | bytes 1032200 | tf_op jit(solution)/shard_map/ppermute | solution.py:74
  235.4 20.0 %collective-permute-start.32 = (bf16[256,672]{1,0:T(8,128)(2,1)S(1)}, bf16[256,672]{1,0:T(8,128)(2,1)S(1)}, u32[]{:S(2)}, u32[]{:S(2)}) collective-permute-start(bf16[256,672]{1,0:T(8,128)(2,1)S(1)} %get-tuple-element.28), channel_id=1, source_target_pairs={{0,2},{1,3},{2,0},{3,1},{4,6},{5,7},{6,4},{7,5},{8,10},{9,11},{10,... | collective-permute-start | bytes 1032200 | tf_op jit(solution)/shard_map/ppermute | solution.py:74
  237.1 18.3 %collective-permute-start.31 = (bf16[256,672]{1,0:T(8,128)(2,1)S(1)}, bf16[256,672]{1,0:T(8,128)(2,1)S(1)}, u32[]{:S(2)}, u32[]{:S(2)}) collective-permute-start(bf16[256,672]{1,0:T(8,128)(2,1)S(1)} %get-tuple-element.26), channel_id=1, source_target_pairs={{0,1},{1,2},{2,3},{3,0},{4,5},{5,6},{6,7},{7,4},{8,9},{9,10},{10,1... | collective-permute-start | bytes 1032200 | tf_op jit(solution)/shard_map/ppermute | solution.py:74
  237.3 32.2 %collective-permute-start.21 = (bf16[320,672]{1,0:T(8,128)(2,1)}, bf16[320,672]{1,0:T(8,128)(2,1)S(1)}, u32[]{:S(2)}, u32[]{:S(2)}) collective-permute-start(bf16[320,672]{1,0:T(8,128)(2,1)} %collective-permute-done.20), channel_id=1, source_target_pairs={{4,0},{8,4},{5,1},{9,5},{6,2},{10,6},{7,3},{11,7},{20,16},{24,20},... | collective-permute-start | bytes 1290248 | tf_op jit(solution)/shard_map/ppermute | solution.py:52
  238.6 32.2 %collective-permute-start.19 = (bf16[320,672]{1,0:T(8,128)(2,1)}, bf16[320,672]{1,0:T(8,128)(2,1)S(1)}, u32[]{:S(2)}, u32[]{:S(2)}) collective-permute-start(bf16[320,672]{1,0:T(8,128)(2,1)} %collective-permute-done.18), channel_id=1, source_target_pairs={{8,12},{9,13},{10,14},{11,15},{24,28},{25,29},{26,30},{27,31}} | collective-permute-start | bytes 1290248 | tf_op jit(solution)/shard_map/ppermute | solution.py:50
  255.5 17.9 %collective-permute-start.34 = (bf16[256,672]{1,0:T(8,128)(2,1)S(1)}, bf16[256,672]{1,0:T(8,128)(2,1)S(1)}, u32[]{:S(2)}, u32[]{:S(2)}) collective-permute-start(bf16[256,672]{1,0:T(8,128)(2,1)S(1)} %fusion.29), channel_id=1, source_target_pairs={{0,16},{16,0},{1,17},{17,1},{2,18},{18,2},{3,19},{19,3},{4,20},{20... | collective-permute-start | bytes 1032200 | tf_op jit(solution)/shard_map/ppermute | solution.py:91
  257.2 16.4 %copy-start.17 = (bf16[4,64,288]{2,1,0:T(8,128)(2,1)S(1)}, bf16[4,64,288]{2,1,0:T(8,128)(2,1)}, u32[]{:S(2)}) copy-start(bf16[4,64,288]{2,1,0:T(8,128)(2,1)} %constant_dynamic-slice_fusion.1) | copy-start | bytes 442372
  257.2 16.4 %copy-start.18 = (bf16[4,64,384]{2,1,0:T(8,128)(2,1)S(1)}, bf16[4,64,384]{2,1,0:T(8,128)(2,1)}, u32[]{:S(2)}) copy-start(bf16[4,64,384]{2,1,0:T(8,128)(2,1)} %constant_dynamic-slice_fusion.2) | copy-start | bytes 589828
  269.5 23.2 %collective-permute-start.22 = (bf16[320,672]{1,0:T(8,128)(2,1)S(1)}, bf16[320,672]{1,0:T(8,128)(2,1)}, u32[]{:S(2)}, u32[]{:S(2)}) collective-permute-start(bf16[320,672]{1,0:T(8,128)(2,1)S(1)} %collective-permute-done.21), channel_id=1, source_target_pairs={{4,0},{5,1},{6,2},{7,3},{20,16},{21,17},{22,18},{23,19}} | collective-permute-start | bytes 1290248 | tf_op jit(solution)/shard_map/ppermute | solution.py:52
  275.1 21.6 %all-to-all-start = ((bf16[4,64,672]{2,1,0:T(8,128)(2,1)}), bf16[4,64,672]{2,1,0:T(8,128)(2,1)S(1)}, u32[]{:S(2)}, u32[]{:S(2)}) async-start(bf16[4,64,672]{2,1,0:T(8,128)(2,1)} %broadcast_select_fusion), calls=%async_computation | async-start | bytes 786432 | tf_op jit(solution)/shard_map/all_to_all | solution.py:168
  287.3 113.2 %reduce-scatter.2.cloned.1.call-start = ((), (), s32[]{:S(2)}) async-start(), calls=%async_computation.2 | async-start | bytes 4096000 | tf_op jit(solution)/shard_map/reduce_scatter | solution.py:200
  301.1 4.9 %collective-permute-start.37 = (bf16[64,1280]{1,0:T(8,128)(2,1)}, bf16[64,1280]{1,0:T(8,128)(2,1)}, u32[]{:S(2)}, u32[]{:S(2)}) collective-permute-start(bf16[64,1280]{1,0:T(8,128)(2,1)} %get-tuple-element.39), channel_id=1, source_target_pairs={{0,3},{1,0},{2,1},{3,2},{4,7},{5,4},{6,5},{7,6},{8,11},{9,8},{10,9... | collective-permute-start | bytes 491528 | tf_op jit(solution)/shard_map/ppermute | solution.py:74
  301.1 10.4 %collective-permute-start.36 = (bf16[64,1280]{1,0:T(8,128)(2,1)}, bf16[64,1280]{1,0:T(8,128)(2,1)}, u32[]{:S(2)}, u32[]{:S(2)}) collective-permute-start(bf16[64,1280]{1,0:T(8,128)(2,1)} %get-tuple-element.40), channel_id=1, source_target_pairs={{0,2},{1,3},{2,0},{3,1},{4,6},{5,7},{6,4},{7,5},{8,10},{9,11},{10,... | collective-permute-start | bytes 491528 | tf_op jit(solution)/shard_map/ppermute | solution.py:74
  302.8 8.8 %collective-permute-start.35 = (bf16[64,1280]{1,0:T(8,128)(2,1)}, bf16[64,1280]{1,0:T(8,128)(2,1)}, u32[]{:S(2)}, u32[]{:S(2)}) collective-permute-start(bf16[64,1280]{1,0:T(8,128)(2,1)} %get-tuple-element.38), channel_id=1, source_target_pairs={{0,1},{1,2},{2,3},{3,0},{4,5},{5,6},{6,7},{7,4},{8,9},{9,10},{10,1... | collective-permute-start | bytes 491528 | tf_op jit(solution)/shard_map/ppermute | solution.py:74
  304.5 9.2 %collective-permute-start.43 = (bf16[160,672]{1,0:T(8,128)(2,1)S(1)}, bf16[160,672]{1,0:T(8,128)(2,1)S(1)}, u32[]{:S(2)}, u32[]{:S(2)}) collective-permute-start(bf16[160,672]{1,0:T(8,128)(2,1)S(1)} %get-tuple-element.32), channel_id=1, source_target_pairs={{0,12},{4,0},{8,4},{12,8},{1,13},{5,1},{9,5},{13,9},{2,14},{6,2},{... | collective-permute-start | bytes 645128 | tf_op jit(solution)/shard_map/ppermute | solution.py:74
  306.0 21.9 %collective-permute-start.42 = (bf16[160,672]{1,0:T(8,128)(2,1)S(1)}, bf16[160,672]{1,0:T(8,128)(2,1)S(1)}, u32[]{:S(2)}, u32[]{:S(2)}) collective-permute-start(bf16[160,672]{1,0:T(8,128)(2,1)S(1)} %get-tuple-element.33), channel_id=1, source_target_pairs={{0,8},{4,12},{8,0},{12,4},{1,9},{5,13},{9,1},{13,5},{2,10},{6,14},... | collective-permute-start | bytes 645128 | tf_op jit(solution)/shard_map/ppermute | solution.py:74
  306.0 21.9 %collective-permute-start.41 = (bf16[160,672]{1,0:T(8,128)(2,1)S(1)}, bf16[160,672]{1,0:T(8,128)(2,1)S(1)}, u32[]{:S(2)}, u32[]{:S(2)}) collective-permute-start(bf16[160,672]{1,0:T(8,128)(2,1)S(1)} %get-tuple-element.31), channel_id=1, source_target_pairs={{0,4},{4,8},{8,12},{12,0},{1,5},{5,9},{9,13},{13,1},{2,6},{6,10},{... | collective-permute-start | bytes 645128 | tf_op jit(solution)/shard_map/ppermute | solution.py:74
  313.1 15.0 %collective-permute-start.38 = (bf16[64,1280]{1,0:T(8,128)(2,1)S(1)}, bf16[64,1280]{1,0:T(8,128)(2,1)S(1)}, u32[]{:S(2)}, u32[]{:S(2)}) collective-permute-start(bf16[64,1280]{1,0:T(8,128)(2,1)S(1)} %multiply_convert_fusion.4), channel_id=1, source_target_pairs={{0,3},{1,0},{2,1},{3,2},{4,7},{5,4},{6,5},{7,6},{8,11},{9,8},{10,9... | collective-permute-start | bytes 491528 | tf_op jit(solution)/shard_map/ppermute | solution.py:84
  313.2 15.0 %collective-permute-start.39 = (bf16[64,1280]{1,0:T(8,128)(2,1)S(1)}, bf16[64,1280]{1,0:T(8,128)(2,1)S(1)}, u32[]{:S(2)}, u32[]{:S(2)}) collective-permute-start(bf16[64,1280]{1,0:T(8,128)(2,1)S(1)} %multiply_convert_fusion.4), channel_id=1, source_target_pairs={{0,2},{1,3},{2,0},{3,1},{4,6},{5,7},{6,4},{7,5},{8,10},{9,11},{10,... | collective-permute-start | bytes 491528 | tf_op jit(solution)/shard_map/ppermute | solution.py:84
  313.7 14.5 %collective-permute-start.40 = (bf16[64,1280]{1,0:T(8,128)(2,1)S(1)}, bf16[64,1280]{1,0:T(8,128)(2,1)S(1)}, u32[]{:S(2)}, u32[]{:S(2)}) collective-permute-start(bf16[64,1280]{1,0:T(8,128)(2,1)S(1)} %multiply_convert_fusion.4), channel_id=1, source_target_pairs={{0,1},{1,2},{2,3},{3,0},{4,5},{5,6},{6,7},{7,4},{8,9},{9,10},{10,1... | collective-permute-start | bytes 491528 | tf_op jit(solution)/shard_map/ppermute | solution.py:84
  400.5 12.4 %copy-start.4 = (bf16[2,320,640]{2,1,0:T(8,128)(2,1)S(1)}, bf16[2,320,640]{2,1,0:T(8,128)(2,1)}, u32[]{:S(2)}) copy-start(bf16[2,320,640]{2,1,0:T(8,128)(2,1)} %reduce-scatter.2.cloned.1.call-done) | copy-start | bytes 2457604
  401.8 11.1 %collective-permute-start.44 = (bf16[2,160,640]{2,1,0:T(8,128)(2,1)S(1)}, bf16[2,160,640]{2,1,0:T(8,128)(2,1)S(1)}, u32[]{:S(2)}, u32[]{:S(2)}) collective-permute-start(bf16[2,160,640]{2,1,0:T(8,128)(2,1)S(1)} %fusion.66), channel_id=1, source_target_pairs={{0,16},{16,0},{1,17},{17,1},{2,18},{18,2},{3,19},{19,3},{4,20},{20... | collective-permute-start | bytes 1228808 | tf_op jit(solution)/shard_map/ppermute | solution.py:91
  (12 other events, 17.5 us)
Sparse Core Ops, SparseCore 0:
  338.3 62.2 reduce-scatter.1
